TPU v7x, 32 devices: a whole 2x2x4 slice. The times are simulated.
32 devices in a mesh: dp: 4 (over y, x), fsdp: 8 (over z, core).
Axes of the slice: x: 2, y: 2, z: 4, core: 2. Of those that a mesh axis runs over, the one named last changes fastest.
Arguments:
- enc_in: bfloat16 [64, 512, 512], P(('dp', 'fsdp')), may hold values from -6 to 6
- dec_in: bfloat16 [64, 512, 512], P(('dp', 'fsdp')), may hold values from -6 to 6
- bucket: int32 [64], P(('dp', 'fsdp')), may hold values from 0 to 2, as said below
- enc_lengths: int32 [64, 4], P(('dp', 'fsdp')), may hold values from 0 to 512, as said below
- dec_lengths: int32 [64, 4], P(('dp', 'fsdp')), may hold values from 0 to 512, as said below
- pred_ids: int32 [64, 512], P(('dp', 'fsdp')), may hold values from 0 to 522
- running_counts: int32 [523], replicated, may hold values from 0 to 15
- enc_attn_in: bfloat16 [786432], P(('dp', 'fsdp')), may hold values from -0.25 to 0.25
- enc_attn_out: bfloat16 [262144], P(('dp', 'fsdp')), may hold values from -1 to 1
- enc_ff_in: bfloat16 [1048576], P(('dp', 'fsdp')), may hold values from -0.25 to 0.25
- enc_ff_out: bfloat16 [1048576], P(('dp', 'fsdp')), may hold values from -0.125 to 0.125
- enc_norms: bfloat16 [2048], P(('dp', 'fsdp')), may hold values from -1.2 to 1.8
- dec_self_in: bfloat16 [786432], P(('dp', 'fsdp')), may hold values from -0.25 to 0.25
- dec_self_out: bfloat16 [262144], P(('dp', 'fsdp')), may hold values from -1 to 1
- dec_cross_q: bfloat16 [262144], P(('dp', 'fsdp')), may hold values from -0.25 to 0.25
- dec_cross_kv: bfloat16 [524288], P(('dp', 'fsdp')), may hold values from -0.25 to 0.25
- dec_cross_out: bfloat16 [262144], P(('dp', 'fsdp')), may hold values from -1 to 1
- dec_ff_in: bfloat16 [1048576], P(('dp', 'fsdp')), may hold values from -0.25 to 0.25
- dec_ff_out: bfloat16 [1048576], P(('dp', 'fsdp')), may hold values from -0.125 to 0.125
- dec_norms: bfloat16 [3072], P(('dp', 'fsdp')), may hold values from -1.2 to 1.8
- enc_cotangent: bfloat16 [64, 512, 512], P(('dp', 'fsdp')), may hold values from -6 to 6
- dec_cotangent: bfloat16 [64, 512, 512], P(('dp', 'fsdp')), may hold values from -6 to 6
Outputs:
- enc_out: bfloat16 [64, 512, 512], P(('dp', 'fsdp'))
- dec_out: bfloat16 [64, 512, 512], P(('dp', 'fsdp'))
- enc_in_grad: bfloat16 [64, 512, 512], P(('dp', 'fsdp'))
- dec_in_grad: bfloat16 [64, 512, 512], P(('dp', 'fsdp'))
- enc_attn_in_grad: float32 [786432], P(('dp', 'fsdp'))
- enc_attn_out_grad: float32 [262144], P(('dp', 'fsdp'))
- enc_ff_in_grad: float32 [1048576], P(('dp', 'fsdp'))
- enc_ff_out_grad: float32 [1048576], P(('dp', 'fsdp'))
- enc_norms_grad: float32 [2048], P(('dp', 'fsdp'))
- dec_self_in_grad: float32 [786432], P(('dp', 'fsdp'))
- dec_self_out_grad: float32 [262144], P(('dp', 'fsdp'))
- dec_cross_q_grad: float32 [262144], P(('dp', 'fsdp'))
- dec_cross_kv_grad: float32 [524288], P(('dp', 'fsdp'))
- dec_cross_out_grad: float32 [262144], P(('dp', 'fsdp'))
- dec_ff_in_grad: float32 [1048576], P(('dp', 'fsdp'))
- dec_ff_out_grad: float32 [1048576], P(('dp', 'fsdp'))
- dec_norms_grad: float32 [3072], P(('dp', 'fsdp'))
- counts: int32 [523], replicated
Inputs may be any that keep to these rules, and one draw needn't show every extreme that they name: `bucket`: a slot of kind b holds 4 / 2**b sequences, each of up to 512 / 4 * 2**b positions; source and target of a pair share the slot and its sequence number; some slot is of kind 2. `enc_lengths`: for a slot of kind b, entries 0 to 4 / 2**b - 1 are its sequences' lengths, from a quarter of 512 / 4 * 2**b to all of it; the other entries are 0; some slot of kind 2 holds a sequence of all 512 positions. `dec_lengths`: as enc_lengths, for the targets.
All inputs are finite; a program needn't handle non-finite values.
Results may differ from a plain program's by a relative error of at most 0.025.
Values may be sent and summed in bfloat16 or wider, within the bound.
No kernel may reach another device: no remote copies, remote signals or barrier semaphores. Data moves between devices by JAX's collectives and lax.ppermute only.
A program may use at most 192 MiB of HBM per device.

v0:
```python
import jax
import jax.numpy as jnp
from jax import lax
from jax.sharding import PartitionSpec as P

D = 512
HEAD = 64
FF = 2048
VOCAB = 523
SLOT = 512


epsilon = 1e-05


def layer_norm(values, norm_gain, norm_shift):
    row_mean = jnp.mean(values, -1, keepdims=True)
    centered = values - row_mean
    variance = jnp.mean(centered * centered, -1, keepdims=True)
    return centered * lax.rsqrt(variance + epsilon) * norm_gain + norm_shift


def gelu_exact(values):
    return jax.nn.gelu(values, approximate=False)


def slot_layout(bucket_kind, lengths):
    positions = jnp.arange(SLOT, dtype=jnp.int32)
    bucket_size = jnp.left_shift(jnp.int32(SLOT // 4), bucket_kind)
    segment = positions // bucket_size
    picker = segment[:, None] == jnp.arange(4, dtype=jnp.int32)[None, :]
    own_length = jnp.sum(jnp.where(picker, lengths[None, :], 0), 1, dtype=jnp.int32)
    is_live = positions % bucket_size < own_length
    return (segment, is_live)


def pair_mask(bucket_kind, query_lengths, key_lengths, causal):
    query_segment, query_live = slot_layout(bucket_kind, query_lengths)
    key_segment, key_live = slot_layout(bucket_kind, key_lengths)
    allowed = (query_segment[:, None] == key_segment[None, :]) & key_live[None, :]
    if causal:
        positions = jnp.arange(SLOT, dtype=jnp.int32)
        allowed = allowed & (positions[None, :] <= positions[:, None])
    return allowed


def forward_product(left, right):
    return jnp.dot(left, right, preferred_element_type=jnp.float32)


def back_product(left, right):
    return lax.dot_general(
        left, right, (((1,), (1,)), ((), ())), preferred_element_type=jnp.float32
    )


def weight_grad(left, right):
    return lax.dot_general(
        left, right, (((0,), (0,)), ((), ())), preferred_element_type=jnp.float32
    )


def split_heads(values):
    return values.reshape(SLOT, D // HEAD, HEAD)


def attention_scores(query_heads, key_heads, allowed):
    scores = jnp.einsum(
        "qhd,khd->hqk", query_heads, key_heads, preferred_element_type=jnp.float32
    ) * HEAD ** (-0.5)
    return jnp.where(allowed[None], scores, -1000000000.0)


def attention_forward(queries, keys_in, values_in, allowed):
    query_heads = split_heads(queries)
    key_heads = split_heads(keys_in)
    value_heads = split_heads(values_in)
    scores = attention_scores(query_heads, key_heads, allowed)
    largest = jnp.max(scores, -1, keepdims=True)
    powers = jnp.exp(scores - largest)
    row_total = jnp.sum(powers, -1, keepdims=True)
    weights = (powers / row_total).astype(jnp.bfloat16)
    context = jnp.einsum("hqk,khd->qhd", weights, value_heads, preferred_element_type=jnp.float32)
    return (context.reshape(SLOT, D), largest[..., 0] + jnp.log(row_total[..., 0]))


def attention_backward(queries, keys_in, values_in, allowed, logsum, grad_context):
    query_heads = split_heads(queries)
    key_heads = split_heads(keys_in)
    value_heads = split_heads(values_in)
    grad_heads = split_heads(grad_context)
    scores = attention_scores(query_heads, key_heads, allowed)
    probabilities = jnp.exp(scores - logsum[..., None])
    grad_value = jnp.einsum(
        "hqk,qhd->khd",
        probabilities.astype(jnp.bfloat16),
        grad_heads,
        preferred_element_type=jnp.float32,
    )
    grad_probs = jnp.einsum(
        "qhd,khd->hqk", grad_heads, value_heads, preferred_element_type=jnp.float32
    )
    row_inner = jnp.sum(probabilities * grad_probs, -1, keepdims=True)
    grad_scores = (probabilities * (grad_probs - row_inner)).astype(jnp.bfloat16)
    grad_query = jnp.einsum(
        "hqk,khd->qhd", grad_scores, key_heads, preferred_element_type=jnp.float32
    ) * HEAD ** (-0.5)
    grad_key = jnp.einsum(
        "hqk,qhd->khd", grad_scores, query_heads, preferred_element_type=jnp.float32
    ) * HEAD ** (-0.5)
    return (grad_query.reshape(SLOT, D), grad_key.reshape(SLOT, D), grad_value.reshape(SLOT, D))


def self_forward(residual, w_in, w_out, norm_gain, norm_shift, bucket, lengths, causal):
    slot_count = bucket.shape[0]
    normed, norm_back = jax.vjp(layer_norm, residual, norm_gain, norm_shift)
    normed_low = normed.astype(jnp.bfloat16)
    projected = (
        forward_product(normed_low, w_in).astype(jnp.bfloat16).reshape(slot_count, SLOT, 3 * D)
    )

    def one_slot(pieces):
        slot_block, bucket_kind, slot_lengths = pieces
        allowed = pair_mask(bucket_kind, slot_lengths, slot_lengths, causal)
        return attention_forward(
            slot_block[:, :D], slot_block[:, D : 2 * D], slot_block[:, 2 * D :], allowed
        )

    context, logsum = lax.map(one_slot, (projected, bucket, lengths))
    context_low = context.reshape(slot_count * SLOT, D).astype(jnp.bfloat16)
    output = residual + forward_product(context_low, w_out)
    return (output, (norm_back, normed_low, projected, logsum, context_low))


def self_backward(grad_output, kept_values, w_in, w_out, bucket, lengths, causal):
    norm_back, normed_low, projected, logsum, context_low = kept_values
    slot_count = bucket.shape[0]
    branch_grad = grad_output.astype(jnp.bfloat16)
    grad_w_out = weight_grad(context_low, branch_grad)
    grad_context = (
        back_product(branch_grad, w_out).astype(jnp.bfloat16).reshape(slot_count, SLOT, D)
    )

    def one_slot(pieces):
        slot_block, slot_logsum, slot_grad, bucket_kind, slot_lengths = pieces
        allowed = pair_mask(bucket_kind, slot_lengths, slot_lengths, causal)
        grads = attention_backward(
            slot_block[:, :D],
            slot_block[:, D : 2 * D],
            slot_block[:, 2 * D :],
            allowed,
            slot_logsum,
            slot_grad,
        )
        return jnp.concatenate(grads, 1).astype(jnp.bfloat16)

    grad_projected = lax.map(one_slot, (projected, logsum, grad_context, bucket, lengths)).reshape(
        slot_count * SLOT, 3 * D
    )
    grad_w_in = weight_grad(normed_low, grad_projected)
    grad_normed = back_product(grad_projected, w_in)
    grad_residual, grad_gain, grad_shift = norm_back(grad_normed)
    return (grad_output + grad_residual, grad_w_in, grad_w_out, grad_gain, grad_shift)


def cross_forward(
    residual,
    memory,
    w_query,
    w_pair,
    w_out,
    norm_gain,
    norm_shift,
    bucket,
    dec_lengths,
    enc_lengths,
):
    slot_count = bucket.shape[0]
    normed, norm_back = jax.vjp(layer_norm, residual, norm_gain, norm_shift)
    normed_low = normed.astype(jnp.bfloat16)
    queries = forward_product(normed_low, w_query).astype(jnp.bfloat16).reshape(slot_count, SLOT, D)
    pairs = forward_product(memory, w_pair).astype(jnp.bfloat16).reshape(slot_count, SLOT, 2 * D)

    def one_slot(pieces):
        query_block, pair_block, bucket_kind, query_lengths, key_lengths = pieces
        allowed = pair_mask(bucket_kind, query_lengths, key_lengths, False)
        return attention_forward(query_block, pair_block[:, :D], pair_block[:, D:], allowed)

    context, logsum = lax.map(one_slot, (queries, pairs, bucket, dec_lengths, enc_lengths))
    context_low = context.reshape(slot_count * SLOT, D).astype(jnp.bfloat16)
    output = residual + forward_product(context_low, w_out)
    return (output, (norm_back, normed_low, queries, pairs, logsum, context_low))


def cross_backward(
    grad_output, kept_values, memory, w_query, w_pair, w_out, bucket, dec_lengths, enc_lengths
):
    norm_back, normed_low, queries, pairs, logsum, context_low = kept_values
    slot_count = bucket.shape[0]
    branch_grad = grad_output.astype(jnp.bfloat16)
    grad_w_out = weight_grad(context_low, branch_grad)
    grad_context = (
        back_product(branch_grad, w_out).astype(jnp.bfloat16).reshape(slot_count, SLOT, D)
    )

    def one_slot(pieces):
        query_block, pair_block, slot_logsum, slot_grad, bucket_kind, query_lengths, key_lengths = (
            pieces
        )
        allowed = pair_mask(bucket_kind, query_lengths, key_lengths, False)
        grad_query, grad_key, grad_value = attention_backward(
            query_block, pair_block[:, :D], pair_block[:, D:], allowed, slot_logsum, slot_grad
        )
        return (
            grad_query.astype(jnp.bfloat16),
            jnp.concatenate([grad_key, grad_value], 1).astype(jnp.bfloat16),
        )

    grad_queries, grad_pairs = lax.map(
        one_slot, (queries, pairs, logsum, grad_context, bucket, dec_lengths, enc_lengths)
    )
    grad_queries = grad_queries.reshape(slot_count * SLOT, D)
    grad_pairs = grad_pairs.reshape(slot_count * SLOT, 2 * D)
    grad_w_query = weight_grad(normed_low, grad_queries)
    grad_normed = back_product(grad_queries, w_query)
    grad_w_pair = weight_grad(memory, grad_pairs)
    grad_memory = back_product(grad_pairs, w_pair)
    grad_residual, grad_gain, grad_shift = norm_back(grad_normed)
    return (
        grad_output + grad_residual,
        grad_memory,
        grad_w_query,
        grad_w_pair,
        grad_w_out,
        grad_gain,
        grad_shift,
    )


def ffn_forward(residual, ff_in, ff_out, norm_gain, norm_shift):
    normed, norm_back = jax.vjp(layer_norm, residual, norm_gain, norm_shift)
    normed_low = normed.astype(jnp.bfloat16)
    hidden_pre = forward_product(normed_low, ff_in)
    active, gelu_back = jax.vjp(gelu_exact, hidden_pre)
    active_low = active.astype(jnp.bfloat16)
    output = residual + forward_product(active_low, ff_out)
    return (output, (norm_back, normed_low, gelu_back, active_low))


def ffn_backward(grad_output, kept_values, ff_in, ff_out):
    norm_back, normed_low, gelu_back, active_low = kept_values
    branch_grad = grad_output.astype(jnp.bfloat16)
    grad_ff_out = weight_grad(active_low, branch_grad)
    grad_active = back_product(branch_grad, ff_out)
    grad_hidden = gelu_back(grad_active)[0].astype(jnp.bfloat16)
    grad_ff_in = weight_grad(normed_low, grad_hidden)
    grad_normed = back_product(grad_hidden, ff_in)
    grad_residual, grad_gain, grad_shift = norm_back(grad_normed)
    return (grad_output + grad_residual, grad_ff_in, grad_ff_out, grad_gain, grad_shift)


def encoder_shapes(gathered):
    return (
        gathered[0].reshape(D, 3 * D),
        gathered[1].reshape(D, D),
        gathered[2].reshape(D, FF),
        gathered[3].reshape(FF, D),
        gathered[4].reshape(4, D).astype(jnp.float32),
    )


def decoder_shapes(gathered):
    return (
        gathered[0].reshape(D, 3 * D),
        gathered[1].reshape(D, D),
        gathered[2].reshape(D, D),
        gathered[3].reshape(D, 2 * D),
        gathered[4].reshape(D, D),
        gathered[5].reshape(D, FF),
        gathered[6].reshape(FF, D),
        gathered[7].reshape(6, D).astype(jnp.float32),
    )


def local(
    enc_in,
    dec_in,
    bucket,
    enc_lengths,
    dec_lengths,
    pred_ids,
    running_counts,
    enc_attn_in,
    enc_attn_out,
    enc_ff_in,
    enc_ff_out,
    enc_norms,
    dec_self_in,
    dec_self_out,
    dec_cross_q,
    dec_cross_kv,
    dec_cross_out,
    dec_ff_in,
    dec_ff_out,
    dec_norms,
    enc_cotangent,
    dec_cotangent,
):
    slot_count = enc_in.shape[0]
    row_count = slot_count * SLOT
    enc_forward = encoder_shapes(
        (
            lax.all_gather(enc_attn_in, ("dp", "fsdp"), axis=0, tiled=True),
            lax.all_gather(enc_attn_out, ("dp", "fsdp"), axis=0, tiled=True),
            lax.all_gather(enc_ff_in, ("dp", "fsdp"), axis=0, tiled=True),
            lax.all_gather(enc_ff_out, ("dp", "fsdp"), axis=0, tiled=True),
            lax.all_gather(enc_norms, ("dp", "fsdp"), axis=0, tiled=True),
        )
    )
    enc_rows = enc_in.reshape(row_count, D).astype(jnp.float32)
    attended, enc_self_kept = self_forward(
        enc_rows,
        enc_forward[0],
        enc_forward[1],
        enc_forward[4][0],
        enc_forward[4][1],
        bucket,
        enc_lengths,
        False,
    )
    encoded, enc_ffn_kept = ffn_forward(
        attended, enc_forward[2], enc_forward[3], enc_forward[4][2], enc_forward[4][3]
    )
    memory = encoded.astype(jnp.bfloat16)
    dec_forward = decoder_shapes(
        (
            lax.all_gather(dec_self_in, ("dp", "fsdp"), axis=0, tiled=True),
            lax.all_gather(dec_self_out, ("dp", "fsdp"), axis=0, tiled=True),
            lax.all_gather(dec_cross_q, ("dp", "fsdp"), axis=0, tiled=True),
            lax.all_gather(dec_cross_kv, ("dp", "fsdp"), axis=0, tiled=True),
            lax.all_gather(dec_cross_out, ("dp", "fsdp"), axis=0, tiled=True),
            lax.all_gather(dec_ff_in, ("dp", "fsdp"), axis=0, tiled=True),
            lax.all_gather(dec_ff_out, ("dp", "fsdp"), axis=0, tiled=True),
            lax.all_gather(dec_norms, ("dp", "fsdp"), axis=0, tiled=True),
        )
    )
    dec_rows = dec_in.reshape(row_count, D).astype(jnp.float32)
    first_out, dec_self_kept = self_forward(
        dec_rows,
        dec_forward[0],
        dec_forward[1],
        dec_forward[7][0],
        dec_forward[7][1],
        bucket,
        dec_lengths,
        True,
    )
    second_out, cross_kept = cross_forward(
        first_out,
        memory,
        dec_forward[2],
        dec_forward[3],
        dec_forward[4],
        dec_forward[7][2],
        dec_forward[7][3],
        bucket,
        dec_lengths,
        enc_lengths,
    )
    decoded, dec_ffn_kept = ffn_forward(
        second_out, dec_forward[5], dec_forward[6], dec_forward[7][4], dec_forward[7][5]
    )
    dec_backward = decoder_shapes(
        (
            lax.all_gather(dec_self_in, ("dp", "fsdp"), axis=0, tiled=True),
            lax.all_gather(dec_self_out, ("dp", "fsdp"), axis=0, tiled=True),
            lax.all_gather(dec_cross_q, ("dp", "fsdp"), axis=0, tiled=True),
            lax.all_gather(dec_cross_kv, ("dp", "fsdp"), axis=0, tiled=True),
            lax.all_gather(dec_cross_out, ("dp", "fsdp"), axis=0, tiled=True),
            lax.all_gather(dec_ff_in, ("dp", "fsdp"), axis=0, tiled=True),
            lax.all_gather(dec_ff_out, ("dp", "fsdp"), axis=0, tiled=True),
            lax.all_gather(dec_norms, ("dp", "fsdp"), axis=0, tiled=True),
        )
    )
    grad_decoded = dec_cotangent.reshape(row_count, D).astype(jnp.float32)
    grad_second, grad_dec_ff_in, grad_dec_ff_out, ffn_gain, ffn_shift = ffn_backward(
        grad_decoded, dec_ffn_kept, dec_backward[5], dec_backward[6]
    )
    (
        grad_first,
        grad_memory,
        grad_cross_q,
        grad_cross_kv,
        grad_cross_out,
        cross_gain,
        cross_shift,
    ) = cross_backward(
        grad_second,
        cross_kept,
        memory,
        dec_backward[2],
        dec_backward[3],
        dec_backward[4],
        bucket,
        dec_lengths,
        enc_lengths,
    )
    grad_dec_rows, grad_self_in, grad_self_out, self_gain, self_shift = self_backward(
        grad_first, dec_self_kept, dec_backward[0], dec_backward[1], bucket, dec_lengths, True
    )
    dec_norm_grads = jnp.concatenate(
        [self_gain, self_shift, cross_gain, cross_shift, ffn_gain, ffn_shift]
    )
    dec_terms = (
        grad_self_in.reshape(-1),
        grad_self_out.reshape(-1),
        grad_cross_q.reshape(-1),
        grad_cross_kv.reshape(-1),
        grad_cross_out.reshape(-1),
        grad_dec_ff_in.reshape(-1),
        grad_dec_ff_out.reshape(-1),
        dec_norm_grads,
    )
    dec_grads = (
        lax.psum_scatter(dec_terms[0], ("dp", "fsdp"), scatter_dimension=0, tiled=True),
        lax.psum_scatter(dec_terms[1], ("dp", "fsdp"), scatter_dimension=0, tiled=True),
        lax.psum_scatter(dec_terms[2], ("dp", "fsdp"), scatter_dimension=0, tiled=True),
        lax.psum_scatter(dec_terms[3], ("dp", "fsdp"), scatter_dimension=0, tiled=True),
        lax.psum_scatter(dec_terms[4], ("dp", "fsdp"), scatter_dimension=0, tiled=True),
        lax.psum_scatter(dec_terms[5], ("dp", "fsdp"), scatter_dimension=0, tiled=True),
        lax.psum_scatter(dec_terms[6], ("dp", "fsdp"), scatter_dimension=0, tiled=True),
        lax.psum_scatter(dec_terms[7], ("dp", "fsdp"), scatter_dimension=0, tiled=True),
    )
    enc_backward = encoder_shapes(
        (
            lax.all_gather(enc_attn_in, ("dp", "fsdp"), axis=0, tiled=True),
            lax.all_gather(enc_attn_out, ("dp", "fsdp"), axis=0, tiled=True),
            lax.all_gather(enc_ff_in, ("dp", "fsdp"), axis=0, tiled=True),
            lax.all_gather(enc_ff_out, ("dp", "fsdp"), axis=0, tiled=True),
            lax.all_gather(enc_norms, ("dp", "fsdp"), axis=0, tiled=True),
        )
    )
    grad_encoded = enc_cotangent.reshape(row_count, D).astype(jnp.float32) + grad_memory
    grad_attended, grad_enc_ff_in, grad_enc_ff_out, second_gain, second_shift = ffn_backward(
        grad_encoded, enc_ffn_kept, enc_backward[2], enc_backward[3]
    )
    grad_enc_rows, grad_attn_in, grad_attn_out, first_gain, first_shift = self_backward(
        grad_attended, enc_self_kept, enc_backward[0], enc_backward[1], bucket, enc_lengths, False
    )
    enc_norm_grads = jnp.concatenate([first_gain, first_shift, second_gain, second_shift])
    enc_terms = (
        grad_attn_in.reshape(-1),
        grad_attn_out.reshape(-1),
        grad_enc_ff_in.reshape(-1),
        grad_enc_ff_out.reshape(-1),
        enc_norm_grads,
    )
    enc_grads = (
        lax.psum_scatter(enc_terms[0], ("dp", "fsdp"), scatter_dimension=0, tiled=True),
        lax.psum_scatter(enc_terms[1], ("dp", "fsdp"), scatter_dimension=0, tiled=True),
        lax.psum_scatter(enc_terms[2], ("dp", "fsdp"), scatter_dimension=0, tiled=True),
        lax.psum_scatter(enc_terms[3], ("dp", "fsdp"), scatter_dimension=0, tiled=True),
        lax.psum_scatter(enc_terms[4], ("dp", "fsdp"), scatter_dimension=0, tiled=True),
    )
    segments, live_flags = jax.vmap(slot_layout)(bucket, dec_lengths)
    hits = (
        pred_ids.reshape(-1)[:, None] == jnp.arange(VOCAB, dtype=jnp.int32)[None, :]
    ) & live_flags.reshape(-1)[:, None]
    local_counts = jnp.sum(hits.astype(jnp.int32), 0, dtype=jnp.int32)
    summed_counts = lax.psum(local_counts, ("dp", "fsdp"))
    counts = running_counts + summed_counts
    out_shape = (slot_count, SLOT, D)
    return (
        memory.reshape(out_shape),
        decoded.astype(jnp.bfloat16).reshape(out_shape),
        grad_enc_rows.astype(jnp.bfloat16).reshape(out_shape),
        grad_dec_rows.astype(jnp.bfloat16).reshape(out_shape),
        enc_grads[0],
        enc_grads[1],
        enc_grads[2],
        enc_grads[3],
        enc_grads[4],
        dec_grads[0],
        dec_grads[1],
        dec_grads[2],
        dec_grads[3],
        dec_grads[4],
        dec_grads[5],
        dec_grads[6],
        dec_grads[7],
        counts,
    )


def solution(mesh):
    return jax.shard_map(
        local,
        mesh=mesh,
        in_specs=(
            P(("dp", "fsdp"), None, None),
            P(("dp", "fsdp"), None, None),
            P(("dp", "fsdp")),
            P(("dp", "fsdp"), None),
            P(("dp", "fsdp"), None),
            P(("dp", "fsdp"), None),
            P(),
            P(("dp", "fsdp")),
            P(("dp", "fsdp")),
            P(("dp", "fsdp")),
            P(("dp", "fsdp")),
            P(("dp", "fsdp")),
            P(("dp", "fsdp")),
            P(("dp", "fsdp")),
            P(("dp", "fsdp")),
            P(("dp", "fsdp")),
            P(("dp", "fsdp")),
            P(("dp", "fsdp")),
            P(("dp", "fsdp")),
            P(("dp", "fsdp")),
            P(("dp", "fsdp"), None, None),
            P(("dp", "fsdp"), None, None),
        ),
        out_specs=(
            P(("dp", "fsdp"), None, None),
            P(("dp", "fsdp"), None, None),
            P(("dp", "fsdp"), None, None),
            P(("dp", "fsdp"), None, None),
            P(("dp", "fsdp")),
            P(("dp", "fsdp")),
            P(("dp", "fsdp")),
            P(("dp", "fsdp")),
            P(("dp", "fsdp")),
            P(("dp", "fsdp")),
            P(("dp", "fsdp")),
            P(("dp", "fsdp")),
            P(("dp", "fsdp")),
            P(("dp", "fsdp")),
            P(("dp", "fsdp")),
            P(("dp", "fsdp")),
            P(("dp", "fsdp")),
            P(),
        ),
        check_vma=False,
    )
```

profile of v0, /device:TPU:0, one launch (start us, length us, event | category | flops | bytes accessed | tf_op | source)
XLA Modules:
  0.0 1183.4 jit_solution(4475878355569605066)
XLA Ops:
  13.7 42.2 %all-reduce.17 = (bf16[2048]{0:T(1024)(128)(2,1)S(1)}, bf16[3072]{0:T(1024)(128)(2,1)S(1)}) all-reduce(bf16[2048]{0:T(1024)(128)(2,1)S(1)} %dynamic-update-slice, bf16[3072]{0:T(1024)(128)(2,1)S(1)} %dynamic-update-slice.1), channel_id=1, replica_groups=mesh['dp'=4,'fsdp'=8] {'dp','fsdp'}, use_global_device_ids=true, to_apply=%add | all-reduce | flops 5120 | bytes 20480
  60.9 43.7 %all_gather.52 = bf16[262144]{0:T(1024)(128)(2,1)S(1)} all-gather(bf16[8192]{0:T(1024)(128)(2,1)} %param.42), channel_id=1, replica_groups=mesh['dp'=4,'fsdp'=8] {'dp','fsdp'}, dimensions={0}, use_global_device_ids=true | all-gather | bytes 540672 | tf_op jit(solution)/shard_map/all_gather | solution.py:314
  108.1 39.1 %all_gather.57 = bf16[262144]{0:T(1024)(128)(2,1)S(1)} all-gather(bf16[8192]{0:T(1024)(128)(2,1)S(1)} %copy-done.102), channel_id=1, replica_groups=mesh['dp'=4,'fsdp'=8] {'dp','fsdp'}, dimensions={0}, use_global_device_ids=true | all-gather | bytes 540672 | tf_op jit(solution)/shard_map/all_gather | solution.py:338
  148.4 40.8 %all_gather.59 = bf16[262144]{0:T(1024)(128)(2,1)S(1)} all-gather(bf16[8192]{0:T(1024)(128)(2,1)S(1)} %copy-done.103), channel_id=1, replica_groups=mesh['dp'=4,'fsdp'=8] {'dp','fsdp'}, dimensions={0}, use_global_device_ids=true | all-gather | bytes 540672 | tf_op jit(solution)/shard_map/all_gather | solution.py:339
  190.4 39.1 %all_gather.60 = bf16[262144]{0:T(1024)(128)(2,1)S(1)} all-gather(bf16[8192]{0:T(1024)(128)(2,1)S(1)} %copy-done.104), channel_id=1, replica_groups=mesh['dp'=4,'fsdp'=8] {'dp','fsdp'}, dimensions={0}, use_global_device_ids=true | all-gather | bytes 540672 | tf_op jit(solution)/shard_map/all_gather | solution.py:341
  246.0 29.4 %while.80 = (s32[]{:T(128)}, bf16[2,512,512]{2,1,0:T(8,128)(2,1)}, f32[2,8,512]{2,1,0:T(8,128)S(1)}, bf16[2,512,1536]{1,2,0:T(8,128)(2,1)S(1)}, s32[2]{0:T(128)S...) while((s32[]{:T(128)}, bf16[2,512,512]{2,1,0:T(8,128)(2,1)}, ...), condition=%wide.region_6.7_spmd, body=%wide.region_2.6_spmd.sunk | while | flops 562570752 | bytes 38939916 | solution.py:129
  292.9 20.7 %while.81 = (s32[]{:T(128)}, bf16[2,512,512]{2,1,0:T(8,128)(2,1)}, f32[2,8,512]{2,1,0:T(8,128)S(1)}, bf16[2,512,1536]{1,2,0:T(8,128)(2,1)}, s32[2]{0:T(128)S(1)}...) while((s32[]{:T(128)}, bf16[2,512,512]{2,1,0:T(8,128)(2,1)}, ...), condition=%wide.region_15.16_spmd, body=%wide.region_11.15_spmd.sunk | while | flops 563095040 | bytes 36842736 | solution.py:129
  324.0 24.4 %multiply_convert_fusion.4 = (bf16[1024,2048]{1,0:T(8,128)(2,1)}, f32[1024,2048]{1,0:T(8,128)}, f32[1024,2048]{1,0:T(8,128)}) fusion(bf16[512,2048]{1,0:T(8,128)(2,1)} %reshape.1536, f32[1024,512]{1,0:T(8,128)S(1)} %copy-done.9, f32[512]{0:T(512)S(1)} %copy-done.100, f32[512]{0:T(512)S(1)} %copy-done.92, f32[1024]{0:T(1024)S(1)} %fusion.137, ...), kind=kOutput, calls=%fused_computation.205 | convolution fusion | flops 2286419968 | bytes 25178112 | tf_op jit(solution)/shard_map/dot_general | solution.py:48
  352.7 5.3 add_convert_fusion.7
  363.0 20.4 %while.82 = (s32[]{:T(128)}, bf16[2,512,512]{2,1,0:T(8,128)(2,1)}, f32[2,8,512]{2,1,0:T(8,128)S(1)}, bf16[2,512,1024]{1,2,0:T(8,128)(2,1)}, s32[2]{0:T(128)S(1)}...) while((s32[]{:T(128)}, bf16[2,512,512]{2,1,0:T(8,128)(2,1)}, ...), condition=%wide.region_22.23_spmd, body=%wide.region_18.22_spmd.sunk | while | flops 562570752 | bytes 35794172 | solution.py:189
  391.3 24.1 %multiply_convert_fusion.3 = (bf16[1024,2048]{1,0:T(8,128)(2,1)}, f32[1024,2048]{1,0:T(8,128)}, f32[1024,2048]{1,0:T(8,128)}) fusion(bf16[512,2048]{1,0:T(8,128)(2,1)} %reshape.1547, f32[1024,512]{1,0:T(8,128)S(1)} %get-tuple-element.918, f32[512]{0:T(512)S(1)} %copy-done.98, f32[512]{0:T(512)S(1)} %copy-done.90, f32[1024]{0:T(1024)S(1)} %fusion.139, ...), kind=kOutput, calls=%fused_computation.192 | convolution fusion | flops 2286419968 | bytes 25178112 | tf_op jit(solution)/shard_map/dot_general | solution.py:48
  416.6 4.8 reshape.1548
  421.4 9.8 add_convert_fusion.1
  438.9 61.4 %while.83 = (s32[]{:T(128)}, bf16[2,512,512]{2,1,0:T(8,128)(2,1)}, bf16[2,512,1024]{2,1,0:T(8,128)(2,1)}, bf16[2,512,1024]{1,2,0:T(8,128)(2,1)}, s32[2]{0:T(128)...) while((s32[]{:T(128)}, bf16[2,512,512]{2,1,0:T(8,128)(2,1)}, ...), condition=%wide.region_30.31_spmd, body=%wide.region_27.30_spmd.sunk | while | flops 1377576448 | bytes 152169904 | solution.py:219
  448.5 5.1 multiply_reduce_fusion.15
  460.9 5.7 fusion.384
  479.2 5.1 multiply_reduce_fusion.15
  491.6 5.7 fusion.384
  504.0 8.5 add_convert_fusion
  549.5 50.8 %while.85 = (s32[]{:T(128)}, bf16[2,512,1536]{1,2,0:T(8,128)(2,1)}, bf16[2,512,1536]{1,2,0:T(8,128)(2,1)}, s32[2]{0:T(128)S(1)}, s32[2,4]{1,0:T(2,128)}, /*index...) while((s32[]{:T(128)}, bf16[2,512,1536]{1,2,0:T(8,128)(2,1)}, ...), condition=%wide.region_44.45_spmd, body=%wide.region_41.44_spmd.sunk | while | flops 1380722176 | bytes 147975552 | solution.py:157
  559.5 5.7 fusion.418
  584.9 5.7 fusion.418
  602.2 48.0 %while.84 = (s32[]{:T(128)}, bf16[2,512,1536]{1,2,0:T(8,128)(2,1)}, bf16[2,512,1536]{1,2,0:T(8,128)(2,1)}, s32[2]{0:T(128)S(1)}, s32[2,4]{1,0:T(2,128)S(1)}, /*i...) while((s32[]{:T(128)}, bf16[2,512,1536]{1,2,0:T(8,128)(2,1)}, ...), condition=%wide.region_36.37_spmd, body=%wide.region_33.36_spmd.sunk | while | flops 1380197888 | bytes 139586880 | solution.py:157
  610.9 5.7 fusion.400
  634.7 5.7 fusion.400
  650.1 5.8 convolution_bitcast_fusion.1
  661.8 5.3 copy.233
  697.7 42.4 %psum.7 = s32[523]{0:T(1024)S(1)} all-reduce(s32[523]{0:T(1024)S(1)} %convert_reduce_fusion), channel_id=1, replica_groups=mesh['dp'=4,'fsdp'=8] {'dp','fsdp'}, use_global_device_ids=true, to_apply=%region_72.73 | all-reduce | flops 523 | bytes 4184 | tf_op jit(solution)/shard_map/psum | solution.py:470
  743.5 4.8 copy.160
  748.3 4.9 fusion.151
  758.1 41.0 %all-reduce.15 = (f32[2048]{0:T(1024)S(1)}, f32[3072]{0:T(1024)S(1)}) all-reduce(f32[2048]{0:T(1024)S(1)} %pad_maximum_fusion.1, f32[3072]{0:T(1024)S(1)} %constant_dynamic-update-slice_fusion.5), channel_id=6, replica_groups=mesh['dp'=4,'fsdp'=8] {'dp','fsdp'}, use_global_device_ids=true, to_apply=%region_55.56.clone | all-reduce | flops 5120 | bytes 40960
  810.6 349.4 %all-reduce.20.cloned.1.call-done = (f32[786432]{0:T(1024)}, f32[262144]{0:T(1024)}, f32[1048576]{0:T(1024)}, f32[1048576]{0:T(1024)}, f32[786432]{0:T(1024)}, /...) async-done(((f32[786432]{0:T(1024)}, f32[262144]{0:T(1024)}, f32[1048576]{0:T(1024)}, ...) | async-done | bytes 29360144
  (669 shorter events, 378.2 us)
Async XLA Ops:
  7.2 99.0 %copy-start.13 = (bf16[2,512,512]{2,1,0:T(8,128)(2,1)S(1)}, bf16[2,512,512]{2,1,0:T(8,128)(2,1)}, u32[]{:S(2)}) copy-start(bf16[2,512,512]{2,1,0:T(8,128)(2,1)} %param.35) | copy-start | bytes 3145732
  7.2 100.9 %copy-start.102 = (bf16[8192]{0:T(1024)(128)(2,1)S(1)}, bf16[8192]{0:T(1024)(128)(2,1)}, u32[]{:S(2)}) copy-start(bf16[8192]{0:T(1024)(128)(2,1)} %param.47) | copy-start | bytes 49156
  7.2 141.2 %copy-start.103 = (bf16[8192]{0:T(1024)(128)(2,1)S(1)}, bf16[8192]{0:T(1024)(128)(2,1)}, u32[]{:S(2)}) copy-start(bf16[8192]{0:T(1024)(128)(2,1)} %param.48) | copy-start | bytes 49156
  7.2 225.3 %all-gather.16.cloned.1.call-start = ((), (), s32[]{:S(2)}) async-start(), calls=%async_computation.4 | async-start | bytes 1081344 | tf_op jit(solution)/shard_map/all_gather | solution.py:340
  8.0 227.0 %all-gather.8.cloned.1.call-start = ((), (), s32[]{:S(2)}) async-start(), calls=%async_computation | async-start | bytes 1622016 | tf_op jit(solution)/shard_map/all_gather | solution.py:313
  8.7 272.2 %all-gather.14.cloned.1.call-start = ((), (), s32[]{:S(2)}) async-start(), calls=%async_computation.3 | async-start | bytes 1622016 | tf_op jit(solution)/shard_map/all_gather | solution.py:337
  9.4 310.3 %all-gather.10.cloned.1.call-start = ((), (), s32[]{:S(2)}) async-start(), calls=%async_computation.1 | async-start | bytes 2162688 | tf_op jit(solution)/shard_map/all_gather | solution.py:315
  10.0 338.4 %all-gather.12.cloned.1.call-start = ((), (), s32[]{:S(2)}) async-start(), calls=%async_computation.2 | async-start | bytes 2162688 | tf_op jit(solution)/shard_map/all_gather | solution.py:316
  10.6 376.3 %all-gather.18.cloned.1.call-start = ((), (), s32[]{:S(2)}) async-start(), calls=%async_computation.5 | async-start | bytes 2162688 | tf_op jit(solution)/shard_map/all_gather | solution.py:342
  11.2 405.4 %all-gather.20.cloned.1.call-start = ((), (), s32[]{:S(2)}) async-start(), calls=%async_computation.6 | async-start | bytes 2162688 | tf_op jit(solution)/shard_map/all_gather | solution.py:343
  11.9 1148.0 %all-reduce.20.cloned.1.call-start = ((), (), s32[]{:S(2)}) async-start(), calls=%async_computation.7 | async-start | bytes 58720256
  56.5 174.1 %copy-start.96 = (f32[512]{0:T(512)}, f32[512]{0:T(512)S(1)}, u32[]{:S(2)}) copy-start(f32[512]{0:T(512)S(1)} %get-tuple-element.907) | copy-start | bytes 6148
  58.0 132.4 %copy-start.104 = (bf16[8192]{0:T(1024)(128)(2,1)S(1)}, bf16[8192]{0:T(1024)(128)(2,1)}, u32[]{:S(2)}) copy-start(bf16[8192]{0:T(1024)(128)(2,1)} %param.50) | copy-start | bytes 49156
  60.9 169.8 %copy-start.11 = (bf16[2,512,512]{2,1,0:T(8,128)(2,1)S(1)}, bf16[2,512,512]{2,1,0:T(8,128)(2,1)}, u32[]{:S(2)}) copy-start(bf16[2,512,512]{2,1,0:T(8,128)(2,1)} %param.34) | copy-start | bytes 3145732
  106.2 124.9 %copy-start.94 = (f32[512]{0:T(512)}, f32[512]{0:T(512)S(1)}, u32[]{:S(2)}) copy-start(f32[512]{0:T(512)S(1)} %get-tuple-element.891) | copy-start | bytes 6148
  231.1 10.6 copy-start.65
  275.5 9.8 copy-start.4
  275.5 9.8 copy-start.70
  279.1 44.8 %copy-start.74 = (f32[1024]{0:T(1024)}, f32[1024]{0:T(1024)S(1)}, u32[]{:S(2)}) copy-start(f32[1024]{0:T(1024)S(1)} %broadcast_multiply_fusion.2) | copy-start | bytes 12292
  280.9 43.0 %copy-start.78 = (f32[1024]{0:T(1024)}, f32[1024]{0:T(1024)S(1)}, u32[]{:S(2)}) copy-start(f32[1024]{0:T(1024)S(1)} %fusion.137) | copy-start | bytes 12292
  292.9 20.8 %copy-start.14 = (bf16[2,512,512]{2,1,0:T(8,128)(2,1)S(1)}, bf16[2,512,512]{2,1,0:T(8,128)(2,1)}, u32[]{:S(2)}) copy-start(bf16[2,512,512]{2,1,0:T(8,128)(2,1)} %param.35) | copy-start | bytes 3145732
  292.9 20.8 %copy-start.42 = (bf16[512,512]{1,0:T(8,128)(2,1)S(1)}, bf16[512,512]{1,0:T(8,128)(2,1)}, u32[]{:S(2)}) copy-start(bf16[512,512]{1,0:T(8,128)(2,1)} %reshape.1541) | copy-start | bytes 1572868
  386.4 48.3 %copy-start.5 = (f32[1024,512]{1,0:T(8,128)}, f32[1024,512]{1,0:T(8,128)S(1)}, u32[]{:S(2)}) copy-start(f32[1024,512]{1,0:T(8,128)S(1)} %get-tuple-element.918) | copy-start | bytes 6291460
  386.4 48.2 %copy-start.76 = (f32[1024]{0:T(1024)}, f32[1024]{0:T(1024)S(1)}, u32[]{:S(2)}) copy-start(f32[1024]{0:T(1024)S(1)} %broadcast_multiply_fusion) | copy-start | bytes 12292
  386.8 47.8 %copy-start.80 = (f32[1024]{0:T(1024)}, f32[1024]{0:T(1024)S(1)}, u32[]{:S(2)}) copy-start(f32[1024]{0:T(1024)S(1)} %fusion.139) | copy-start | bytes 12292
  421.3 9.9 copy-start.57
  504.0 8.5 copy-start.10
  504.0 8.5 copy-start.55
  504.0 8.5 copy-start.75
  549.5 52.7 %copy-start.71 = (f32[2,8,512]{2,1,0:T(8,128)S(1)}, f32[2,8,512]{2,1,0:T(8,128)}, u32[]{:S(2)}) copy-start(f32[2,8,512]{2,1,0:T(8,128)} %copy-done.70) | copy-start | bytes 98308
  549.5 52.7 %copy-start.130 = (s32[2,4]{1,0:T(2,128)S(1)}, s32[2,4]{1,0:T(2,128)}, u32[]{:S(2)}) copy-start(s32[2,4]{1,0:T(2,128)} %copy-done.129) | copy-start | bytes 100
  695.8 44.2 %copy-start.113 = (s32[523]{0:T(1024)S(1)}, s32[523]{0:T(1024)}, u32[]{:S(2)}) copy-start(s32[523]{0:T(1024)} %param.40) | copy-start | bytes 6280
  (127 other events, 455.9 us)
Sparse Core Ops, SparseCore 0:
  11.1 56.4 all-gather.15
  70.6 54.7 all-gather.7
  128.3 54.3 all-gather.13
  185.6 56.1 all-gather.9
  244.6 55.2 all-gather.11
  302.8 55.3 all-gather.17
  361.2 55.3 all-gather.19
  696.0 463.9 all-reduce.19
where the time goes:
time: 1190 us; the launch traced here: 1180 us
  waiting for transfers between devices  355 us (30%)
  blocking collectives  288 us (24%)
  matrix products  276 us (23%)
  local copies, waits for them, and re-layouts  181 us (15%)
  other arithmetic  57.1 us (5%)
  between operations  15.9 us (1%)
    unnamed x9, waiting for transfers between devices  354 us
    unnamed x2, blocking collectives  83.2 us
    dot_general x11, matrix products, forward_product(): return jnp.dot(left, right, preferred_element_type=jnp.float32)  75.7 us
    unnamed x283, local copies, waits for them, and re-layouts  50.9 us
    all_gather x1, blocking collectives, local(): lax.all_gather(enc_attn_out, ('dp', 'fsdp'), axis=0, tiled=True)  43.7 us
    psum x1, blocking collectives, local(): summed_counts = lax.psum(local_counts, ('dp', 'fsdp'))  42.4 us
    all_gather x1, blocking collectives, local(): lax.all_gather(dec_cross_q, ('dp', 'fsdp'), axis=0, tiled=True)  40.8 us
    dot_general x11, matrix products, back_product(): lax.dot_general(left, right, (((1,), (1,)), ((), ())), preferred_element_...  40.8 us
  transfers between devices with their start and end apart: 8, of which 2 were waited for; matrix products, arithmetic and copies ran while one was open for 19% of the time, Pallas kernels for 0%

commit v1 on v0

v1 whole, which is shorter than its diff:
```python
import functools
import math
import jax
import jax.numpy as jnp
from jax import lax
from jax.experimental import pallas as pl
from jax.experimental.pallas import tpu as pltpu
from jax.sharding import PartitionSpec as P

D = 512
HEAD = 64
FF = 2048
VOCAB = 523
SLOT = 512
SHARDS = 32
BLOCKS = FF // D
EPS = 1e-05
PAIR = 2 * HEAD
PAIRS = D // PAIR
GROUP = 16
MASKED = -(2.0**30)
BF = jnp.bfloat16
F32 = jnp.float32
VMEM_LIMIT = 56 << 20

SELF_ROWS, SELF_IN, SELF_OUT = 64, 0, 48
FFN_ROWS, FFN_IN, FFN_OUT = 128, 0, 64
CROSS_ROWS, CROSS_Q, CROSS_KV, CROSS_OUT = 64, 0, 16, 48


def nn(left, right):
    return lax.dot_general(left, right, (((1,), (0,)), ((), ())), preferred_element_type=F32)


def nt(left, right):
    return lax.dot_general(left, right, (((1,), (1,)), ((), ())), preferred_element_type=F32)


def wide(ref, start, block):
    first = start + 16 * block
    return ref[:, :, first : first + 16, :].reshape(D, D)


def tall(ref, start, block):
    return ref[4 * block : 4 * block + 4, :, start : start + 64, :].reshape(D, D)


def put_wide(core, keep_ref, send_ref, start, block, value):
    rows = slice(start + 16 * block, start + 16 * block + 16)
    shards = value.reshape(SHARDS // 2, 2, 16, D)
    keep_ref[:, rows, :] = jnp.where(core == 0, shards[:, 0], shards[:, 1]).astype(BF)
    send_ref[:, rows, :] = jnp.where(core == 0, shards[:, 1], shards[:, 0]).astype(BF)


def put_tall(core, keep_ref, send_ref, start, block, value):
    rows = slice(start, start + 64)
    lead = slice(4 * block, 4 * block + 4)
    shards = value.reshape(4, 2, 64, D)
    keep_ref[lead, rows, :] = jnp.where(core == 0, shards[:, 0], shards[:, 1]).astype(BF)
    send_ref[lead, rows, :] = jnp.where(core == 0, shards[:, 1], shards[:, 0]).astype(BF)


class Weights:
    def __init__(self, own, other, places, half):
        self.arrays = (own[0], other[0], own[1], other[1])
        self.places = places
        self.half = half


def weight_copies(pieces, places, half, core, ref, sems, low, high):
    copies = []
    for number, place in enumerate(places):
        first, last = max(low, number * half), min(high, (number + 1) * half)
        if first < last:
            source = slice(place + first - number * half, place + last - number * half)
            for other in range(2):
                copies.append(
                    pltpu.make_async_copy(
                        pieces[2 * number + other].at[:, source, :],
                        ref.at[:, core if other == 0 else 1 - core, first - low : last - low, :],
                        sems.at[2 * number + other],
                    )
                )
    return copies


def on_first_slot(action, copies):
    @pl.when(pl.program_id(0) == 0)
    def _():
        for copy in copies:
            getattr(copy, action)()


def norm_grad_rows(ref, gains_and_shifts):
    rows = jnp.concatenate(gains_and_shifts + [jnp.zeros((8 - len(gains_and_shifts), D), F32)], 0)
    add_up(ref, rows)


def last_slot():
    return pl.program_id(0) == pl.num_programs(0) - 1


def lanes_of(pair):
    return slice(pair * PAIR, (pair + 1) * PAIR)


def normalize(values):
    centered = values - jnp.mean(values, -1, keepdims=True)
    scale = lax.rsqrt(jnp.mean(centered * centered, -1, keepdims=True) + EPS)
    return centered * scale, scale


def norm_backward(grad_normed, unit, scale, gain):
    grad_unit = grad_normed * gain
    first = jnp.mean(grad_unit, -1, keepdims=True)
    second = jnp.mean(grad_unit * unit, -1, keepdims=True)
    grad_gain = jnp.sum(grad_normed * unit, 0, keepdims=True)
    grad_shift = jnp.sum(grad_normed, 0, keepdims=True)
    return scale * (grad_unit - first - unit * second), grad_gain, grad_shift


def gelu_both(hidden):
    size = jnp.abs(hidden)
    ratio = 1.0 / (1.0 + (0.3275911 / math.sqrt(2.0)) * size)
    bell = jnp.exp(-0.5 * hidden * hidden)
    series = 0.5 * 1.061405429
    for factor in (-1.453152027, 1.421413741, -0.284496736, 0.254829592):
        series = series * ratio + 0.5 * factor
    tail = series * ratio * bell
    share = jnp.where(hidden >= 0, 1.0 - tail, tail)
    return hidden * share, share + hidden * bell * (1.0 / math.sqrt(2.0 * math.pi))


def lane_index():
    return lax.broadcasted_iota(jnp.int32, (1, 128), 1)


def query_extra(kind):
    place = lax.broadcasted_iota(jnp.int32, (SLOT, 128), 0)
    lane = lax.broadcasted_iota(jnp.int32, (SLOT, 128), 1)
    return (lax.shift_right_logical(place, kind + 7) == lane).astype(F32).astype(BF)


def key_extra(kind, lengths):
    place = lax.broadcasted_iota(jnp.int32, (SLOT, 128), 0)
    lane = lax.broadcasted_iota(jnp.int32, (SLOT, 128), 1)
    size = lax.shift_left(jnp.int32(128), kind)
    within = place & (size - 1)
    limit = jnp.where(
        lane == 0, lengths[0], jnp.where(lane == 1, lengths[1], jnp.where(lane == 2, lengths[2], lengths[3]))
    )
    allowed = (lax.shift_right_logical(place, kind + 7) == lane) & (within < limit)
    return jnp.where(allowed | (lane >= 4), 0.0, MASKED).astype(BF)


def halves():
    lane = lane_index()
    return ((lane < HEAD).astype(F32).astype(BF), (lane >= HEAD).astype(F32).astype(BF))


def future(rows, columns, first):
    row = lax.broadcasted_iota(jnp.int32, (rows, columns), 0)
    column = lax.broadcasted_iota(jnp.int32, (rows, columns), 1) + first
    return row <= column


def attend(query_of, key_of, value_of, store, kind, lengths, causal):
    step = 256 if causal else SLOT
    query_lanes = query_extra(kind)
    key_lanes = key_extra(kind, lengths)
    ones = jnp.ones((HEAD, SLOT), BF)
    logsums = []
    for pair in range(PAIRS):
        queries = query_of(pair) * BF(HEAD**-0.5)
        keys = jnp.concatenate([key_of(pair), key_lanes], 1)
        values = value_of(pair).T
        parts = []
        for half, mask in enumerate(halves()):
            own = jnp.concatenate([queries * mask, query_lanes], 1)
            head_values = jnp.concatenate([values[:HEAD], ones] if half == 0 else [ones, values[HEAD:]], 0)
            columns, sums = [], []
            for first in range(0, SLOT, step):
                seen = first + step if causal else SLOT
                scores = nt(keys[:seen], own[first : first + step])
                if causal:
                    scores = jnp.where(future(seen, step, first), scores, MASKED)
                largest = jnp.max(scores, 0, keepdims=True)
                powers = jnp.exp(scores - largest).astype(BF)
                context = nn(head_values[:, :seen], powers)
                total = context[HEAD : HEAD + 1] if half == 0 else context[0:1]
                columns.append((context[:HEAD] if half == 0 else context[HEAD:]) / total)
                sums.append(largest + jnp.log(total))
            parts.append(jnp.concatenate(columns, 1))
            logsums.append(jnp.concatenate(sums, 1))
        store(pair, jnp.concatenate(parts, 0).T)
    spread = jnp.concatenate([jnp.broadcast_to(row, (GROUP, SLOT)) for row in logsums], 0).T
    return split(spread, 4)


def split(values, first):
    lane = lane_index() % GROUP
    high = values.astype(BF).astype(F32)
    rest = values - high
    middle = rest.astype(BF).astype(F32)
    low = rest - middle
    terms = jnp.where(
        lane == first, high, jnp.where(lane == first + 1, middle, jnp.where(lane == first + 2, low, 0.0))
    )
    return (-terms).astype(BF)


def attend_back(query_of, key_of, value_of, grad_of, contexts, grads, store, logsums, kind, lengths, causal):
    step = 256 if causal else SLOT
    query_lanes = query_extra(kind) + logsums
    key_lanes = key_extra(kind, lengths)
    products = grads.astype(F32) * contexts
    high = products.astype(BF)
    low = (products - high.astype(F32)).astype(BF)
    source = lax.broadcasted_iota(jnp.int32, (D, 128), 0) // HEAD
    target = lax.broadcasted_iota(jnp.int32, (D, 128), 1) // GROUP
    picker = (source == target).astype(F32).astype(BF)
    inner_lanes = split(nn(high, picker) + nn(low, picker), 0)
    lane = lane_index()
    within, group = lane % GROUP, lane // GROUP
    for pair in range(PAIRS):
        queries = query_of(pair) * BF(HEAD**-0.5)
        keys, values, grad_context = key_of(pair), value_of(pair), grad_of(pair)
        keys_t, queries_t, grad_t = keys.T, queries.T, grad_context.T
        grad_queries, grad_keys, grad_values = [], [], []
        for half, mask in enumerate(halves()):
            head = 2 * pair + half
            sum_lanes = ((group == head) & (within >= 4) & (within < 7)).astype(F32).astype(BF)
            one_lanes = ((group == head) & (within < 3)).astype(F32).astype(BF)
            left = jnp.concatenate([keys, key_lanes + sum_lanes], 1)
            right = jnp.concatenate([queries * mask, query_lanes], 1)
            value_left = jnp.concatenate([values, jnp.broadcast_to(one_lanes, (SLOT, 128))], 1)
            grad_right = jnp.concatenate([grad_context * mask, inner_lanes], 1)
            rows = slice(half * HEAD, half * HEAD + HEAD)
            head_keys, head_queries, head_grads = keys_t[rows], queries_t[rows], grad_t[rows]
            for_queries, for_keys, for_values = [], None, None
            for first in range(0, SLOT, step):
                seen = first + step if causal else SLOT
                here = slice(first, first + step)
                scores = nt(left[:seen], right[here])
                if causal:
                    scores = jnp.where(future(seen, step, first), scores, MASKED)
                weights = jnp.exp(scores)
                grad_weights = nt(value_left[:seen], grad_right[here])
                grad_scores = (weights * grad_weights).astype(BF)
                for_queries.append(nn(head_keys[:, :seen], grad_scores))
                key_part = nt(head_queries[:, here], grad_scores)
                value_part = nt(head_grads[:, here], weights.astype(BF))
                if seen < SLOT:
                    none = jnp.zeros((HEAD, SLOT - seen), F32)
                    key_part = jnp.concatenate([key_part, none], 1)
                    value_part = jnp.concatenate([value_part, none], 1)
                for_keys = key_part if for_keys is None else for_keys + key_part
                for_values = value_part if for_values is None else for_values + value_part
            grad_queries.append(jnp.concatenate(for_queries, 1))
            grad_keys.append(for_keys)
            grad_values.append(for_values)
        store(
            pair,
            (jnp.concatenate(grad_queries, 0) * HEAD**-0.5).T.astype(BF),
            jnp.concatenate(grad_keys, 0).T.astype(BF),
            jnp.concatenate(grad_values, 0).T.astype(BF),
        )


def lengths_at(ref, slot):
    return [ref[slot, entry] for entry in range(4)]


def at(ref, start):
    return lambda pair: ref[0, :, start + pair * PAIR : start + (pair + 1) * PAIR]


def add_up(ref, value):
    slot = pl.program_id(0)

    @pl.when(slot == 0)
    def _():
        ref[...] = value

    @pl.when(slot > 0)
    def _():
        ref[...] += value


def project_kernel(me_ref, x_ref, w0, w1, w2, w3, norm_ref, qkv_ref, weights_ref, sems, *, places, half):
    copies = weight_copies((w0, w1, w2, w3), places, half, me_ref[4], weights_ref, sems, SELF_IN, SELF_OUT)
    on_first_slot("start", copies)
    unit, _ = normalize(x_ref[0].astype(F32))
    normed = (unit * norm_ref[0:1] + norm_ref[1:2]).astype(BF)
    on_first_slot("wait", copies)
    for block in range(3):
        qkv_ref[0, :, block * D : (block + 1) * D] = nn(normed, wide(weights_ref, 0, block)).astype(BF)


def keep_context(context_ref, rest_ref):
    def store(pair, context):
        high = context.astype(BF)
        context_ref[0, :, lanes_of(pair)] = high
        rest_ref[0, :, lanes_of(pair)] = (context - high.astype(F32)).astype(BF)

    return store


def self_attend_kernel(
    kind_ref,
    lengths_ref,
    me_ref,
    x_ref,
    qkv_ref,
    w0,
    w1,
    w2,
    w3,
    out_ref,
    context_ref,
    rest_ref,
    sums_ref,
    weights_ref,
    sems,
    *,
    places,
    half,
    causal,
):
    slot = pl.program_id(0)
    copies = weight_copies((w0, w1, w2, w3), places, half, me_ref[4], weights_ref, sems, SELF_OUT, SELF_ROWS)
    on_first_slot("start", copies)
    sums_ref[0] = attend(
        at(qkv_ref, 0),
        at(qkv_ref, D),
        at(qkv_ref, 2 * D),
        keep_context(context_ref, rest_ref),
        kind_ref[slot],
        lengths_at(lengths_ref, slot),
        causal,
    )
    on_first_slot("wait", copies)
    out_ref[0] = x_ref[0].astype(F32) + nn(context_ref[0], wide(weights_ref, 0, 0))


def cross_forward_kernel(
    kind_ref,
    lengths_ref,
    me_ref,
    r_ref,
    memory_ref,
    w0,
    w1,
    w2,
    w3,
    norm_ref,
    out_ref,
    q_ref,
    kv_ref,
    context_ref,
    rest_ref,
    sums_ref,
    weights_ref,
    sems,
    *,
    places,
    half,
):
    slot = pl.program_id(0)
    copies = weight_copies((w0, w1, w2, w3), places, half, me_ref[4], weights_ref, sems, 0, CROSS_ROWS)
    on_first_slot("start", copies)
    values = r_ref[0]
    unit, _ = normalize(values)
    normed = (unit * norm_ref[2:3] + norm_ref[3:4]).astype(BF)
    memory = memory_ref[0]
    on_first_slot("wait", copies)
    q_ref[0] = nn(normed, wide(weights_ref, CROSS_Q, 0)).astype(BF)
    for block in range(2):
        kv_ref[0, :, block * D : (block + 1) * D] = nn(memory, wide(weights_ref, CROSS_KV, block)).astype(BF)
    sums_ref[0] = attend(
        at(q_ref, 0),
        at(kv_ref, 0),
        at(kv_ref, D),
        keep_context(context_ref, rest_ref),
        kind_ref[slot],
        lengths_at(lengths_ref, slot),
        False,
    )
    out_ref[0] = values + nn(context_ref[0], wide(weights_ref, CROSS_OUT, 0))


def ffn_forward_kernel(
    me_ref, r_ref, w0, w1, w2, w3, norm_ref, out_ref, active_ref, slope_ref, weights_ref, sems, *, places, half
):
    copies = weight_copies((w0, w1, w2, w3), places, half, me_ref[4], weights_ref, sems, 0, FFN_ROWS)
    on_first_slot("start", copies)
    values = r_ref[0]
    unit, _ = normalize(values)
    normed = (unit * norm_ref[2:3] + norm_ref[3:4]).astype(BF)
    total = values
    on_first_slot("wait", copies)
    for block in range(BLOCKS):
        active, slope = gelu_both(nn(normed, wide(weights_ref, FFN_IN, block)))
        active = active.astype(BF)
        active_ref[0, :, block * D : (block + 1) * D] = active
        slope_ref[0, :, block * D : (block + 1) * D] = slope.astype(BF)
        total = total + nn(active, tall(weights_ref, FFN_OUT, block))
    out_ref[0] = total.astype(BF)


def ffn_back(grad_out, unit, scale, normed, gain, active_of, slope_of, w_ref, sums_ref):
    low = grad_out.astype(BF)
    normed_t = normed.T
    grad_normed = None
    for block in range(BLOCKS):
        grad_active = nt(low, tall(w_ref, FFN_OUT, block))
        grad_hidden = (grad_active * slope_of(block)).astype(BF)
        add_up(sums_ref.at[1, block], nn(active_of(block).T, low))
        add_up(sums_ref.at[0, block], nn(normed_t, grad_hidden))
        part = nt(grad_hidden, wide(w_ref, FFN_IN, block))
        grad_normed = part if grad_normed is None else grad_normed + part
    grad, grad_gain, grad_shift = norm_backward(grad_normed, unit, scale, gain)
    return grad_out + grad, grad_gain, grad_shift


def ffn_put(core, sums_ref, keep_ref, send_ref):
    @pl.when(last_slot())
    def _():
        for block in range(BLOCKS):
            put_wide(core, keep_ref, send_ref, FFN_IN, block, sums_ref[0, block])
            put_tall(core, keep_ref, send_ref, FFN_OUT, block, sums_ref[1, block])


def ffn_both_kernel(
    me_ref,
    r_ref,
    cotangent_ref,
    w0,
    w1,
    w2,
    w3,
    norm_ref,
    out_ref,
    grad_ref,
    keep_ref,
    send_ref,
    norm_grad_ref,
    weights_ref,
    sems,
    active_ref,
    slope_ref,
    sums_ref,
    *,
    places,
    half,
):
    copies = weight_copies((w0, w1, w2, w3), places, half, me_ref[4], weights_ref, sems, 0, FFN_ROWS)
    on_first_slot("start", copies)
    values = r_ref[0]
    unit, scale = normalize(values)
    gain = norm_ref[4:5]
    normed = (unit * gain + norm_ref[5:6]).astype(BF)
    total = values
    on_first_slot("wait", copies)
    for block in range(BLOCKS):
        active, slope = gelu_both(nn(normed, wide(weights_ref, FFN_IN, block)))
        active = active.astype(BF)
        active_ref[block] = active
        slope_ref[block] = slope
        total = total + nn(active, tall(weights_ref, FFN_OUT, block))
    out_ref[0] = total.astype(BF)
    grad, grad_gain, grad_shift = ffn_back(
        cotangent_ref[0].astype(F32),
        unit,
        scale,
        normed,
        gain,
        lambda block: active_ref[block],
        lambda block: slope_ref[block],
        weights_ref,
        sums_ref,
    )
    grad_ref[0] = grad
    norm_grad_rows(norm_grad_ref, [grad_gain, grad_shift])
    ffn_put(me_ref[4], sums_ref, keep_ref, send_ref)


def ffn_backward_kernel(
    me_ref,
    grad_out_ref,
    r_ref,
    active_ref,
    slope_ref,
    w0,
    w1,
    w2,
    w3,
    norm_ref,
    grad_ref,
    keep_ref,
    send_ref,
    norm_grad_ref,
    weights_ref,
    sems,
    sums_ref,
    *,
    places,
    half,
):
    copies = weight_copies((w0, w1, w2, w3), places, half, me_ref[4], weights_ref, sems, 0, FFN_ROWS)
    on_first_slot("start", copies)
    unit, scale = normalize(r_ref[0])
    gain = norm_ref[2:3]
    normed = (unit * gain + norm_ref[3:4]).astype(BF)
    on_first_slot("wait", copies)
    grad, grad_gain, grad_shift = ffn_back(
        grad_out_ref[0],
        unit,
        scale,
        normed,
        gain,
        lambda block: active_ref[0, :, block * D : (block + 1) * D],
        lambda block: slope_ref[0, :, block * D : (block + 1) * D].astype(F32),
        weights_ref,
        sums_ref,
    )
    grad_ref[0] = grad
    norm_grad_rows(norm_grad_ref, [grad_gain, grad_shift])
    ffn_put(me_ref[4], sums_ref, keep_ref, send_ref)


def attend_back_kernel(
    kind_ref,
    lengths_ref,
    me_ref,
    grad_out_ref,
    q_ref,
    kv_ref,
    context_ref,
    rest_ref,
    sums_in_ref,
    w0,
    w1,
    w2,
    w3,
    proj_ref,
    weights_ref,
    sems,
    low_ref,
    *,
    places,
    half,
    causal,
    start,
    key_at,
):
    slot = pl.program_id(0)
    copies = weight_copies((w0, w1, w2, w3), places, half, me_ref[4], weights_ref, sems, start, start + 16)
    on_first_slot("start", copies)
    on_first_slot("wait", copies)
    low_ref[0] = nt(grad_out_ref[0].astype(BF), wide(weights_ref, 0, 0)).astype(BF)

    def store(pair, grad_query, grad_key, grad_value):
        for number, value in enumerate((grad_query, grad_key, grad_value)):
            proj_ref[0, :, number * D + pair * PAIR : number * D + (pair + 1) * PAIR] = value

    attend_back(
        at(q_ref, 0),
        at(kv_ref, key_at),
        at(kv_ref, key_at + D),
        at(low_ref, 0),
        context_ref[0].astype(F32) + rest_ref[0].astype(F32),
        low_ref[0],
        store,
        sums_in_ref[0],
        kind_ref[slot],
        lengths_at(lengths_ref, slot),
        causal,
    )


def cross_weight_kernel(
    me_ref,
    grad_out_ref,
    r_ref,
    memory_ref,
    context_ref,
    proj_ref,
    cotangent_ref,
    w0,
    w1,
    w2,
    w3,
    norm_ref,
    grad_ref,
    memory_grad_ref,
    keep_ref,
    send_ref,
    norm_grad_ref,
    weights_ref,
    sems,
    sums_ref,
    *,
    places,
    half,
):
    copies = weight_copies((w0, w1, w2, w3), places, half, me_ref[4], weights_ref, sems, 0, CROSS_OUT)
    on_first_slot("start", copies)
    grad_out = grad_out_ref[0]
    unit, scale = normalize(r_ref[0])
    gain = norm_ref[2:3]
    normed_t = (unit * gain + norm_ref[3:4]).astype(BF).T
    memory_t = memory_ref[0].T
    for_query, for_key, for_value = (proj_ref[0, :, part * D : (part + 1) * D] for part in range(3))
    add_up(sums_ref.at[3], nn(context_ref[0].T, grad_out.astype(BF)))
    add_up(sums_ref.at[0], nn(normed_t, for_query))
    add_up(sums_ref.at[1], nn(memory_t, for_key))
    add_up(sums_ref.at[2], nn(memory_t, for_value))
    on_first_slot("wait", copies)
    memory_grad_ref[0] = (
        cotangent_ref[0].astype(F32)
        + nt(for_key, wide(weights_ref, CROSS_KV, 0))
        + nt(for_value, wide(weights_ref, CROSS_KV, 1))
    )
    grad_normed = nt(for_query, wide(weights_ref, CROSS_Q, 0))
    grad, grad_gain, grad_shift = norm_backward(grad_normed, unit, scale, gain)
    grad_ref[0] = grad_out + grad
    norm_grad_rows(norm_grad_ref, [grad_gain, grad_shift])

    @pl.when(last_slot())
    def _():
        core = me_ref[4]
        put_wide(core, keep_ref, send_ref, CROSS_Q, 0, sums_ref[0])
        put_wide(core, keep_ref, send_ref, CROSS_KV, 0, sums_ref[1])
        put_wide(core, keep_ref, send_ref, CROSS_KV, 1, sums_ref[2])
        put_wide(core, keep_ref, send_ref, CROSS_OUT, 0, sums_ref[3])


def self_weight_kernel(
    me_ref, grad_out_ref, x_ref, context_ref, proj_ref, norm_ref, keep_ref, send_ref, sums_ref
):
    unit, _ = normalize(x_ref[0].astype(F32))
    normed_t = (unit * norm_ref[0:1] + norm_ref[1:2]).astype(BF).T
    for block in range(3):
        add_up(sums_ref.at[block], nn(normed_t, proj_ref[0, :, block * D : (block + 1) * D]))
    add_up(sums_ref.at[3], nn(context_ref[0].T, grad_out_ref[0].astype(BF)))

    @pl.when(last_slot())
    def _():
        core = me_ref[4]
        for block in range(3):
            put_wide(core, keep_ref, send_ref, SELF_IN, block, sums_ref[block])
        put_wide(core, keep_ref, send_ref, SELF_OUT, 0, sums_ref[3])


def self_rows_kernel(
    me_ref,
    grad_out_ref,
    x_ref,
    proj_ref,
    w0,
    w1,
    w2,
    w3,
    norm_ref,
    grad_ref,
    norm_grad_ref,
    weights_ref,
    sems,
    *,
    places,
    half,
):
    copies = weight_copies((w0, w1, w2, w3), places, half, me_ref[4], weights_ref, sems, SELF_IN, SELF_OUT)
    on_first_slot("start", copies)
    unit, scale = normalize(x_ref[0].astype(F32))
    on_first_slot("wait", copies)
    grad_normed = None
    for block in range(3):
        part = nt(proj_ref[0, :, block * D : (block + 1) * D], wide(weights_ref, 0, block))
        grad_normed = part if grad_normed is None else grad_normed + part
    grad, grad_gain, grad_shift = norm_backward(grad_normed, unit, scale, norm_ref[0:1])
    grad_ref[0] = (grad_out_ref[0] + grad).astype(BF)
    norm_grad_rows(norm_grad_ref, [grad_gain, grad_shift])


def per_slot(*shape):
    return pl.BlockSpec((1,) + shape, lambda slot: (slot,) + (0,) * len(shape))


def whole_block(*shape):
    return pl.BlockSpec(shape, lambda slot: (0,) * len(shape))


def scalars():
    return pl.BlockSpec(memory_space=pltpu.SMEM)


def call(kernel, name, slots, ins, outs, scratch, *args, flops=0):
    return pl.pallas_call(
        kernel,
        name=name,
        grid=(slots,),
        in_specs=ins,
        out_specs=[spec for spec, _, _ in outs],
        out_shape=[jax.ShapeDtypeStruct(shape, dtype) for _, shape, dtype in outs],
        scratch_shapes=scratch,
        cost_estimate=pl.CostEstimate(flops=flops, bytes_accessed=8 << 20, transcendentals=0),
        compiler_params=pltpu.CompilerParams(vmem_limit_bytes=VMEM_LIMIT, dimension_semantics=("arbitrary",)),
    )(*args)


def slot_array(slots, width, dtype):
    return (per_slot(SLOT, width), (slots, SLOT, width), dtype)


def grad_group(rows):
    return [(whole_block(SHARDS // 2, rows, D), (SHARDS // 2, rows, D), BF)] * 2


NORM_GRADS = (whole_block(8, D), (8, D), F32)
IN_HBM = [pl.BlockSpec(memory_space=pl.ANY)] * 4


def weight_scratch(rows):
    return [pltpu.VMEM((SHARDS // 2, 2, rows, D), BF), pltpu.SemaphoreType.DMA((4,))]


def bound(kernel, weights, **options):
    return functools.partial(kernel, places=weights.places, half=weights.half, **options)


def project(me, rows, weights, norms, name):
    slots = rows.shape[0]
    return call(
        bound(project_kernel, weights),
        name,
        slots,
        [scalars(), per_slot(SLOT, D)] + IN_HBM + [whole_block(*norms.shape)],
        [slot_array(slots, 3 * D, BF)],
        weight_scratch(SELF_OUT - SELF_IN),
        me,
        rows,
        *weights.arrays,
        norms,
        flops=slots * 2 * SLOT * D * D * 3,
    )[0]


def self_attend(kinds, lengths, me, rows, qkv, weights, causal, name):
    slots = rows.shape[0]
    return call(
        bound(self_attend_kernel, weights, causal=causal),
        name,
        slots,
        [scalars(), scalars(), scalars(), per_slot(SLOT, D), per_slot(SLOT, 3 * D)] + IN_HBM,
        [slot_array(slots, D, F32), slot_array(slots, D, BF), slot_array(slots, D, BF), slot_array(slots, 128, BF)],
        weight_scratch(SELF_ROWS - SELF_OUT),
        kinds,
        lengths,
        me,
        rows,
        qkv,
        *weights.arrays,
        flops=slots * 2 * SLOT * D * D * 12,
    )


def cross_forward(kinds, lengths, me, rows, memory, weights, norms):
    slots = rows.shape[0]
    return call(
        bound(cross_forward_kernel, weights),
        "cross_forward",
        slots,
        [scalars(), scalars(), scalars(), per_slot(SLOT, D), per_slot(SLOT, D)]
        + IN_HBM
        + [whole_block(*norms.shape)],
        [
            slot_array(slots, D, F32),
            slot_array(slots, D, BF),
            slot_array(slots, 2 * D, BF),
            slot_array(slots, D, BF),
            slot_array(slots, D, BF),
            slot_array(slots, 128, BF),
        ],
        weight_scratch(CROSS_ROWS),
        kinds,
        lengths,
        me,
        rows,
        memory,
        *weights.arrays,
        norms,
        flops=slots * 2 * SLOT * D * D * 16,
    )


def ffn_forward(me, rows, weights, norms):
    slots = rows.shape[0]
    return call(
        bound(ffn_forward_kernel, weights),
        "ffn_forward",
        slots,
        [scalars(), per_slot(SLOT, D)] + IN_HBM + [whole_block(*norms.shape)],
        [slot_array(slots, D, BF), slot_array(slots, FF, BF), slot_array(slots, FF, BF)],
        weight_scratch(FFN_ROWS),
        me,
        rows,
        *weights.arrays,
        norms,
        flops=slots * 2 * SLOT * D * FF * 4,
    )


def ffn_both(me, rows, cotangent, weights, norms):
    slots = rows.shape[0]
    return call(
        bound(ffn_both_kernel, weights),
        "ffn_both",
        slots,
        [scalars(), per_slot(SLOT, D), per_slot(SLOT, D)] + IN_HBM + [whole_block(*norms.shape)],
        [slot_array(slots, D, BF), slot_array(slots, D, F32)] + grad_group(FFN_ROWS) + [NORM_GRADS],
        weight_scratch(FFN_ROWS)
        + [
            pltpu.VMEM((BLOCKS, SLOT, D), BF),
            pltpu.VMEM((BLOCKS, SLOT, D), F32),
            pltpu.VMEM((2, BLOCKS, D, D), F32),
        ],
        me,
        rows,
        cotangent,
        *weights.arrays,
        norms,
        flops=slots * 2 * SLOT * D * FF * 8,
    )


def ffn_backward(me, grad_out, rows, active, slope, weights, norms):
    slots = rows.shape[0]
    return call(
        bound(ffn_backward_kernel, weights),
        "ffn_backward",
        slots,
        [scalars(), per_slot(SLOT, D), per_slot(SLOT, D), per_slot(SLOT, FF), per_slot(SLOT, FF)]
        + IN_HBM
        + [whole_block(*norms.shape)],
        [slot_array(slots, D, F32)] + grad_group(FFN_ROWS) + [NORM_GRADS],
        weight_scratch(FFN_ROWS) + [pltpu.VMEM((2, BLOCKS, D, D), F32)],
        me,
        grad_out,
        rows,
        active,
        slope,
        *weights.arrays,
        norms,
        flops=slots * 2 * SLOT * D * FF * 6,
    )


def attend_backward(kinds, lengths, me, grad_out, q, kv, kept, weights, causal, start, key_at, name):
    slots = grad_out.shape[0]
    return call(
        bound(attend_back_kernel, weights, causal=causal, start=start, key_at=key_at),
        name,
        slots,
        [scalars(), scalars(), scalars(), per_slot(SLOT, D)]
        + [per_slot(SLOT, part.shape[-1]) for part in (q, kv)]
        + [per_slot(SLOT, D), per_slot(SLOT, D), per_slot(SLOT, 128)]
        + IN_HBM,
        [slot_array(slots, 3 * D, BF)],
        weight_scratch(16) + [pltpu.VMEM((1, SLOT, D), BF)],
        kinds,
        lengths,
        me,
        grad_out,
        q,
        kv,
        *kept,
        *weights.arrays,
        flops=slots * 2 * SLOT * D * D * 20,
    )[0]


def cross_weights(me, grad_out, rows, memory, context, proj, cotangent, weights, norms):
    slots = rows.shape[0]
    return call(
        bound(cross_weight_kernel, weights),
        "cross_weights",
        slots,
        [scalars()]
        + [per_slot(SLOT, D)] * 4
        + [per_slot(SLOT, 3 * D), per_slot(SLOT, D)]
        + IN_HBM
        + [whole_block(*norms.shape)],
        [slot_array(slots, D, F32), slot_array(slots, D, F32)] + grad_group(CROSS_ROWS) + [NORM_GRADS],
        weight_scratch(CROSS_OUT) + [pltpu.VMEM((4, D, D), F32)],
        me,
        grad_out,
        rows,
        memory,
        context,
        proj,
        cotangent,
        *weights.arrays,
        norms,
        flops=slots * 2 * SLOT * D * D * 8,
    )


def self_weights(me, grad_out, rows, context, proj, norms, name):
    slots = rows.shape[0]
    return call(
        self_weight_kernel,
        name,
        slots,
        [scalars()] + [per_slot(SLOT, D)] * 3 + [per_slot(SLOT, 3 * D), whole_block(*norms.shape)],
        grad_group(SELF_ROWS),
        [pltpu.VMEM((4, D, D), F32)],
        me,
        grad_out,
        rows,
        context,
        proj,
        norms,
        flops=slots * 2 * SLOT * D * D * 5,
    )


def self_rows(me, grad_out, rows, proj, weights, norms, name):
    slots = rows.shape[0]
    return call(
        bound(self_rows_kernel, weights),
        name,
        slots,
        [scalars(), per_slot(SLOT, D), per_slot(SLOT, D), per_slot(SLOT, 3 * D)] + IN_HBM + [whole_block(*norms.shape)],
        [slot_array(slots, D, BF), NORM_GRADS],
        weight_scratch(SELF_OUT - SELF_IN),
        me,
        grad_out,
        rows,
        proj,
        *weights.arrays,
        norms,
        flops=slots * 2 * SLOT * D * D * 5,
    )


def axis_sizes(mesh):
    dp, fsdp = mesh.shape["dp"], mesh.shape["fsdp"]
    core = 2 if fsdp % 2 == 0 else 1
    side = math.isqrt(dp)
    first, second = (side, side) if side * side == dp else (dp, 1)
    return (first, second, fsdp // core, core)


AXES = ("dp", "fsdp")
CUBE = (2, 2, 4, 2)
A_BIT, B_BIT, HIGH_BIT, LOW_BIT, CORE_BIT = 16, 8, 4, 2, 1


def swapped(values, bit):
    return lax.ppermute(values, AXES, [(device, device ^ bit) for device in range(SHARDS)])


def moved(values, sizes, axis, shift):
    stride = math.prod(sizes[axis + 1 :])
    pairs = []
    for device in range(math.prod(sizes)):
        place = device // stride % sizes[axis]
        pairs.append((device, device + ((place + shift) % sizes[axis] - place) * stride))
    return lax.ppermute(values, AXES, pairs)


def sum_everywhere(values, sizes):
    if sizes == CUBE:
        for bit in (CORE_BIT, B_BIT, A_BIT, LOW_BIT, HIGH_BIT):
            values = values + swapped(values, bit)
        return values
    for axis in (3, 1, 0, 2):
        total = values
        for shift in range(1, sizes[axis]):
            total = total + moved(values, sizes, axis, shift)
        values = total
    return values


def packed(flat, rows, columns, devices):
    part = flat.reshape(rows // devices, columns // D, D)
    return jnp.swapaxes(part, 0, 1).reshape(-1, D)


def unpacked(part, rows, columns, devices):
    return jnp.swapaxes(part.reshape(columns // D, rows // devices, D), 0, 1).reshape(-1)


SELF_SHAPES = ((D, 3 * D), (D, D))
FFN_SHAPES = ((D, FF), (FF, D))
CROSS_SHAPES = ((D, D), (D, 2 * D), (D, D))


def rows_of(shapes, devices=SHARDS):
    return sum(rows * columns for rows, columns in shapes) // D // devices


def joined(own, other, place, axis):
    return jnp.where(place == 0, jnp.stack([own, other], axis), jnp.stack([other, own], axis))


def gather_cube(groups, extra, me):
    parts = [jnp.concatenate([packed(flat, *shape, SHARDS) for flat, shape in group], 0) for group in groups]
    halves_of = [part.shape[0] // 2 for part in parts]
    one = [part[:half] for part, half in zip(parts, halves_of)]
    two = [part[half:] for part, half in zip(parts, halves_of)] + ([] if extra is None else [extra])
    count = sum(halves_of)
    values = jnp.concatenate(one + two, 0)
    values = joined(values, swapped(values, LOW_BIT), me[3], 0)
    other = swapped(values, HIGH_BIT)
    one = joined(values[:, :count], other[:, :count], me[2], 0)
    two = joined(values[:, count:], other[:, count:], me[2], 0)
    one_other, two_other = swapped(one, B_BIT), swapped(two, A_BIT)
    one, two = joined(one, one_other, me[1], 0), joined(two, two_other, me[0], 0)
    one_other, two_other = swapped(one, A_BIT), swapped(two, B_BIT)
    one, two = joined(one, one_other, me[0], 0), joined(two, two_other, me[1], 1)
    one_other, two_other = swapped(one, CORE_BIT), swapped(two, CORE_BIT)
    own = [half.reshape(SHARDS // 2, -1, D) for half in (one, two)]
    other = [half.reshape(SHARDS // 2, -1, D) for half in (one_other, two_other)]
    results, place = [], 0
    for half in halves_of:
        results.append(Weights(own, other, (place, place), half))
        place += half
    if extra is None:
        return results, None
    lines = joined(own[1][:, place], other[1][:, place], me[4], 1)
    return results, lines.reshape(SHARDS, D)


def gather_plain(groups, extra, devices):
    results = []
    for group in groups:
        parts = []
        for flat, shape in group:
            full = lax.all_gather(flat, AXES, axis=0, tiled=True).reshape(SHARDS, shape[0] // SHARDS, shape[1] // D, D)
            parts.append(jnp.swapaxes(full, 1, 2).reshape(SHARDS, -1, D))
        whole = jnp.concatenate(parts, 1)
        half = whole.shape[1] // 2
        own = [whole[0::2, :half], whole[0::2, half:]]
        other = [whole[1::2, :half], whole[1::2, half:]]
        results.append(Weights(own, other, (0, 0), half))
    return results, None if extra is None else lax.all_gather(extra[0], AXES, axis=0)


def both_halves(refs, rows):
    return slice(0, rows // 2), slice(rows // 2, rows)


def first_sum_kernel(me_ref, *refs):
    members = (len(refs) - 4) // 2
    send_one, keep_one, send_two, keep_two = refs[-4:]
    a, b = me_ref[0], me_ref[1]
    place = 0
    for member in range(members):
        keep, got = refs[member], refs[members + member]
        half = keep.shape[3] // 2
        low, high, here = slice(0, half), slice(half, 2 * half), slice(place, place + half)
        for other in range(2):
            for ref, pick in ((send_one, 1 - b), (keep_one, b)):
                ref[other, 0, here] = keep[other, pick, 0, low] + got[other, pick, 0, low]
            for ref, pick in ((send_two, 1 - a), (keep_two, a)):
                ref[other, 0, here] = keep[pick, other, 0, high] + got[pick, other, 0, high]
        place += half


def second_sum_kernel(me_ref, keep_one, got_one, keep_two, got_two, send_a, kept_a, send_b, kept_b):
    a, b = me_ref[0], me_ref[1]
    for ref, pick in ((send_a, 1 - a), (kept_a, a)):
        ref[0] = keep_one[pick, 0] + got_one[pick, 0]
    for ref, pick in ((send_b, 1 - b), (kept_b, b)):
        ref[0] = keep_two[pick, 0] + got_two[pick, 0]


def third_sum_kernel(me_ref, keep_one, got_one, keep_two, got_two, send, keep):
    z = me_ref[2]
    half = keep_one.shape[2]
    for ref, pick in ((send, 1 - z), (keep, z)):
        ref[0, :half] = keep_one[pick, 0] + got_one[pick, 0]
        ref[0, half:] = keep_two[pick, 0] + got_two[pick, 0]


def fourth_sum_kernel(me_ref, keep, got, send, kept):
    z = me_ref[3]
    for ref, pick in ((send, 1 - z), (kept, z)):
        ref[...] = keep[pick] + got[pick]


def sum_call(kernel, name, steps, me, args, ins, outs):
    return pl.pallas_call(
        kernel,
        name=name,
        grid=(steps,),
        in_specs=[scalars()] + ins,
        out_specs=[spec for spec, _ in outs],
        out_shape=[jax.ShapeDtypeStruct(shape, BF) for _, shape in outs],
        cost_estimate=pl.CostEstimate(flops=0, bytes_accessed=2 * sum(arg.size for arg in args) * 3 // 2, transcendentals=0),
        compiler_params=pltpu.CompilerParams(vmem_limit_bytes=VMEM_LIMIT, dimension_semantics=("arbitrary",)),
    )(me, *args)


def scatter_cube(groups, me, name):
    got = [swapped(send, CORE_BIT) for _, send, _ in groups]
    views = [part.reshape(2, 2, 4, -1, D) for part in [keep for keep, _, _ in groups] + got]
    half = sum(rows_of(shapes) for _, _, shapes in groups) // 2
    quad = (pl.BlockSpec((2, 1, half, D), lambda z: (0, z, 0, 0)), (2, 4, half, D))
    send_one, keep_one, send_two, keep_two = sum_call(
        first_sum_kernel,
        name + "_sum_1",
        4,
        me,
        views,
        [pl.BlockSpec((2, 2, 1, view.shape[3], D), lambda z: (0, 0, z, 0, 0)) for view in views],
        [quad] * 4,
    )
    got_one, got_two = swapped(send_one, B_BIT), swapped(send_two, A_BIT)
    line = (pl.BlockSpec((1, half, D), lambda z: (z, 0, 0)), (4, half, D))
    send_one, keep_one, send_two, keep_two = sum_call(
        second_sum_kernel,
        name + "_sum_2",
        4,
        me,
        [keep_one, got_one, keep_two, got_two],
        [quad[0]] * 4,
        [line] * 4,
    )
    got_one, got_two = swapped(send_one, A_BIT), swapped(send_two, B_BIT)
    views = [part.reshape(2, 2, half, D) for part in (keep_one, got_one, keep_two, got_two)]
    send, keep = sum_call(
        third_sum_kernel,
        name + "_sum_3",
        2,
        me,
        views,
        [pl.BlockSpec((2, 1, half, D), lambda z: (0, z, 0, 0))] * 4,
        [(pl.BlockSpec((1, 2 * half, D), lambda z: (z, 0, 0)), (2, 2 * half, D))] * 2,
    )
    got = swapped(send, HIGH_BIT)
    send, keep = sum_call(
        fourth_sum_kernel,
        name + "_sum_4",
        1,
        me,
        [keep, got],
        [whole_block(2, 2 * half, D)] * 2,
        [(whole_block(2 * half, D), (2 * half, D))] * 2,
    )
    own = keep.astype(F32) + swapped(send, LOW_BIT).astype(F32)
    results, place = [], 0
    for _, _, shapes in groups:
        part = rows_of(shapes) // 2
        rows = jnp.concatenate([own[place : place + part], own[half + place : half + place + part]], 0)
        place += part
        first = 0
        for shape in shapes:
            count = rows_of((shape,))
            results.append(unpacked(rows[first : first + count], *shape, SHARDS))
            first += count
    return results


def scatter_plain(groups, devices):
    results = []
    for keep, send, shapes in groups:
        grads = jnp.stack([keep, send], 1).reshape(SHARDS, -1, D)
        first = 0
        for rows, columns in shapes:
            count = rows_of(((rows, columns),))
            part = grads[:, first : first + count].reshape(SHARDS, columns // D, rows // SHARDS, D)
            flat = jnp.swapaxes(part, 1, 2).reshape(devices, -1)
            results.append(lax.psum_scatter(flat, AXES, scatter_dimension=0, tiled=True).reshape(-1).astype(F32))
            first += count
    return results


def count_live(kinds, lengths, ids):
    positions = jnp.arange(SLOT, dtype=jnp.int32)[None, :]
    size = jnp.left_shift(jnp.int32(SLOT // 4), kinds)[:, None]
    sequence = positions // size
    limit = jnp.zeros_like(sequence)
    for entry in range(4):
        limit = jnp.where(sequence == entry, lengths[:, entry : entry + 1], limit)
    live = positions % size < limit
    hits = (ids.reshape(-1)[:, None] == jnp.arange(VOCAB, dtype=jnp.int32)[None, :]) & live.reshape(-1)[:, None]
    return jnp.sum(hits.astype(F32), 0)


def local(
    sizes,
    enc_in,
    dec_in,
    bucket,
    enc_lengths,
    dec_lengths,
    pred_ids,
    running_counts,
    enc_attn_in,
    enc_attn_out,
    enc_ff_in,
    enc_ff_out,
    enc_norms,
    dec_self_in,
    dec_self_out,
    dec_cross_q,
    dec_cross_kv,
    dec_cross_out,
    dec_ff_in,
    dec_ff_out,
    dec_norms,
    enc_cotangent,
    dec_cotangent,
):
    devices = math.prod(sizes)
    cube = sizes == CUBE
    index = lax.axis_index("dp") * lax.axis_size("fsdp") + lax.axis_index("fsdp")
    if cube:
        me = jnp.stack([index >> 4 & 1, index >> 3 & 1, index >> 2 & 1, index >> 1 & 1, index & 1]).astype(jnp.int32)
    else:
        me = jnp.zeros((5,), jnp.int32)

    def gather(groups, extra=None):
        return gather_cube(groups, extra, me) if cube else gather_plain(groups, extra, devices)

    def scatter(name, *groups):
        return scatter_cube(groups, me, name) if cube else scatter_plain(groups, devices)

    enc_count, dec_count = enc_norms.shape[0], dec_norms.shape[0]
    both = jnp.concatenate([enc_norms, dec_norms])
    norm_part = jnp.pad(both[None, :], ((0, 7), (0, D - both.shape[0])))
    enc_self_group = list(zip((enc_attn_in, enc_attn_out), SELF_SHAPES))
    dec_self_group = list(zip((dec_self_in, dec_self_out), SELF_SHAPES))
    enc_ff_group = list(zip((enc_ff_in, enc_ff_out), FFN_SHAPES))
    cross_group = list(zip((dec_cross_q, dec_cross_kv, dec_cross_out), CROSS_SHAPES))
    dec_ff_group = list(zip((dec_ff_in, dec_ff_out), FFN_SHAPES))
    (enc_self_w, dec_self_w), norm_lines = gather([enc_self_group, dec_self_group], norm_part)
    (enc_ff_w,), _ = gather([enc_ff_group])
    (cross_w, dec_ff_w), _ = gather([cross_group, dec_ff_group])
    enc_norm = norm_lines[:, :enc_count].reshape(4, D).astype(F32)
    dec_norm = norm_lines[:, enc_count : enc_count + dec_count].reshape(6, D).astype(F32)

    enc_qkv = project(me, enc_in, enc_self_w, enc_norm, "enc_project")
    dec_qkv = project(me, dec_in, dec_self_w, dec_norm, "dec_project")
    attended, *enc_kept = self_attend(bucket, enc_lengths, me, enc_in, enc_qkv, enc_self_w, False, "enc_attend")
    first_out, *dec_kept = self_attend(bucket, dec_lengths, me, dec_in, dec_qkv, dec_self_w, True, "dec_attend")
    memory, active, slope = ffn_forward(me, attended, enc_ff_w, enc_norm)
    second_out, cross_q, cross_kv, *cross_kept = cross_forward(
        bucket, enc_lengths, me, first_out, memory, cross_w, dec_norm
    )
    decoded, grad_second, dec_ff_keep, dec_ff_send, ffn_norm_g = ffn_both(
        me, second_out, dec_cotangent, dec_ff_w, dec_norm
    )
    cross_proj = attend_backward(
        bucket,
        enc_lengths,
        me,
        grad_second,
        cross_q,
        cross_kv,
        cross_kept,
        cross_w,
        False,
        CROSS_OUT,
        0,
        "cross_attend_back",
    )
    grad_first, grad_memory, cross_keep, cross_send, cross_norm_g = cross_weights(
        me, grad_second, first_out, memory, cross_kept[0], cross_proj, enc_cotangent, cross_w, dec_norm
    )
    (dec_ff_in_g, dec_ff_out_g, cross_q_g, cross_kv_g, cross_out_g) = scatter(
        "dec", (dec_ff_keep, dec_ff_send, FFN_SHAPES), (cross_keep, cross_send, CROSS_SHAPES)
    )
    grad_attended, enc_ff_keep, enc_ff_send, enc_ffn_norm_g = ffn_backward(
        me, grad_memory, attended, active, slope, enc_ff_w, enc_norm
    )
    dec_proj = attend_backward(
        bucket, dec_lengths, me, grad_first, dec_qkv, dec_qkv, dec_kept, dec_self_w, True, SELF_OUT, D, "dec_attend_back"
    )
    dec_self_keep, dec_self_send = self_weights(
        me, grad_first, dec_in, dec_kept[0], dec_proj, dec_norm, "dec_self_weights"
    )
    (enc_ff_in_g, enc_ff_out_g, dec_self_in_g, dec_self_out_g) = scatter(
        "mid", (enc_ff_keep, enc_ff_send, FFN_SHAPES), (dec_self_keep, dec_self_send, SELF_SHAPES)
    )
    enc_proj = attend_backward(
        bucket,
        enc_lengths,
        me,
        grad_attended,
        enc_qkv,
        enc_qkv,
        enc_kept,
        enc_self_w,
        False,
        SELF_OUT,
        D,
        "enc_attend_back",
    )
    enc_self_keep, enc_self_send = self_weights(
        me, grad_attended, enc_in, enc_kept[0], enc_proj, enc_norm, "enc_self_weights"
    )
    (enc_attn_in_g, enc_attn_out_g) = scatter("enc", (enc_self_keep, enc_self_send, SELF_SHAPES))
    grad_enc_in, enc_self_norm_g = self_rows(me, grad_attended, enc_in, enc_proj, enc_self_w, enc_norm, "enc_self_rows")
    grad_dec_in, dec_self_norm_g = self_rows(me, grad_first, dec_in, dec_proj, dec_self_w, dec_norm, "dec_self_rows")

    counted = jnp.pad(count_live(bucket, dec_lengths, pred_ids), (0, 2 * D - VOCAB)).reshape(2, D)
    small = jnp.concatenate(
        [part[:2] for part in (enc_self_norm_g, enc_ffn_norm_g, dec_self_norm_g, cross_norm_g, ffn_norm_g, counted)]
        + [jnp.zeros((4, D), F32)],
        0,
    )
    small = sum_everywhere(small, sizes)
    enc_norm_own = lax.dynamic_slice(small[:4].reshape(-1), (index * enc_count,), (enc_count,))
    dec_norm_own = lax.dynamic_slice(small[4:10].reshape(-1), (index * dec_count,), (dec_count,))
    counts = running_counts + small[10:12].reshape(-1)[:VOCAB].astype(jnp.int32)
    return (
        memory,
        decoded,
        grad_enc_in,
        grad_dec_in,
        enc_attn_in_g,
        enc_attn_out_g,
        enc_ff_in_g,
        enc_ff_out_g,
        enc_norm_own,
        dec_self_in_g,
        dec_self_out_g,
        cross_q_g,
        cross_kv_g,
        cross_out_g,
        dec_ff_in_g,
        dec_ff_out_g,
        dec_norm_own,
        counts,
    )


def solution(mesh):
    rows = P(AXES, None, None)
    pair = P(AXES, None)
    flat = P(AXES)
    return jax.shard_map(
        functools.partial(local, axis_sizes(mesh)),
        mesh=mesh,
        in_specs=(rows, rows, flat, pair, pair, pair, P()) + (flat,) * 13 + (rows, rows),
        out_specs=(rows,) * 4 + (flat,) * 13 + (P(),),
        check_vma=False,
    )
```

time: 1190 us -> 511 us (0.43)
  blocking collectives: 288 us -> 0 us
  matrix products: 276 us -> 0 us
  Pallas kernels: 0 us -> 273 us
  waiting for transfers between devices: 355 us -> 130 us
  local copies, waits for them, and re-layouts: 181 us -> 37.6 us
  starting transfers between devices: 0.3 us -> 51.9 us
  other arithmetic: 57.1 us -> 9.79 us
  between operations: 15.9 us -> 2.09 us
    unnamed x9 -> x0, waiting for transfers between devices: 354 us -> none
    dot_general x75 -> x0, matrix products: 276 us -> none  [the longest x11 75.7 us: forward_product(): return jnp.dot(left, right, preferred_element_type=jnp.float32)]
    pallas_call x0 -> x28, Pallas kernels: none -> 273 us  [the longest x16 236 us: call(): pl.pallas_call(kernel, name=name, grid=(slots,), in_specs=ins, out_specs=...]
    all_gather x4 -> x0, blocking collectives: 163 us -> none  [the longest x1 43.7 us: local(): lax.all_gather(enc_attn_out, ('dp', 'fsdp'), axis=0, tiled=True)]
    ppermute x0 -> x52, waiting for transfers between devices: none -> 130 us  [swapped(): lax.ppermute(values, AXES, [(device, device ^ bit) for device in range(SH...]
    unnamed x2 -> x0, blocking collectives: 83.2 us -> none
    ppermute x0 -> x52, starting transfers between devices: none -> 51.9 us  [swapped(): lax.ppermute(values, AXES, [(device, device ^ bit) for device in range(SH...]
    psum x1 -> x0, blocking collectives: 42.4 us -> none  [local(): summed_counts = lax.psum(local_counts, ('dp', 'fsdp'))]
  transfers between devices with their start and end apart: 8 -> 52, of which waited for: 2 -> 16; matrix products, arithmetic and copies ran while one was open for 19% -> 6% of each run, Pallas kernels for 0% -> 38%
where the time goes in v1:
time: 511 us; the launch traced here: 504 us
  Pallas kernels  273 us (53%)
  waiting for transfers between devices  130 us (25%)
  starting transfers between devices  51.9 us (10%)
  local copies, waits for them, and re-layouts  37.6 us (7%)
  other arithmetic  9.79 us (2%)
    pallas_call x16, Pallas kernels, call(): pl.pallas_call(kernel, name=name, grid=(slots,), in_specs=ins, out_specs=...  236 us
    ppermute x52, waiting for transfers between devices, swapped(): lax.ppermute(values, AXES, [(device, device ^ bit) for device in range(SH...  130 us
    ppermute x52, starting transfers between devices, swapped(): lax.ppermute(values, AXES, [(device, device ^ bit) for device in range(SH...  51.9 us
    pallas_call x12, Pallas kernels, sum_call(): pl.pallas_call(kernel, name=name, grid=(steps,), in_specs=[scalars()] + i...  36.7 us
    unnamed x100, local copies, waits for them, and re-layouts  15.2 us
  transfers between devices with their start and end apart: 52, of which 16 were waited for; matrix products, arithmetic and copies ran while one was open for 6% of the time, Pallas kernels for 38%

profile of v1, /device:TPU:0, one launch (start us, length us, event | category | flops | bytes accessed | tf_op | source)
XLA Modules:
  0.0 503.7 jit_solution(5930022776821293576)
XLA Ops:
  19.5 3.8 collective-permute-done.16
  23.5 22.4 %collective-permute-done.9 = bf16[2,128,512]{2,1,0:T(8,128)(2,1)S(1)} collective-permute-done((bf16[2,128,512]{2,1,0:T(8,128)(2,1)S(1)}, bf16[2,128,512]{2,1,0:T(8,128)(2,1)S(1)}, u32[]{:S(2)}, u32[]{:S(2)}) %collective-permute-start.9) | collective-permute-done | bytes 262176 | tf_op jit(solution)/shard_map/ppermute | solution.py:962
  65.0 4.3 collective-permute-done.21
  71.0 21.4 %collective-permute-done.6 = bf16[2,2,2,72,512]{4,3,2,1,0:T(8,128)(2,1)S(1)} collective-permute-done((bf16[2,2,2,72,512]{4,3,2,1,0:T(8,128)(2,1)S(1)}, bf16[2,2,2,72,512]{4,3,2,1,0:T(8,128)(2,1)S(1)}, u32[]{:S(2)}, u32[]{:S(2)}) %collective-permute-start.6) | collective-permute-done | bytes 589856 | tf_op jit(solution)/shard_map/ppermute | solution.py:962
  99.2 10.1 %collective-permute-done.22 = bf16[2,2,2,96,512]{4,3,2,1,0:T(8,128)(2,1)S(1)} collective-permute-done((bf16[2,2,2,96,512]{4,3,2,1,0:T(8,128)(2,1)S(1)}, bf16[2,2,2,96,512]{4,3,2,1,0:T(8,128)(2,1)S(1)}, u32[]{:S(2)}, u32[]{:S(2)}) %collective-permute-start.22) | collective-permute-done | bytes 786464 | tf_op jit(solution)/shard_map/ppermute | solution.py:962
  119.7 6.4 %dec_project.1.qkv_ref.q_ref.kv_ref = bf16[2,512,1536]{2,1,0:T(8,128)(2,1)} custom-call(s32[5]{0:T(128)} %stack.395.me_ref, bf16[2,512,512]{2,1,0:T(8,128)(2,1)} %x_ref.15, bf16[16,64,512]{2,1,0:T(8,128)(2,1)} %bitcast.228, bf16[16,64,512]{2,1,0:T(8,128)(2,1)} %bitcast.236, bf16[16,72,512]{2,1,0:T(8,128)(2,1)} %bitcast.211, bf16[16,72,512]{2,1,0:T(8,128)(2,1)} %bitcast.220, ...), custom_call_target="tpu_custom_call" | custom-call | flops 1610612736 | bytes 8388608 | tf_op jit(solution)/shard_map/dec_project/pallas_call | solution.py:700
  126.0 13.2 %dec_attend.1 = (f32[2,512,512]{2,1,0:T(8,128)}, bf16[2,512,512]{2,1,0:T(8,128)(2,1)}, bf16[2,512,512]{2,1,0:T(8,128)(2,1)}, bf16[2,512,128]{2,1,0:T(8,128)(2,1)}) custom-call(s32[2]{0:T(128)} %kind_ref.11, s32[2,4]{1,0:T(2,128)} %lengths_ref.11, s32[5]{0:T(128)} %stack.395.me_ref, bf16[2,512,512]{2,1,0:T(8,128)(2,1)} %x_ref.15, ...), custom_call_target="tpu_custom_call" | custom-call | flops 6442450944 | bytes 8388608 | tf_op jit(solution)/shard_map/dec_attend/pallas_call | solution.py:700
  140.0 6.0 %enc_project.1.qkv_ref.q_ref.kv_ref = bf16[2,512,1536]{2,1,0:T(8,128)(2,1)} custom-call(s32[5]{0:T(128)} %stack.395.me_ref, bf16[2,512,512]{2,1,0:T(8,128)(2,1)} %x_ref.14, bf16[16,64,512]{2,1,0:T(8,128)(2,1)} %bitcast.230, bf16[16,64,512]{2,1,0:T(8,128)(2,1)} %bitcast.238, bf16[16,72,512]{2,1,0:T(8,128)(2,1)} %bitcast.213, bf16[16,72,512]{2,1,0:T(8,128)(2,1)} %bitcast.222, ...), custom_call_target="tpu_custom_call" | custom-call | flops 1610612736 | bytes 8388608 | tf_op jit(solution)/shard_map/enc_project/pallas_call | solution.py:700
  146.0 13.2 %enc_attend.1 = (f32[2,512,512]{2,1,0:T(8,128)}, bf16[2,512,512]{2,1,0:T(8,128)(2,1)}, bf16[2,512,512]{2,1,0:T(8,128)(2,1)}, bf16[2,512,128]{2,1,0:T(8,128)(2,1)}) custom-call(s32[2]{0:T(128)} %kind_ref.11, s32[2,4]{1,0:T(2,128)} %lengths_ref.10, s32[5]{0:T(128)} %stack.395.me_ref, bf16[2,512,512]{2,1,0:T(8,128)(2,1)} %x_ref.14, ...), custom_call_target="tpu_custom_call" | custom-call | flops 6442450944 | bytes 8388608 | tf_op jit(solution)/shard_map/enc_attend/pallas_call | solution.py:700
  159.2 16.3 %ffn_forward.1 = (bf16[2,512,512]{2,1,0:T(8,128)(2,1)}, bf16[2,512,2048]{2,1,0:T(8,128)(2,1)}, bf16[2,512,2048]{2,1,0:T(8,128)(2,1)}) custom-call(s32[5]{0:T(128)} %stack.395.me_ref, f32[2,512,512]{2,1,0:T(8,128)} %get-tuple-element.93.r_ref, bf16[16,64,512]{2,1,0:T(8,128)(2,1)} %bitcast.45.w0, bf16[16,64,512]{2,1,0:T(8,128)(2,1)} %bitcast.46.w1, ...), custom_call_target="tpu_custom_call" | custom-call | flops 8589934592 | bytes 8388608 | tf_op jit(solution)/shard_map/ffn_forward/pallas_call | solution.py:700
  178.2 16.1 %cross_forward.1 = (f32[2,512,512]{2,1,0:T(8,128)}, bf16[2,512,512]{2,1,0:T(8,128)(2,1)}, bf16[2,512,1024]{2,1,0:T(8,128)(2,1)}, bf16[2,512,512]{2,1,0:T(8,128)(...) custom-call(s32[2]{0:T(128)} %kind_ref.11, s32[2,4]{1,0:T(2,128)} %lengths_ref.10, s32[5]{0:T(128)} %stack.395.me_ref, ...), custom_call_target="tpu_custom_call" | custom-call | flops 8589934592 | bytes 8388608 | tf_op jit(solution)/shard_map/cross_forward/pallas_call | solution.py:700
  194.4 31.1 %ffn_both.1 = (bf16[2,512,512]{2,1,0:T(8,128)(2,1)}, f32[2,512,512]{2,1,0:T(8,128)}, bf16[16,128,512]{2,1,0:T(8,128)(2,1)}, bf16[16,128,512]{2,1,0:T(8,128)(2,1)}, f32[8,512]{1,0:T(8,128)}) custom-call(s32[5]{0:T(128)} %stack.395.me_ref, f32[2,512,512]{2,1,0:T(8,128)} %get-tuple-element.96.r_ref, bf16[2,512,512]{2,1,0:T(8,128)(2,1)} %cotangent_ref.2, ...), custom_call_target="tpu_custom_call" | custom-call | flops 17179869184 | bytes 8388608 | tf_op jit(solution)/shard_map/ffn_both/pallas_call | solution.py:700
  225.5 20.3 %cross_attend_back.1.proj_ref = bf16[2,512,1536]{2,1,0:T(8,128)(2,1)} custom-call(s32[2]{0:T(128)} %kind_ref.11, s32[2,4]{1,0:T(2,128)} %lengths_ref.10, s32[5]{0:T(128)} %stack.395.me_ref, f32[2,512,512]{2,1,0:T(8,128)} %get-tuple-element.98.grad_out_ref, bf16[2,512,512]{2,1,0:T(8,128)(2,1)} %get-tuple-element.100.q_ref, ...), custom_call_target="tpu_custom_call" | custom-call | flops 10737418240 | bytes 8388608 | tf_op jit(solution)/shard_map/cross_attend_back/pallas_call | solution.py:700
  245.8 13.3 %cross_weights.1 = (f32[2,512,512]{2,1,0:T(8,128)}, f32[2,512,512]{2,1,0:T(8,128)}, bf16[16,64,512]{2,1,0:T(8,128)(2,1)}, bf16[16,64,512]{2,1,0:T(8,128)(2,1)}, f32[8,512]{1,0:T(8,128)}) custom-call(s32[5]{0:T(128)} %stack.395.me_ref, f32[2,512,512]{2,1,0:T(8,128)} %get-tuple-element.98.grad_out_ref, f32[2,512,512]{2,1,0:T(8,128)} %get-tuple-element.95.r_ref, ...), custom_call_target="tpu_custom_call" | custom-call | flops 4294967296 | bytes 8388608 | tf_op jit(solution)/shard_map/cross_weights/pallas_call | solution.py:700
  259.6 23.6 %ffn_backward.1 = (f32[2,512,512]{2,1,0:T(8,128)}, bf16[16,128,512]{2,1,0:T(8,128)(2,1)}, bf16[16,128,512]{2,1,0:T(8,128)(2,1)}, f32[8,512]{1,0:T(8,128)}) custom-call(s32[5]{0:T(128)} %stack.395.me_ref, f32[2,512,512]{2,1,0:T(8,128)} %get-tuple-element.104.grad_out_ref, f32[2,512,512]{2,1,0:T(8,128)} %get-tuple-element.93.r_ref, ...), custom_call_target="tpu_custom_call" | custom-call | flops 12884901888 | bytes 8388608 | tf_op jit(solution)/shard_map/ffn_backward/pallas_call | solution.py:700
  283.4 22.4 %dec_attend_back.1.proj_ref = bf16[2,512,1536]{2,1,0:T(8,128)(2,1)} custom-call(s32[2]{0:T(128)} %kind_ref.11, s32[2,4]{1,0:T(2,128)} %lengths_ref.11, s32[5]{0:T(128)} %stack.395.me_ref, f32[2,512,512]{2,1,0:T(8,128)} %get-tuple-element.112.grad_out_ref, bf16[2,512,1536]{2,1,0:T(8,128)(2,1)} %dec_project.1.qkv_ref.q_ref.kv_ref, ...), custom_call_target="tpu_custom_call" | custom-call | flops 10737418240 | bytes 8388608 | tf_op jit(solution)/shard_map/dec_attend_back/pallas_call | solution.py:700
  305.8 21.6 %enc_attend_back.1.proj_ref = bf16[2,512,1536]{2,1,0:T(8,128)(2,1)} custom-call(s32[2]{0:T(128)} %kind_ref.11, s32[2,4]{1,0:T(2,128)} %lengths_ref.10, s32[5]{0:T(128)} %stack.395.me_ref, f32[2,512,512]{2,1,0:T(8,128)} %get-tuple-element.107.grad_out_ref, bf16[2,512,1536]{2,1,0:T(8,128)(2,1)} %enc_project.1.qkv_ref.q_ref.kv_ref, ...), custom_call_target="tpu_custom_call" | custom-call | flops 10737418240 | bytes 8388608 | tf_op jit(solution)/shard_map/enc_attend_back/pallas_call | solution.py:700
  327.4 7.3 %dec_self_rows.1 = (bf16[2,512,512]{2,1,0:T(8,128)(2,1)}, f32[8,512]{1,0:T(8,128)}) custom-call(s32[5]{0:T(128)} %stack.395.me_ref, f32[2,512,512]{2,1,0:T(8,128)} %get-tuple-element.112.grad_out_ref, bf16[2,512,512]{2,1,0:T(8,128)(2,1)} %x_ref.15, bf16[2,512,1536]{2,1,0:T(8,128)(2,1)} %dec_attend_back.1.proj_ref, bf16[16,64,512]{2,1,0:T(8,128)(2,1)} %bitcast.234, ...), custom_call_target="tpu_custom_call" | custom-call | flops 2684354560 | bytes 8388608 | tf_op jit(solution)/shard_map/dec_self_rows/pallas_call | solution.py:700
  335.5 7.4 %enc_self_rows.1 = (bf16[2,512,512]{2,1,0:T(8,128)(2,1)}, f32[8,512]{1,0:T(8,128)}) custom-call(s32[5]{0:T(128)} %stack.395.me_ref, f32[2,512,512]{2,1,0:T(8,128)} %get-tuple-element.107.grad_out_ref, bf16[2,512,512]{2,1,0:T(8,128)(2,1)} %x_ref.14, bf16[2,512,1536]{2,1,0:T(8,128)(2,1)} %enc_attend_back.1.proj_ref, bf16[16,64,512]{2,1,0:T(8,128)(2,1)} %bitcast.235, ...), custom_call_target="tpu_custom_call" | custom-call | flops 2684354560 | bytes 8388608 | tf_op jit(solution)/shard_map/enc_self_rows/pallas_call | solution.py:700
  346.3 8.8 %enc_self_weights.1 = (bf16[16,64,512]{2,1,0:T(8,128)(2,1)}, bf16[16,64,512]{2,1,0:T(8,128)(2,1)}) custom-call(s32[5]{0:T(128)} %stack.395.me_ref, f32[2,512,512]{2,1,0:T(8,128)} %get-tuple-element.107.grad_out_ref, bf16[2,512,512]{2,1,0:T(8,128)(2,1)} %x_ref.14, bf16[2,512,512]{2,1,0:T(8,128)(2,1)} %get-tuple-element.108.context_ref, ...), custom_call_target="tpu_custom_call" | custom-call | flops 2684354560 | bytes 8388608 | tf_op jit(solution)/shard_map/enc_self_weights/pallas_call | solution.py:700
  355.2 8.9 %dec_self_weights.1 = (bf16[16,64,512]{2,1,0:T(8,128)(2,1)}, bf16[16,64,512]{2,1,0:T(8,128)(2,1)}) custom-call(s32[5]{0:T(128)} %stack.395.me_ref, f32[2,512,512]{2,1,0:T(8,128)} %get-tuple-element.112.grad_out_ref, bf16[2,512,512]{2,1,0:T(8,128)(2,1)} %x_ref.15, bf16[2,512,512]{2,1,0:T(8,128)(2,1)} %get-tuple-element.113.context_ref, ...), custom_call_target="tpu_custom_call" | custom-call | flops 2684354560 | bytes 8388608 | tf_op jit(solution)/shard_map/dec_self_weights/pallas_call | solution.py:700
  365.6 4.9 dec_sum_1.1
  373.8 3.6 enc_sum_1.1
  377.4 14.2 %collective-permute-done.41 = f32[16,512]{1,0:T(8,128)S(1)} collective-permute-done((f32[16,512]{1,0:T(8,128)S(1)}, f32[16,512]{1,0:T(8,128)S(1)}, u32[]{:S(2)}, u32[]{:S(2)}) %collective-permute-start.41) | collective-permute-done | bytes 32800 | tf_op jit(solution)/shard_map/ppermute | solution.py:962
  395.4 5.0 mid_sum_1.1
  403.3 21.0 %collective-permute-done.26.got_two = bf16[2,4,32,512]{3,2,1,0:T(8,128)(2,1)S(1)} collective-permute-done((bf16[2,4,32,512]{3,2,1,0:T(8,128)(2,1)S(1)}, bf16[2,4,32,512]{3,2,1,0:T(8,128)(2,1)S(1)}, u32[]{:S(2)}, u32[]{:S(2)}) %collective-permute-start.26) | collective-permute-done | bytes 262176 | tf_op jit(solution)/shard_map/ppermute | solution.py:962
  424.4 3.4 collective-permute-start.43
  427.7 3.3 enc_sum_2.1
  433.2 4.0 dec_sum_2.1
  444.6 4.0 mid_sum_2.1
  465.2 17.1 %collective-permute-done.50.got = bf16[2,192,512]{2,1,0:T(8,128)(2,1)S(1)} collective-permute-done((bf16[2,192,512]{2,1,0:T(8,128)(2,1)}, bf16[2,192,512]{2,1,0:T(8,128)(2,1)S(1)}, u32[]{:S(2)}, u32[]{:S(2)}) %collective-permute-start.50) | collective-permute-done | bytes 393248 | tf_op jit(solution)/shard_map/ppermute | solution.py:962
  493.9 3.1 collective-permute-done.38
  (334 shorter events, 120.2 us)
Async XLA Ops:
  16.3 29.6 %collective-permute-start.9 = (bf16[2,128,512]{2,1,0:T(8,128)(2,1)S(1)}, bf16[2,128,512]{2,1,0:T(8,128)(2,1)S(1)}, u32[]{:S(2)}, u32[]{:S(2)}) collective-permute-start(bf16[2,128,512]{2,1,0:T(8,128)(2,1)S(1)} %maximum_select_fusion.28), channel_id=1, source_target_pairs={{0,4},{1,5},{2,6},{3,7},{4,0},{5,1},{6,2},{7,3},{8,12},{9,13},{10,... | collective-permute-start | bytes 786440 | tf_op jit(solution)/shard_map/ppermute | solution.py:962
  19.1 32.8 %collective-permute-start.1 = (bf16[2,136,512]{2,1,0:T(8,128)(2,1)S(1)}, bf16[2,136,512]{2,1,0:T(8,128)(2,1)S(1)}, u32[]{:S(2)}, u32[]{:S(2)}) collective-permute-start(bf16[2,136,512]{2,1,0:T(8,128)(2,1)S(1)} %maximum_select_fusion.25), channel_id=1, source_target_pairs={{0,4},{1,5},{2,6},{3,7},{4,0},{5,1},{6,2},{7,3},{8,12},{9,13},{10,... | collective-permute-start | bytes 835592 | tf_op jit(solution)/shard_map/ppermute | solution.py:962
  23.4 33.6 %collective-permute-start.17 = (bf16[2,192,512]{2,1,0:T(8,128)(2,1)S(1)}, bf16[2,192,512]{2,1,0:T(8,128)(2,1)S(1)}, u32[]{:S(2)}, u32[]{:S(2)}) collective-permute-start(bf16[2,192,512]{2,1,0:T(8,128)(2,1)S(1)} %maximum_select_fusion.18), channel_id=1, source_target_pairs={{0,4},{1,5},{2,6},{3,7},{4,0},{5,1},{6,2},{7,3},{8,12},{9,13},{10,... | collective-permute-start | bytes 1179656 | tf_op jit(solution)/shard_map/ppermute | solution.py:962
  47.7 14.8 %collective-permute-start.10 = (bf16[2,2,64,512]{3,2,1,0:T(8,128)(2,1)S(1)}, bf16[2,2,64,512]{3,2,1,0:T(8,128)(2,1)S(1)}, u32[]{:S(2)}, u32[]{:S(2)}) collective-permute-start(bf16[2,2,64,512]{3,2,1,0:T(8,128)(2,1)S(1)} %maximum_select_fusion.30), channel_id=1, source_target_pairs={{0,8},{1,9},{2,10},{3,11},{4,12},{5,13},{6,14},{7,15},{8,0},{9,1},... | collective-permute-start | bytes 786440 | tf_op jit(solution)/shard_map/ppermute | solution.py:962
  58.9 35.4 %collective-permute-start.18 = (bf16[2,2,96,512]{3,2,1,0:T(8,128)(2,1)S(1)}, bf16[2,2,96,512]{3,2,1,0:T(8,128)(2,1)S(1)}, u32[]{:S(2)}, u32[]{:S(2)}) collective-permute-start(bf16[2,2,96,512]{3,2,1,0:T(8,128)(2,1)S(1)} %maximum_select_fusion.20), channel_id=1, source_target_pairs={{0,8},{1,9},{2,10},{3,11},{4,12},{5,13},{6,14},{7,15},{8,0},{9,1},... | collective-permute-start | bytes 1179656 | tf_op jit(solution)/shard_map/ppermute | solution.py:962
  60.9 33.1 %collective-permute-start.14 = (bf16[2,2,2,64,512]{4,3,2,1,0:T(8,128)(2,1)S(1)}, bf16[2,2,2,64,512]{4,3,2,1,0:T(8,128)(2,1)S(1)}, u32[]{:S(2)}, u32[]{:S(2)}) collective-permute-start(bf16[2,2,2,64,512]{4,3,2,1,0:T(8,128)(2,1)S(1)} %maximum_select_fusion.17), channel_id=1, source_target_pairs={{0,8},{1,9},{2,10},{3,11},{4,12},{5,13},{6,14},{7,15},{8,0},{9,1},... | collective-permute-start | bytes 1572872 | tf_op jit(solution)/shard_map/ppermute | solution.py:962
  62.5 29.8 %collective-permute-start.6 = (bf16[2,2,2,72,512]{4,3,2,1,0:T(8,128)(2,1)S(1)}, bf16[2,2,2,72,512]{4,3,2,1,0:T(8,128)(2,1)S(1)}, u32[]{:S(2)}, u32[]{:S(2)}) collective-permute-start(bf16[2,2,2,72,512]{4,3,2,1,0:T(8,128)(2,1)S(1)} %maximum_select_fusion.11), channel_id=1, source_target_pairs={{0,8},{1,9},{2,10},{3,11},{4,12},{5,13},{6,14},{7,15},{8,0},{9,1},... | collective-permute-start | bytes 1769480 | tf_op jit(solution)/shard_map/ppermute | solution.py:962
  63.3 32.6 %collective-permute-start.11 = (bf16[2,2,2,64,512]{4,3,2,1,0:T(8,128)(2,1)S(1)}, bf16[2,2,2,64,512]{4,3,2,1,0:T(8,128)(2,1)S(1)}, u32[]{:S(2)}, u32[]{:S(2)}) collective-permute-start(bf16[2,2,2,64,512]{4,3,2,1,0:T(8,128)(2,1)S(1)} %maximum_select_fusion.15), channel_id=1, source_target_pairs={{0,16},{1,17},{2,18},{3,19},{4,20},{5,21},{6,22},{7,23},{8,24},{9,... | collective-permute-start | bytes 1572872 | tf_op jit(solution)/shard_map/ppermute | solution.py:962
  69.3 25.7 %collective-permute-start.3 = (bf16[2,2,2,64,512]{4,3,2,1,0:T(8,128)(2,1)S(1)}, bf16[2,2,2,64,512]{4,3,2,1,0:T(8,128)(2,1)S(1)}, u32[]{:S(2)}, u32[]{:S(2)}) collective-permute-start(bf16[2,2,2,64,512]{4,3,2,1,0:T(8,128)(2,1)S(1)} %maximum_select_fusion.13), channel_id=1, source_target_pairs={{0,16},{1,17},{2,18},{3,19},{4,20},{5,21},{6,22},{7,23},{8,24},{9,... | collective-permute-start | bytes 1572872 | tf_op jit(solution)/shard_map/ppermute | solution.py:962
  92.3 16.9 %collective-permute-start.22 = (bf16[2,2,2,96,512]{4,3,2,1,0:T(8,128)(2,1)S(1)}, bf16[2,2,2,96,512]{4,3,2,1,0:T(8,128)(2,1)S(1)}, u32[]{:S(2)}, u32[]{:S(2)}) collective-permute-start(bf16[2,2,2,96,512]{4,3,2,1,0:T(8,128)(2,1)S(1)} %maximum_select_fusion.9), channel_id=1, source_target_pairs={{0,8},{1,9},{2,10},{3,11},{4,12},{5,13},{6,14},{7,15},{8,0},{9,1},... | collective-permute-start | bytes 2359304 | tf_op jit(solution)/shard_map/ppermute | solution.py:962
  94.0 23.5 %collective-permute-start.7 = (bf16[2,2,2,2,72,512]{5,4,3,2,0,1:T(8,128)(2,1)S(1)}, bf16[2,2,2,2,72,512]{5,4,3,2,0,1:T(8,128)(2,1)S(1)}, u32[]{:S(2)}, u32[]{:S(2)}) collective-permute-start(bf16[2,2,2,2,72,512]{5,4,3,2,0,1:T(8,128)(2,1)S(1)} %maximum_select_fusion.2), channel_id=1, source_target_pairs={{0,1},{1,0},{2,3},{3,2},{4,5},{5,4},{6,7},{7,6},{8,9},{9,8},{10,11... | collective-permute-start | bytes 3538952 | tf_op jit(solution)/shard_map/ppermute | solution.py:962
  94.3 21.7 %collective-permute-start.15 = (bf16[2,2,2,2,64,512]{5,4,3,2,0,1:T(8,128)(2,1)S(1)}, bf16[2,2,2,2,64,512]{5,4,3,2,0,1:T(8,128)(2,1)S(1)}, u32[]{:S(2)}, u32[]{:S(2)}) collective-permute-start(bf16[2,2,2,2,64,512]{5,4,3,2,0,1:T(8,128)(2,1)S(1)} %maximum_select_fusion.5), channel_id=1, source_target_pairs={{0,1},{1,0},{2,3},{3,2},{4,5},{5,4},{6,7},{7,6},{8,9},{9,8},{10,11... | collective-permute-start | bytes 3145736 | tf_op jit(solution)/shard_map/ppermute | solution.py:962
  95.0 19.5 %collective-permute-start.19 = (bf16[2,2,2,96,512]{4,3,2,1,0:T(8,128)(2,1)S(1)}, bf16[2,2,2,96,512]{4,3,2,1,0:T(8,128)(2,1)S(1)}, u32[]{:S(2)}, u32[]{:S(2)}) collective-permute-start(bf16[2,2,2,96,512]{4,3,2,1,0:T(8,128)(2,1)S(1)} %maximum_select_fusion.7), channel_id=1, source_target_pairs={{0,16},{1,17},{2,18},{3,19},{4,20},{5,21},{6,22},{7,23},{8,24},{9,... | collective-permute-start | bytes 2359304 | tf_op jit(solution)/shard_map/ppermute | solution.py:962
  95.9 22.8 %collective-permute-start.4 = (bf16[2,2,2,2,64,512]{5,4,3,2,1,0:T(8,128)(2,1)S(1)}, bf16[2,2,2,2,64,512]{5,4,3,2,1,0:T(8,128)(2,1)S(1)}, u32[]{:S(2)}, u32[]{:S(2)}) collective-permute-start(bf16[2,2,2,2,64,512]{5,4,3,2,1,0:T(8,128)(2,1)S(1)} %maximum_select_fusion.3), channel_id=1, source_target_pairs={{0,1},{1,0},{2,3},{3,2},{4,5},{5,4},{6,7},{7,6},{8,9},{9,8},{10,11... | collective-permute-start | bytes 3145736 | tf_op jit(solution)/shard_map/ppermute | solution.py:962
  109.3 49.9 %collective-permute-start.12 = (bf16[2,2,2,2,64,512]{5,4,3,2,1,0:T(8,128)(2,1)}, bf16[2,2,2,2,64,512]{5,4,3,2,1,0:T(8,128)(2,1)}, u32[]{:S(2)}, u32[]{:S(2)}) collective-permute-start(bf16[2,2,2,2,64,512]{5,4,3,2,1,0:T(8,128)(2,1)} %maximum_select_fusion.4), channel_id=1, source_target_pairs={{0,1},{1,0},{2,3},{3,2},{4,5},{5,4},{6,7},{7,6},{8,9},{9,8},{10,11... | collective-permute-start | bytes 3145736 | tf_op jit(solution)/shard_map/ppermute | solution.py:962
  114.5 61.0 %collective-permute-start.23 = (bf16[2,2,2,2,96,512]{5,4,3,2,0,1:T(8,128)(2,1)}, bf16[2,2,2,2,96,512]{5,4,3,2,0,1:T(8,128)(2,1)}, u32[]{:S(2)}, u32[]{:S(2)}) collective-permute-start(bf16[2,2,2,2,96,512]{5,4,3,2,0,1:T(8,128)(2,1)} %maximum_select_fusion.1), channel_id=1, source_target_pairs={{0,1},{1,0},{2,3},{3,2},{4,5},{5,4},{6,7},{7,6},{8,9},{9,8},{10,11... | collective-permute-start | bytes 4718600 | tf_op jit(solution)/shard_map/ppermute | solution.py:962
  116.0 62.2 %collective-permute-start.20 = (bf16[2,2,2,2,96,512]{5,4,3,2,1,0:T(8,128)(2,1)}, bf16[2,2,2,2,96,512]{5,4,3,2,1,0:T(8,128)(2,1)}, u32[]{:S(2)}, u32[]{:S(2)}) collective-permute-start(bf16[2,2,2,2,96,512]{5,4,3,2,1,0:T(8,128)(2,1)} %maximum_select_fusion), channel_id=1, source_target_pairs={{0,1},{1,0},{2,3},{3,2},{4,5},{5,4},{6,7},{7,6},{8,9},{9,8},{10,11... | collective-permute-start | bytes 4718600 | tf_op jit(solution)/shard_map/ppermute | solution.py:962
  259.1 105.5 %collective-permute-start.45 = (bf16[16,64,512]{2,1,0:T(8,128)(2,1)}, bf16[16,64,512]{2,1,0:T(8,128)(2,1)S(1)}, u32[]{:S(2)}, u32[]{:S(2)}) collective-permute-start(bf16[16,64,512]{2,1,0:T(8,128)(2,1)} %get-tuple-element.155), channel_id=1, source_target_pairs={{0,1},{1,0},{2,3},{3,2},{4,5},{5,4},{6,7},{7,6},{8,9},{9,8},{10,11... | collective-permute-start | bytes 3145736 | tf_op jit(solution)/shard_map/ppermute | solution.py:962
  259.2 106.1 %collective-permute-start.44 = (bf16[16,128,512]{2,1,0:T(8,128)(2,1)}, bf16[16,128,512]{2,1,0:T(8,128)(2,1)}, u32[]{:S(2)}, u32[]{:S(2)}) collective-permute-start(bf16[16,128,512]{2,1,0:T(8,128)(2,1)} %get-tuple-element.154), channel_id=1, source_target_pairs={{0,1},{1,0},{2,3},{3,2},{4,5},{5,4},{6,7},{7,6},{8,9},{9,8},{10,11... | collective-permute-start | bytes 6291464 | tf_op jit(solution)/shard_map/ppermute | solution.py:962
  283.3 110.8 %collective-permute-start.31 = (bf16[16,128,512]{2,1,0:T(8,128)(2,1)}, bf16[16,128,512]{2,1,0:T(8,128)(2,1)S(1)}, u32[]{:S(2)}, u32[]{:S(2)}) collective-permute-start(bf16[16,128,512]{2,1,0:T(8,128)(2,1)} %get-tuple-element.133), channel_id=1, source_target_pairs={{0,1},{1,0},{2,3},{3,2},{4,5},{5,4},{6,7},{7,6},{8,9},{9,8},{10,11... | collective-permute-start | bytes 6291464 | tf_op jit(solution)/shard_map/ppermute | solution.py:962
  345.8 18.3 %collective-permute-start.39 = (f32[16,512]{1,0:T(8,128)S(1)}, f32[16,512]{1,0:T(8,128)S(1)}, u32[]{:S(2)}, u32[]{:S(2)}) collective-permute-start(f32[16,512]{1,0:T(8,128)S(1)} %concatenate.319), channel_id=1, source_target_pairs={{0,1},{1,0},{2,3},{3,2},{4,5},{5,4},{6,7},{7,6},{8,9},{9,8},{10,11... | collective-permute-start | bytes 98312 | tf_op jit(solution)/shard_map/ppermute | solution.py:962
  355.1 17.1 %collective-permute-start.24 = (bf16[16,64,512]{2,1,0:T(8,128)(2,1)}, bf16[16,64,512]{2,1,0:T(8,128)(2,1)S(1)}, u32[]{:S(2)}, u32[]{:S(2)}) collective-permute-start(bf16[16,64,512]{2,1,0:T(8,128)(2,1)} %get-tuple-element.118), channel_id=1, source_target_pairs={{0,1},{1,0},{2,3},{3,2},{4,5},{5,4},{6,7},{7,6},{8,9},{9,8},{10,11... | collective-permute-start | bytes 3145736 | tf_op jit(solution)/shard_map/ppermute | solution.py:962
  364.1 28.6 %collective-permute-start.32 = (bf16[16,64,512]{2,1,0:T(8,128)(2,1)}, bf16[16,64,512]{2,1,0:T(8,128)(2,1)S(1)}, u32[]{:S(2)}, u32[]{:S(2)}) collective-permute-start(bf16[16,64,512]{2,1,0:T(8,128)(2,1)} %get-tuple-element.134), channel_id=1, source_target_pairs={{0,1},{1,0},{2,3},{3,2},{4,5},{5,4},{6,7},{7,6},{8,9},{9,8},{10,11... | collective-permute-start | bytes 3145736 | tf_op jit(solution)/shard_map/ppermute | solution.py:962
  370.5 61.1 %collective-permute-start.46 = (bf16[2,4,96,512]{3,2,1,0:T(8,128)(2,1)}, bf16[2,4,96,512]{3,2,1,0:T(8,128)(2,1)S(1)}, u32[]{:S(2)}, u32[]{:S(2)}) collective-permute-start(bf16[2,4,96,512]{3,2,1,0:T(8,128)(2,1)} %get-tuple-element.157), channel_id=1, source_target_pairs={{0,8},{1,9},{2,10},{3,11},{4,12},{5,13},{6,14},{7,15},{8,0},{9,1},... | collective-permute-start | bytes 2359304 | tf_op jit(solution)/shard_map/ppermute | solution.py:962
  371.7 61.5 %collective-permute-start.47 = (bf16[2,4,96,512]{3,2,1,0:T(8,128)(2,1)}, bf16[2,4,96,512]{3,2,1,0:T(8,128)(2,1)}, u32[]{:S(2)}, u32[]{:S(2)}) collective-permute-start(bf16[2,4,96,512]{3,2,1,0:T(8,128)(2,1)} %get-tuple-element.159), channel_id=1, source_target_pairs={{0,16},{1,17},{2,18},{3,19},{4,20},{5,21},{6,22},{7,23},{8,24},{9,... | collective-permute-start | bytes 2359304 | tf_op jit(solution)/shard_map/ppermute | solution.py:962
  372.2 19.4 %collective-permute-start.41 = (f32[16,512]{1,0:T(8,128)S(1)}, f32[16,512]{1,0:T(8,128)S(1)}, u32[]{:S(2)}, u32[]{:S(2)}) collective-permute-start(f32[16,512]{1,0:T(8,128)S(1)} %add.64), channel_id=1, source_target_pairs={{0,16},{1,17},{2,18},{3,19},{4,20},{5,21},{6,22},{7,23},{8,24},{9,... | collective-permute-start | bytes 98312 | tf_op jit(solution)/shard_map/ppermute | solution.py:962
  400.3 43.1 %collective-permute-start.33 = (bf16[2,4,96,512]{3,2,1,0:T(8,128)(2,1)}, bf16[2,4,96,512]{3,2,1,0:T(8,128)(2,1)S(1)}, u32[]{:S(2)}, u32[]{:S(2)}) collective-permute-start(bf16[2,4,96,512]{3,2,1,0:T(8,128)(2,1)} %get-tuple-element.136), channel_id=1, source_target_pairs={{0,8},{1,9},{2,10},{3,11},{4,12},{5,13},{6,14},{7,15},{8,0},{9,1},... | collective-permute-start | bytes 2359304 | tf_op jit(solution)/shard_map/ppermute | solution.py:962
  401.2 42.2 %collective-permute-start.34 = (bf16[2,4,96,512]{3,2,1,0:T(8,128)(2,1)}, bf16[2,4,96,512]{3,2,1,0:T(8,128)(2,1)S(1)}, u32[]{:S(2)}, u32[]{:S(2)}) collective-permute-start(bf16[2,4,96,512]{3,2,1,0:T(8,128)(2,1)} %get-tuple-element.138), channel_id=1, source_target_pairs={{0,16},{1,17},{2,18},{3,19},{4,20},{5,21},{6,22},{7,23},{8,24},{9,... | collective-permute-start | bytes 2359304 | tf_op jit(solution)/shard_map/ppermute | solution.py:962
  401.7 22.6 %collective-permute-start.26 = (bf16[2,4,32,512]{3,2,1,0:T(8,128)(2,1)S(1)}, bf16[2,4,32,512]{3,2,1,0:T(8,128)(2,1)S(1)}, u32[]{:S(2)}, u32[]{:S(2)}) collective-permute-start(bf16[2,4,32,512]{3,2,1,0:T(8,128)(2,1)S(1)} %copy-done.33), channel_id=1, source_target_pairs={{0,16},{1,17},{2,18},{3,19},{4,20},{5,21},{6,22},{7,23},{8,24},{9,... | collective-permute-start | bytes 786440 | tf_op jit(solution)/shard_map/ppermute | solution.py:962
  437.2 16.0 %collective-permute-start.48 = (bf16[4,96,512]{2,1,0:T(8,128)(2,1)}, bf16[4,96,512]{2,1,0:T(8,128)(2,1)S(1)}, u32[]{:S(2)}, u32[]{:S(2)}) collective-permute-start(bf16[4,96,512]{2,1,0:T(8,128)(2,1)} %get-tuple-element.161), channel_id=1, source_target_pairs={{0,16},{1,17},{2,18},{3,19},{4,20},{5,21},{6,22},{7,23},{8,24},{9,... | collective-permute-start | bytes 1179656 | tf_op jit(solution)/shard_map/ppermute | solution.py:962
  456.4 25.8 %collective-permute-start.50 = (bf16[2,192,512]{2,1,0:T(8,128)(2,1)}, bf16[2,192,512]{2,1,0:T(8,128)(2,1)S(1)}, u32[]{:S(2)}, u32[]{:S(2)}) collective-permute-start(bf16[2,192,512]{2,1,0:T(8,128)(2,1)} %get-tuple-element.165), channel_id=1, source_target_pairs={{0,4},{1,5},{2,6},{3,7},{4,0},{5,1},{6,2},{7,3},{8,12},{9,13},{10,... | collective-permute-start | bytes 1179656 | tf_op jit(solution)/shard_map/ppermute | solution.py:962
  462.9 25.6 %collective-permute-start.37 = (bf16[2,192,512]{2,1,0:T(8,128)(2,1)}, bf16[2,192,512]{2,1,0:T(8,128)(2,1)S(1)}, u32[]{:S(2)}, u32[]{:S(2)}) collective-permute-start(bf16[2,192,512]{2,1,0:T(8,128)(2,1)} %get-tuple-element.144), channel_id=1, source_target_pairs={{0,4},{1,5},{2,6},{3,7},{4,0},{5,1},{6,2},{7,3},{8,12},{9,13},{10,... | collective-permute-start | bytes 1179656 | tf_op jit(solution)/shard_map/ppermute | solution.py:962
  (54 other events, 369.1 us)

commit v2 on v1

v2 whole, which is shorter than its diff:
```python
import functools
import math
import jax
import jax.numpy as jnp
from jax import lax
from jax.experimental import pallas as pl
from jax.experimental.pallas import tpu as pltpu
from jax.sharding import PartitionSpec as P

D = 512
HEAD = 64
FF = 2048
VOCAB = 523
SLOT = 512
SHARDS = 32
BLOCKS = FF // D
EPS = 1e-05
PAIR = 2 * HEAD
PAIRS = D // PAIR
GROUP = 16
MASKED = -(2.0**30)
COST = 3.0
UPPER_MB = 56
BF = jnp.bfloat16
F32 = jnp.float32

SELF_ROWS, SELF_IN, SELF_OUT = 64, 0, 48
FFN_ROWS, FFN_IN, FFN_OUT = 128, 0, 64
CROSS_ROWS, CROSS_Q, CROSS_KV, CROSS_OUT = 64, 0, 16, 48


def nn(left, right):
    return lax.dot_general(left, right, (((1,), (0,)), ((), ())), preferred_element_type=F32)


def nt(left, right):
    return lax.dot_general(left, right, (((1,), (1,)), ((), ())), preferred_element_type=F32)


def wide(ref, start, block):
    first = start + 16 * block
    return ref[:, :, first : first + 16, :].reshape(D, D)


def tall(ref, start, block):
    return ref[4 * block : 4 * block + 4, :, start : start + 64, :].reshape(D, D)


def put_shards(core, refs, lead, rows, shards):
    if len(refs) == 1:
        refs[0][lead, :, rows, :] = shards.astype(BF)
    else:
        refs[0][lead, rows, :] = jnp.where(core == 0, shards[:, 0], shards[:, 1]).astype(BF)
        refs[1][lead, rows, :] = jnp.where(core == 0, shards[:, 1], shards[:, 0]).astype(BF)


def put_wide(core, refs, start, block, value):
    rows = slice(start + 16 * block, start + 16 * block + 16)
    put_shards(core, refs, slice(0, SHARDS // 2), rows, value.reshape(SHARDS // 2, 2, 16, D))


def put_tall(core, refs, start, block, value):
    put_shards(core, refs, slice(4 * block, 4 * block + 4), slice(start, start + 64), value.reshape(4, 2, 64, D))


class Weights:
    def __init__(self, arrays, place, half):
        self.arrays = arrays
        self.place = place
        self.half = half


def weight_copies(pieces, place, half, core, ref, sems, low, high):
    if len(pieces) == 1:
        return [pltpu.make_async_copy(pieces[0].at[:, :, place + low : place + high, :], ref, sems.at[0])]
    copies = []
    for number in range(2):
        first, last = max(low, number * half), min(high, (number + 1) * half)
        if first < last:
            source = slice(place + first - number * half, place + last - number * half)
            for other in range(2):
                copies.append(
                    pltpu.make_async_copy(
                        pieces[2 * number + other].at[:, source, :],
                        ref.at[:, core if other == 0 else 1 - core, first - low : last - low, :],
                        sems.at[2 * number + other],
                    )
                )
    return copies


def on_first_slot(action, copies):
    @pl.when(pl.program_id(0) == 0)
    def _():
        for copy in copies:
            getattr(copy, action)()


def norm_grad_rows(ref, gains_and_shifts):
    rows = jnp.concatenate(gains_and_shifts + [jnp.zeros((8 - len(gains_and_shifts), D), F32)], 0)
    add_up(ref, rows)


def last_slot():
    return pl.program_id(0) == pl.num_programs(0) - 1


def lanes_of(pair):
    return slice(pair * PAIR, (pair + 1) * PAIR)


def normalize(values):
    centered = values - jnp.mean(values, -1, keepdims=True)
    scale = lax.rsqrt(jnp.mean(centered * centered, -1, keepdims=True) + EPS)
    return centered * scale, scale


def norm_backward(grad_normed, unit, scale, gain):
    grad_unit = grad_normed * gain
    first = jnp.mean(grad_unit, -1, keepdims=True)
    second = jnp.mean(grad_unit * unit, -1, keepdims=True)
    grad_gain = jnp.sum(grad_normed * unit, 0, keepdims=True)
    grad_shift = jnp.sum(grad_normed, 0, keepdims=True)
    return scale * (grad_unit - first - unit * second), grad_gain, grad_shift


def gelu_both(hidden):
    size = jnp.abs(hidden)
    ratio = 1.0 / (1.0 + (0.3275911 / math.sqrt(2.0)) * size)
    bell = jnp.exp(-0.5 * hidden * hidden)
    series = 0.5 * 1.061405429
    for factor in (-1.453152027, 1.421413741, -0.284496736, 0.254829592):
        series = series * ratio + 0.5 * factor
    tail = series * ratio * bell
    share = jnp.where(hidden >= 0, 1.0 - tail, tail)
    return hidden * share, share + hidden * bell * (1.0 / math.sqrt(2.0 * math.pi))


def lane_index():
    return lax.broadcasted_iota(jnp.int32, (1, 128), 1)


def query_extra(kind):
    place = lax.broadcasted_iota(jnp.int32, (SLOT, 128), 0)
    lane = lax.broadcasted_iota(jnp.int32, (SLOT, 128), 1)
    return (lax.shift_right_logical(place, kind + 7) == lane).astype(F32).astype(BF)


def key_extra(kind, lengths):
    place = lax.broadcasted_iota(jnp.int32, (SLOT, 128), 0)
    lane = lax.broadcasted_iota(jnp.int32, (SLOT, 128), 1)
    size = lax.shift_left(jnp.int32(128), kind)
    within = place & (size - 1)
    limit = jnp.where(
        lane == 0, lengths[0], jnp.where(lane == 1, lengths[1], jnp.where(lane == 2, lengths[2], lengths[3]))
    )
    allowed = (lax.shift_right_logical(place, kind + 7) == lane) & (within < limit)
    return jnp.where(allowed | (lane >= 4), 0.0, MASKED).astype(BF)


def halves():
    lane = lane_index()
    return ((lane < HEAD).astype(F32).astype(BF), (lane >= HEAD).astype(F32).astype(BF))


def future(rows, columns, first):
    row = lax.broadcasted_iota(jnp.int32, (rows, columns), 0)
    column = lax.broadcasted_iota(jnp.int32, (rows, columns), 1) + first
    return row <= column


def pipelined(items, ahead, start, finish):
    waiting = []
    for number, item in enumerate(items):
        while len(waiting) <= ahead and number + len(waiting) < len(items):
            waiting.append(start(*items[number + len(waiting)]))
        finish(*item, waiting.pop(0))


def attend(query_of, key_of, value_of, store, kind, lengths, causal):
    step = 256
    query_lanes = query_extra(kind)
    key_lanes = key_extra(kind, lengths)
    ones = jnp.ones((HEAD, SLOT), BF)
    mask = halves()
    inputs, parts, sums = {}, {}, {}

    def seen(first):
        return first + step if causal else SLOT

    def start(pair, half, first):
        if pair not in inputs:
            queries = query_of(pair) * BF(HEAD**-0.5)
            inputs[pair] = (queries, jnp.concatenate([key_of(pair), key_lanes], 1), value_of(pair).T)
        queries, keys, _ = inputs[pair]
        own = jnp.concatenate([queries[first : first + step] * mask[half], query_lanes[first : first + step]], 1)
        return nt(keys[: seen(first)], own)

    def finish(pair, half, first, scores):
        values = inputs[pair][2]
        if causal:
            scores = jnp.where(future(seen(first), step, first), scores, MASKED)
        largest = jnp.max(scores, 0, keepdims=True)
        powers = jnp.exp(scores - largest).astype(BF)
        head_values = jnp.concatenate([values[:HEAD], ones] if half == 0 else [ones, values[HEAD:]], 0)
        context = nn(head_values[:, : seen(first)], powers)
        total = context[HEAD : HEAD + 1] if half == 0 else context[0:1]
        parts[pair, half, first] = (context[:HEAD] if half == 0 else context[HEAD:]) * (1.0 / total)
        sums[pair, half, first] = largest + jnp.log(total)
        if half == 1 and first == SLOT - step:
            rows = [jnp.concatenate([parts[pair, side, at] for at in range(0, SLOT, step)], 1) for side in range(2)]
            store(pair, jnp.concatenate(rows, 0).T)

    items = [(pair, half, first) for pair in range(PAIRS) for half in range(2) for first in range(0, SLOT, step)]
    pipelined(items, 4, start, finish)
    spread = [
        jnp.broadcast_to(jnp.concatenate([sums[pair, half, at] for at in range(0, SLOT, step)], 1), (GROUP, SLOT))
        for pair in range(PAIRS)
        for half in range(2)
    ]
    return split(jnp.concatenate(spread, 0).T, 4)


def split(values, first):
    lane = lane_index() % GROUP
    high = values.astype(BF).astype(F32)
    rest = values - high
    middle = rest.astype(BF).astype(F32)
    low = rest - middle
    terms = jnp.where(
        lane == first, high, jnp.where(lane == first + 1, middle, jnp.where(lane == first + 2, low, 0.0))
    )
    return (-terms).astype(BF)


def attend_back(query_of, key_of, value_of, grad_of, contexts, grads, store, logsums, kind, lengths, causal):
    step = 256 if causal else SLOT
    query_lanes = query_extra(kind) + logsums
    key_lanes = key_extra(kind, lengths)
    products = grads.astype(F32) * contexts
    high = products.astype(BF)
    low = (products - high.astype(F32)).astype(BF)
    source = lax.broadcasted_iota(jnp.int32, (D, 128), 0) // HEAD
    target = lax.broadcasted_iota(jnp.int32, (D, 128), 1) // GROUP
    picker = (source == target).astype(F32).astype(BF)
    inner_lanes = split(nn(high, picker) + nn(low, picker), 0)
    lane = lane_index()
    within, group = lane % GROUP, lane // GROUP
    mask = halves()
    inputs, heads, results = {}, {}, {}

    def seen(first):
        return first + step if causal else SLOT

    def start(pair, half, first):
        if pair not in inputs:
            inputs[pair] = (query_of(pair) * BF(HEAD**-0.5), key_of(pair), value_of(pair), grad_of(pair), key_of(pair).T)
        queries, keys, values, grad_context, _ = inputs[pair]
        if (pair, half) not in heads:
            head = 2 * pair + half
            sum_lanes = ((group == head) & (within >= 4) & (within < 7)).astype(F32).astype(BF)
            one_lanes = ((group == head) & (within < 3)).astype(F32).astype(BF)
            heads[pair, half] = (
                jnp.concatenate([keys, key_lanes + sum_lanes], 1),
                jnp.concatenate([queries * mask[half], query_lanes], 1),
                jnp.concatenate([values, jnp.broadcast_to(one_lanes, (SLOT, 128))], 1),
                jnp.concatenate([grad_context * mask[half], inner_lanes], 1),
            )
        left, right, value_left, grad_right = heads[pair, half]
        here = slice(first, first + step)
        return nt(left[: seen(first)], right[here]), nt(value_left[: seen(first)], grad_right[here])

    def finish(pair, half, first, products):
        scores, grad_weights = products
        queries, _, _, grad_context, keys_t = inputs[pair]
        if causal:
            scores = jnp.where(future(seen(first), step, first), scores, MASKED)
        weights = jnp.exp(scores)
        grad_scores = (weights * grad_weights).astype(BF)
        here = slice(first, first + step)
        for_queries = nn(keys_t[half * HEAD : half * HEAD + HEAD, : seen(first)], grad_scores)
        for_keys = nn(grad_scores, queries[here] * mask[half])
        for_values = nn(weights.astype(BF), grad_context[here] * mask[half])
        if seen(first) < SLOT:
            none = jnp.zeros((SLOT - seen(first), PAIR), F32)
            for_keys = jnp.concatenate([for_keys, none], 0)
            for_values = jnp.concatenate([for_values, none], 0)
        results[pair, half, first] = (for_queries, for_keys, for_values)
        if half == 1 and first == SLOT - step:
            places = range(0, SLOT, step)
            rows = [jnp.concatenate([results[pair, side, at][0] for at in places], 1) for side in range(2)]
            keys_sum, values_sum = (
                functools.reduce(jnp.add, [results[pair, side, at][number] for side in range(2) for at in places])
                for number in (1, 2)
            )
            store(
                pair,
                (jnp.concatenate(rows, 0) * HEAD**-0.5).T.astype(BF),
                keys_sum.astype(BF),
                values_sum.astype(BF),
            )

    items = [(pair, half, first) for pair in range(PAIRS) for half in range(2) for first in range(0, SLOT, step)]
    pipelined(items, 2 if causal else 1, start, finish)


def lengths_at(ref, slot):
    return [ref[slot, entry] for entry in range(4)]


def at(ref, start):
    return lambda pair: ref[0, :, start + pair * PAIR : start + (pair + 1) * PAIR]


def add_up(ref, value):
    slot = pl.program_id(0)

    @pl.when(slot == 0)
    def _():
        ref[...] = value

    @pl.when(slot > 0)
    def _():
        ref[...] += value


def project_kernel(me_ref, x_ref, w, norm_ref, qkv_ref, weights_ref, sems, *, place, half):
    copies = weight_copies(w, place, half, me_ref[4], weights_ref, sems, SELF_IN, SELF_OUT)
    on_first_slot("start", copies)
    unit, _ = normalize(x_ref[0].astype(F32))
    normed = (unit * norm_ref[0:1] + norm_ref[1:2]).astype(BF)
    on_first_slot("wait", copies)
    for block in range(3):
        qkv_ref[0, :, block * D : (block + 1) * D] = nn(normed, wide(weights_ref, 0, block)).astype(BF)


def keep_context(context_ref, rest_ref):
    def store(pair, context):
        high = context.astype(BF)
        context_ref[0, :, lanes_of(pair)] = high
        rest_ref[0, :, lanes_of(pair)] = (context - high.astype(F32)).astype(BF)

    return store


def self_attend_kernel(
    kind_ref,
    lengths_ref,
    me_ref,
    x_ref,
    qkv_ref,
    w,
    out_ref,
    context_ref,
    rest_ref,
    sums_ref,
    weights_ref,
    sems,
    *,
    place,
    half,
    causal,
):
    slot = pl.program_id(0)
    copies = weight_copies(w, place, half, me_ref[4], weights_ref, sems, SELF_OUT, SELF_ROWS)
    on_first_slot("start", copies)
    sums_ref[0] = attend(
        at(qkv_ref, 0),
        at(qkv_ref, D),
        at(qkv_ref, 2 * D),
        keep_context(context_ref, rest_ref),
        kind_ref[slot],
        lengths_at(lengths_ref, slot),
        causal,
    )
    on_first_slot("wait", copies)
    out_ref[0] = x_ref[0].astype(F32) + nn(context_ref[0], wide(weights_ref, 0, 0))


def ffn_forward_kernel(
    me_ref, r_ref, w, norm_ref, out_ref, active_ref, slope_ref, weights_ref, sems, *, place, half
):
    copies = weight_copies(w, place, half, me_ref[4], weights_ref, sems, 0, FFN_ROWS)
    on_first_slot("start", copies)
    values = r_ref[0]
    unit, _ = normalize(values)
    normed = (unit * norm_ref[2:3] + norm_ref[3:4]).astype(BF)
    total = values
    on_first_slot("wait", copies)
    for block in range(BLOCKS):
        active, slope = gelu_both(nn(normed, wide(weights_ref, FFN_IN, block)))
        active = active.astype(BF)
        active_ref[0, :, block * D : (block + 1) * D] = active
        slope_ref[0, :, block * D : (block + 1) * D] = slope.astype(BF)
        total = total + nn(active, tall(weights_ref, FFN_OUT, block))
    out_ref[0] = total.astype(BF)


def ffn_back(grad_out, unit, scale, normed, gain, active_of, slope_of, w_ref, sums_ref):
    low = grad_out.astype(BF)
    normed_t = normed.T
    grad_normed = None
    for block in range(BLOCKS):
        grad_active = nt(low, tall(w_ref, FFN_OUT, block))
        grad_hidden = (grad_active * slope_of(block)).astype(BF)
        add_up(sums_ref.at[1, block], nn(active_of(block).T, low))
        add_up(sums_ref.at[0, block], nn(normed_t, grad_hidden))
        part = nt(grad_hidden, wide(w_ref, FFN_IN, block))
        grad_normed = part if grad_normed is None else grad_normed + part
    grad, grad_gain, grad_shift = norm_backward(grad_normed, unit, scale, gain)
    return grad_out + grad, grad_gain, grad_shift


def ffn_put(core, sums_ref, grads):
    @pl.when(last_slot())
    def _():
        for block in range(BLOCKS):
            put_wide(core, grads, FFN_IN, block, sums_ref[0, block])
            put_tall(core, grads, FFN_OUT, block, sums_ref[1, block])


def ffn_backward_kernel(
    me_ref,
    grad_out_ref,
    r_ref,
    active_ref,
    slope_ref,
    w,
    norm_ref,
    grad_ref,
    grads,
    norm_grad_ref,
    weights_ref,
    sems,
    sums_ref,
    *,
    place,
    half,
):
    copies = weight_copies(w, place, half, me_ref[4], weights_ref, sems, 0, FFN_ROWS)
    on_first_slot("start", copies)
    unit, scale = normalize(r_ref[0])
    gain = norm_ref[2:3]
    normed = (unit * gain + norm_ref[3:4]).astype(BF)
    on_first_slot("wait", copies)
    grad, grad_gain, grad_shift = ffn_back(
        grad_out_ref[0],
        unit,
        scale,
        normed,
        gain,
        lambda block: active_ref[0, :, block * D : (block + 1) * D],
        lambda block: slope_ref[0, :, block * D : (block + 1) * D].astype(F32),
        weights_ref,
        sums_ref,
    )
    grad_ref[0] = grad
    norm_grad_rows(norm_grad_ref, [grad_gain, grad_shift])
    ffn_put(me_ref[4], sums_ref, grads)


def attend_back_kernel(
    kind_ref,
    lengths_ref,
    me_ref,
    grad_out_ref,
    q_ref,
    kv_ref,
    context_ref,
    rest_ref,
    sums_in_ref,
    w,
    proj_ref,
    weights_ref,
    sems,
    low_ref,
    *,
    place,
    half,
    causal,
    start,
    key_at,
):
    slot = pl.program_id(0)
    copies = weight_copies(w, place, half, me_ref[4], weights_ref, sems, start, start + 16)
    on_first_slot("start", copies)
    on_first_slot("wait", copies)
    low_ref[0] = nt(grad_out_ref[0].astype(BF), wide(weights_ref, 0, 0)).astype(BF)

    def store(pair, grad_query, grad_key, grad_value):
        for number, value in enumerate((grad_query, grad_key, grad_value)):
            proj_ref[0, :, number * D + pair * PAIR : number * D + (pair + 1) * PAIR] = value

    attend_back(
        at(q_ref, 0),
        at(kv_ref, key_at),
        at(kv_ref, key_at + D),
        at(low_ref, 0),
        context_ref[0].astype(F32) + rest_ref[0].astype(F32),
        low_ref[0],
        store,
        sums_in_ref[0],
        kind_ref[slot],
        lengths_at(lengths_ref, slot),
        causal,
    )


def upper_kernel(
    kind_ref,
    lengths_ref,
    me_ref,
    r_ref,
    memory_ref,
    enc_cotangent_ref,
    dec_cotangent_ref,
    w_cross,
    w_ff,
    norm_ref,
    out_ref,
    grad_ref,
    memory_grad_ref,
    ff_grads,
    cross_grads,
    norm_grad_ref,
    cross_ref,
    cross_sems,
    ff_ref,
    ff_sems,
    qkv_ref,
    context_ref,
    low_ref,
    proj_ref,
    active_ref,
    slope_ref,
    second_ref,
    ff_sums_ref,
    sums_ref,
    *,
    cross_place,
    cross_half,
    ff_place,
    ff_half,
):
    slot = pl.program_id(0)
    core = me_ref[4]
    copies = weight_copies(w_cross, cross_place, cross_half, core, cross_ref, cross_sems, 0, CROSS_ROWS)
    ff_copies = weight_copies(w_ff, ff_place, ff_half, core, ff_ref, ff_sems, 0, FFN_ROWS)
    on_first_slot("start", copies + ff_copies)
    kind, lengths = kind_ref[slot], lengths_at(lengths_ref, slot)
    unit, scale = normalize(r_ref[0])
    gain = norm_ref[2:3]
    normed = (unit * gain + norm_ref[3:4]).astype(BF)
    memory = memory_ref[0]
    on_first_slot("wait", copies)
    qkv_ref[0, :, :D] = nn(normed, wide(cross_ref, CROSS_Q, 0)).astype(BF)
    for block in range(2):
        qkv_ref[0, :, (block + 1) * D : (block + 2) * D] = nn(memory, wide(cross_ref, CROSS_KV, block)).astype(BF)

    def keep(pair, context):
        context_ref[:, lanes_of(pair)] = context

    logsums = attend(at(qkv_ref, 0), at(qkv_ref, D), at(qkv_ref, 2 * D), keep, kind, lengths, False)
    second = r_ref[0] + nn(context_ref[...].astype(BF), wide(cross_ref, CROSS_OUT, 0))

    ff_unit, ff_scale = normalize(second)
    ff_gain = norm_ref[4:5]
    ff_normed = (ff_unit * ff_gain + norm_ref[5:6]).astype(BF)
    on_first_slot("wait", ff_copies)
    total = second
    for block in range(BLOCKS):
        active, slope = gelu_both(nn(ff_normed, wide(ff_ref, FFN_IN, block)))
        active = active.astype(BF)
        active_ref[block] = active
        slope_ref[block] = slope.astype(BF)
        total = total + nn(active, tall(ff_ref, FFN_OUT, block))
    out_ref[0] = total.astype(BF)
    grad_second, ff_gain_grad, ff_shift_grad = ffn_back(
        dec_cotangent_ref[0].astype(F32),
        ff_unit,
        ff_scale,
        ff_normed,
        ff_gain,
        lambda block: active_ref[block],
        lambda block: slope_ref[block].astype(F32),
        ff_ref,
        ff_sums_ref,
    )
    second_ref[...] = grad_second
    ffn_put(core, ff_sums_ref, ff_grads)

    low = second_ref[...].astype(BF)
    add_up(sums_ref.at[3], nn(context_ref[...].astype(BF).T, low))
    low_ref[0] = nt(low, wide(cross_ref, CROSS_OUT, 0)).astype(BF)

    def store(pair, grad_query, grad_key, grad_value):
        for number, value in enumerate((grad_query, grad_key, grad_value)):
            proj_ref[number, :, lanes_of(pair)] = value

    attend_back(
        at(qkv_ref, 0),
        at(qkv_ref, D),
        at(qkv_ref, 2 * D),
        at(low_ref, 0),
        context_ref[...],
        low_ref[0],
        store,
        logsums,
        kind,
        lengths,
        False,
    )
    unit, scale = normalize(r_ref[0])
    normed_t = (unit * gain + norm_ref[3:4]).astype(BF).T
    memory_t = memory_ref[0].T
    add_up(sums_ref.at[0], nn(normed_t, proj_ref[0]))
    add_up(sums_ref.at[1], nn(memory_t, proj_ref[1]))
    add_up(sums_ref.at[2], nn(memory_t, proj_ref[2]))
    memory_grad_ref[0] = (
        enc_cotangent_ref[0].astype(F32)
        + nt(proj_ref[1], wide(cross_ref, CROSS_KV, 0))
        + nt(proj_ref[2], wide(cross_ref, CROSS_KV, 1))
    )
    grad, grad_gain, grad_shift = norm_backward(nt(proj_ref[0], wide(cross_ref, CROSS_Q, 0)), unit, scale, gain)
    grad_ref[0] = second_ref[...] + grad
    norm_grad_rows(norm_grad_ref, [grad_gain, grad_shift, ff_gain_grad, ff_shift_grad])

    @pl.when(last_slot())
    def _():
        put_wide(core, cross_grads, CROSS_Q, 0, sums_ref[0])
        put_wide(core, cross_grads, CROSS_KV, 0, sums_ref[1])
        put_wide(core, cross_grads, CROSS_KV, 1, sums_ref[2])
        put_wide(core, cross_grads, CROSS_OUT, 0, sums_ref[3])


def self_weight_kernel(
    me_ref, grad_out_ref, x_ref, context_ref, proj_ref, norm_ref, grads, sums_ref
):
    unit, _ = normalize(x_ref[0].astype(F32))
    normed_t = (unit * norm_ref[0:1] + norm_ref[1:2]).astype(BF).T
    for block in range(3):
        add_up(sums_ref.at[block], nn(normed_t, proj_ref[0, :, block * D : (block + 1) * D]))
    add_up(sums_ref.at[3], nn(context_ref[0].T, grad_out_ref[0].astype(BF)))

    @pl.when(last_slot())
    def _():
        core = me_ref[4]
        for block in range(3):
            put_wide(core, grads, SELF_IN, block, sums_ref[block])
        put_wide(core, grads, SELF_OUT, 0, sums_ref[3])


def self_rows_kernel(
    me_ref,
    grad_out_ref,
    x_ref,
    proj_ref,
    w,
    norm_ref,
    grad_ref,
    norm_grad_ref,
    weights_ref,
    sems,
    *,
    place,
    half,
):
    copies = weight_copies(w, place, half, me_ref[4], weights_ref, sems, SELF_IN, SELF_OUT)
    on_first_slot("start", copies)
    unit, scale = normalize(x_ref[0].astype(F32))
    on_first_slot("wait", copies)
    grad_normed = None
    for block in range(3):
        part = nt(proj_ref[0, :, block * D : (block + 1) * D], wide(weights_ref, 0, block))
        grad_normed = part if grad_normed is None else grad_normed + part
    grad, grad_gain, grad_shift = norm_backward(grad_normed, unit, scale, norm_ref[0:1])
    grad_ref[0] = (grad_out_ref[0] + grad).astype(BF)
    norm_grad_rows(norm_grad_ref, [grad_gain, grad_shift])


def per_slot(*shape):
    return pl.BlockSpec((1,) + shape, lambda slot: (slot,) + (0,) * len(shape))


def whole_block(*shape):
    return pl.BlockSpec(shape, lambda slot: (0,) * len(shape))


def scalars():
    return pl.BlockSpec(memory_space=pltpu.SMEM)


def in_place():
    return pl.BlockSpec(memory_space=pl.ANY)


def in_vmem():
    return pl.BlockSpec(memory_space=pltpu.VMEM)


class Order:
    def __init__(self):
        self.token = ()

    def call(self, kernel, name, steps, ins, outs, scratch, args, megabytes, us):
        leaf = lambda out: isinstance(out[0], pl.BlockSpec)
        shaped = lambda out: pltpu.HBM(*out[1:3]) if out[3:] else jax.ShapeDtypeStruct(*out[1:])
        specs = [out[0] if leaf(out) else tuple(part[0] for part in out) for out in outs]
        shapes = [shaped(out) if leaf(out) else tuple(shaped(part) for part in out) for out in outs]
        place = len(ins) + len(outs)

        def body(before, *refs):
            refs[place][...] = jnp.zeros((8, 128), F32)
            kernel(*refs[:place], *refs[place + 1 :])

        *results, token = pl.pallas_call(
            body,
            name=name,
            grid=(steps,),
            in_specs=[tuple(in_place() for _ in self.token)] + ins,
            out_specs=specs + [whole_block(8, 128)],
            out_shape=shapes + [jax.ShapeDtypeStruct((8, 128), F32)],
            scratch_shapes=scratch,
            cost_estimate=pl.CostEstimate(flops=int(COST * us * 1.15e9), bytes_accessed=1 << 16, transcendentals=0),
            compiler_params=pltpu.CompilerParams(
                vmem_limit_bytes=megabytes << 20, dimension_semantics=("arbitrary",)
            ),
        )(self.token, *args)
        self.token = (token,)
        return results


def slot_array(slots, width, dtype, to_hbm=False):
    return (per_slot(SLOT, width), (slots, SLOT, width), dtype) + (("hbm",) if to_hbm else ())


def stay(*arrays):
    return tuple(pltpu.with_memory_space_constraint(array, pltpu.HBM) for array in arrays)


def grad_group(rows, parted):
    shape, count = ((SHARDS // 2, rows, D), 2) if parted else ((SHARDS // 2, 2, rows, D), 1)
    once = pl.BlockSpec(shape, lambda slot: (0,) * len(shape), pipeline_mode=pl.Buffered(1))
    return ((once, shape, BF),) * count


NORM_GRADS = (whole_block(8, D), (8, D), F32)


def weight_scratch(rows):
    return [pltpu.VMEM((SHARDS // 2, 2, rows, D), BF), pltpu.SemaphoreType.DMA((4,))]


def bound(kernel, weights, **options):
    return functools.partial(kernel, place=weights.place, half=weights.half, **options)


def held(weights):
    return tuple(in_place() for _ in weights.arrays)


def project(order, me, rows, weights, norms, name):
    slots = rows.shape[0]
    return order.call(
        bound(project_kernel, weights),
        name,
        slots,
        [scalars(), per_slot(SLOT, D), held(weights), whole_block(*norms.shape)],
        [slot_array(slots, 3 * D, BF)],
        weight_scratch(SELF_OUT - SELF_IN),
        (me, *stay(rows), stay(*weights.arrays), norms),
        12,
        5,
    )[0]


def self_attend(order, kinds, lengths, me, rows, qkv, weights, causal, name):
    slots = rows.shape[0]
    return order.call(
        bound(self_attend_kernel, weights, causal=causal),
        name,
        slots,
        [scalars(), scalars(), scalars(), per_slot(SLOT, D), per_slot(SLOT, 3 * D), held(weights)],
        [slot_array(slots, D, F32, True)] + [slot_array(slots, D, BF, True)] * 2 + [slot_array(slots, 128, BF, True)],
        weight_scratch(SELF_ROWS - SELF_OUT),
        (kinds, lengths, me, *stay(rows), qkv, stay(*weights.arrays)),
        20,
        10,
    )


def ffn_forward(order, me, rows, weights, norms):
    slots = rows.shape[0]
    return order.call(
        bound(ffn_forward_kernel, weights),
        "ffn_forward",
        slots,
        [scalars(), per_slot(SLOT, D), held(weights), whole_block(*norms.shape)],
        [slot_array(slots, D, BF, True), slot_array(slots, FF, BF, True), slot_array(slots, FF, BF, True)],
        weight_scratch(FFN_ROWS),
        (me, *stay(rows), stay(*weights.arrays), norms),
        24,
        16,
    )


def ffn_backward(order, me, grad_out, rows, active, slope, weights, norms, parted):
    slots = rows.shape[0]
    return order.call(
        bound(ffn_backward_kernel, weights),
        "ffn_backward",
        slots,
        [
            scalars(),
            per_slot(SLOT, D),
            per_slot(SLOT, D),
            per_slot(SLOT, FF),
            per_slot(SLOT, FF),
            held(weights),
            whole_block(*norms.shape),
        ],
        [slot_array(slots, D, F32), grad_group(FFN_ROWS, parted), NORM_GRADS],
        weight_scratch(FFN_ROWS) + [pltpu.VMEM((2, BLOCKS, D, D), F32)],
        (me, *stay(grad_out, rows, active, slope), stay(*weights.arrays), norms),
        38,
        22,
    )


def attend_backward(order, kinds, lengths, me, grad_out, q, kv, kept, weights, causal, start, key_at, name):
    slots = grad_out.shape[0]
    return order.call(
        bound(attend_back_kernel, weights, causal=causal, start=start, key_at=key_at),
        name,
        slots,
        [scalars(), scalars(), scalars(), per_slot(SLOT, D)]
        + [per_slot(SLOT, part.shape[-1]) for part in (q, kv)]
        + [per_slot(SLOT, D), per_slot(SLOT, D), per_slot(SLOT, 128), held(weights)],
        [slot_array(slots, 3 * D, BF)],
        weight_scratch(16) + [pltpu.VMEM((1, SLOT, D), BF)],
        (kinds, lengths, me, grad_out, *stay(q, kv, *kept), stay(*weights.arrays)),
        26,
        16,
    )[0]


def upper(order, kinds, lengths, me, rows, memory, enc_cotangent, dec_cotangent, w_cross, w_ff, norms, parted):
    slots = rows.shape[0]
    return order.call(
        functools.partial(
            upper_kernel, cross_place=w_cross.place, cross_half=w_cross.half, ff_place=w_ff.place, ff_half=w_ff.half
        ),
        "upper_decoder",
        slots,
        [scalars(), scalars(), scalars()]
        + [per_slot(SLOT, D)] * 4
        + [held(w_cross), held(w_ff), whole_block(*norms.shape)],
        [
            slot_array(slots, D, BF, True),
            slot_array(slots, D, F32),
            slot_array(slots, D, F32, True),
            grad_group(FFN_ROWS, parted),
            grad_group(CROSS_ROWS, parted),
            NORM_GRADS,
        ],
        weight_scratch(CROSS_ROWS)
        + weight_scratch(FFN_ROWS)
        + [
            pltpu.VMEM((1, SLOT, 3 * D), BF),
            pltpu.VMEM((SLOT, D), F32),
            pltpu.VMEM((1, SLOT, D), BF),
            pltpu.VMEM((3, SLOT, D), BF),
            pltpu.VMEM((BLOCKS, SLOT, D), BF),
            pltpu.VMEM((BLOCKS, SLOT, D), BF),
            pltpu.VMEM((SLOT, D), F32),
            pltpu.VMEM((2, BLOCKS, D, D), F32),
            pltpu.VMEM((4, D, D), F32),
        ],
        (
            kinds,
            lengths,
            me,
            *stay(rows, memory, enc_cotangent, dec_cotangent),
            stay(*w_cross.arrays),
            stay(*w_ff.arrays),
            norms,
        ),
        UPPER_MB,
        60,
    )


def self_weights(order, me, grad_out, rows, context, proj, norms, parted, name):
    slots = rows.shape[0]
    return order.call(
        self_weight_kernel,
        name,
        slots,
        [scalars()] + [per_slot(SLOT, D)] * 3 + [per_slot(SLOT, 3 * D), whole_block(*norms.shape)],
        [grad_group(SELF_ROWS, parted)],
        [pltpu.VMEM((4, D, D), F32)],
        (me, grad_out, *stay(rows, context), proj, norms),
        20,
        8,
    )[0]


def self_rows(order, me, grad_out, rows, proj, weights, norms, name):
    slots = rows.shape[0]
    return order.call(
        bound(self_rows_kernel, weights),
        name,
        slots,
        [scalars(), per_slot(SLOT, D), per_slot(SLOT, D), per_slot(SLOT, 3 * D), held(weights), whole_block(*norms.shape)],
        [slot_array(slots, D, BF), NORM_GRADS],
        weight_scratch(SELF_OUT - SELF_IN),
        (me, *stay(grad_out, rows), proj, stay(*weights.arrays), norms),
        16,
        7,
    )


def axis_sizes(mesh):
    dp, fsdp = mesh.shape["dp"], mesh.shape["fsdp"]
    core = 2 if fsdp % 2 == 0 else 1
    side = math.isqrt(dp)
    first, second = (side, side) if side * side == dp else (dp, 1)
    return (first, second, fsdp // core, core)


AXES = ("dp", "fsdp")
CUBE = (2, 2, 4, 2)
A_BIT, B_BIT, HIGH_BIT, LOW_BIT, CORE_BIT = 16, 8, 4, 2, 1


def swapped(values, bit):
    return lax.ppermute(values, AXES, [(device, device ^ bit) for device in range(SHARDS)])


def moved(values, sizes, axis, shift):
    stride = math.prod(sizes[axis + 1 :])
    pairs = []
    for device in range(math.prod(sizes)):
        place = device // stride % sizes[axis]
        pairs.append((device, device + ((place + shift) % sizes[axis] - place) * stride))
    return lax.ppermute(values, AXES, pairs)


def sum_everywhere(values, sizes):
    for axis in (3, 1, 0, 2):
        total = values
        for shift in range(1, sizes[axis]):
            total = total + moved(values, sizes, axis, shift)
        values = total
    return values


def packed(flat, rows, columns, devices):
    part = flat.reshape(rows // devices, columns // D, D)
    return jnp.swapaxes(part, 0, 1).reshape(-1, D)


def unpacked(part, rows, columns, devices):
    return jnp.swapaxes(part.reshape(columns // D, rows // devices, D), 0, 1).reshape(-1)


SELF_SHAPES = ((D, 3 * D), (D, D))
FFN_SHAPES = ((D, FF), (FF, D))
CROSS_SHAPES = ((D, D), (D, 2 * D), (D, D))


def rows_of(shapes, devices=SHARDS):
    return sum(rows * columns for rows, columns in shapes) // D // devices


def rows_in(groups):
    return sum(rows_of(shapes) for shapes in groups)


def join_copy_kernel(me_ref, sources, results, sems, *, plan):
    copies = []
    for result, (source, _, bit, axis) in zip(results, plan):
        for other, ref in enumerate(sources[source]):
            place = me_ref[bit] if other == 0 else 1 - me_ref[bit]
            target = result.at[place] if axis == 0 else result.at[:, place]
            copies.append(pltpu.make_async_copy(ref, target, sems.at[len(copies)]))
    for copy in copies:
        copy.start()
    for copy in copies:
        copy.wait()


def join_kernel(me_ref, sources, results, *, plan):
    for result, (source, rows, bit, axis) in zip(results, plan):
        for other, ref in enumerate(sources[source]):
            place = me_ref[bit] if other == 0 else 1 - me_ref[bit]
            if axis == 0:
                result[place] = ref[...]
            else:
                for lead in range(2):
                    result[lead, place] = ref[lead] if rows is None else ref[lead, rows]


def join(order, me, name, sources, plan, to_hbm=False):
    outs = []
    for source, rows, _, axis in plan:
        shape = sources[source][0].shape
        count = shape[-2] if rows is None else rows.stop - rows.start
        shape = (2, *shape[:-2], count, D) if axis == 0 else (shape[0], 2, *shape[1:-2], count, D)
        outs.append((in_place(), shape, BF, "hbm") if to_hbm else (in_vmem(), shape, BF))
    return order.call(
        functools.partial(join_copy_kernel if to_hbm else join_kernel, plan=plan),
        name,
        1,
        [scalars(), [(in_vmem(), in_vmem())] * len(sources)],
        [tuple(outs)],
        [pltpu.SemaphoreType.DMA((2 * len(plan),))] if to_hbm else [],
        (me, sources),
        20,
        1,
    )[0]


def pack_kernel(me_ref, flats, extra, out_ref, *scratch, plan):
    for flat, wide_ref, (rows, blocks, places) in zip(flats, scratch, plan):
        wide_ref[...] = flat[...].astype(F32)
        for block, place in enumerate(places):
            for chunk in range(4):
                part = wide_ref[pl.ds(4 * block + chunk, rows, stride=4 * blocks), :]
                out_ref[place : place + rows, 128 * chunk : 128 * chunk + 128] = part.astype(BF)
    if extra:
        place = out_ref.shape[0] - 16
        out_ref[place:, :] = jnp.broadcast_to(extra[0][...], (16, D))


def pack_groups(order, me, name, groups, extra):
    counts = [rows_of([shape for _, shape in group]) for group in groups]
    total = sum(counts)
    flats, plan, scratch, before = [], [], [], 0
    for group, count in zip(groups, counts):
        first = 0
        for flat, (rows, columns) in group:
            rows, blocks = rows // SHARDS, columns // D
            places = []
            for block in range(blocks):
                at = first + block * rows
                places.append(before + at if at < count // 2 else total // 2 + before + at - count // 2)
            first += rows * blocks
            flats.append(flat.reshape(-1, 128))
            plan.append((rows, blocks, tuple(places)))
            scratch.append(pltpu.VMEM((rows * blocks * 4, 128), F32))
        before += count // 2
    rows = total + (0 if extra is None else 16)
    return order.call(
        functools.partial(pack_kernel, plan=plan),
        name + "_pack",
        1,
        [scalars(), tuple(in_vmem() for _ in flats), () if extra is None else (in_vmem(),)],
        [(in_vmem(), (rows, D), BF)],
        scratch,
        (me, tuple(flats), () if extra is None else (extra,)),
        20,
        1,
    )[0]


def gather_cube(order, me, name, groups, spans, extra, results):
    halves_of = [rows_of([shape for _, shape in group]) // 2 for group in groups]
    count = sum(halves_of)
    values = pack_groups(order, me, name, groups, extra)
    total = values.shape[0]
    yield
    got = swapped(values, HIGH_BIT)
    yield
    (values,) = join(order, me, name + "_join_1", [(values, got)], [(0, None, 2, 0)])
    got = swapped(values, LOW_BIT)
    yield
    plan, members, place = [], [], 0
    for span in spans:
        members.append([halves_of.pop(0) for _ in range(span)])
        end = place + sum(members[-1])
        plan.append((0, slice(place, end), 3, 1))
        plan.append((0, slice(count + place, total if end == count else count + end), 3, 1))
        place = end
    parts = join(order, me, name + "_join_2", [(values, got)], plan)
    for number, held_halves in enumerate(members):
        last = extra is not None and number == len(members) - 1
        results.append(
            Exchange(
                lambda kept, number=number, held_halves=held_halves, last=last: gather_rest(
                    order, me, f"{name}_{number}", parts[2 * number], parts[2 * number + 1], held_halves, last, kept
                )
            )
        )
    yield


def gather_rest(order, me, name, one, two, halves_of, extra, results):
    got = swapped(one, B_BIT), swapped(two, A_BIT)
    yield
    one, two = join(
        order, me, name + "_join_3", [(one, got[0]), (two, got[1])], [(0, None, 1, 0), (1, None, 0, 0)]
    )
    got = swapped(one, A_BIT), swapped(two, B_BIT)
    yield
    one, two = join(
        order, me, name + "_join_4", [(one, got[0]), (two, got[1])], [(0, None, 0, 0), (1, None, 1, 1)], True
    )
    got = swapped(one, CORE_BIT), swapped(two, CORE_BIT)
    arrays = tuple(part.reshape(SHARDS // 2, -1, D) for part in (one, got[0], two, got[1]))
    place = 0
    for half in halves_of:
        results.append(Weights(arrays, place, half))
        place += half
    if extra:
        own, other = arrays[2][:, place], arrays[3][:, place]
        lines = jnp.where(me[4] == 0, jnp.stack([own, other], 1), jnp.stack([other, own], 1))
        results.append(lines.reshape(SHARDS, D))
    yield


def gather_plain(groups, spans, extra, devices, results):
    if devices == SHARDS:
        parts = [packed(flat, *shape, SHARDS) for group in groups for flat, shape in group]
        whole = lax.all_gather(jnp.concatenate(parts, 0), AXES, axis=0)
    else:
        parts = []
        for flat, shape in [pair for group in groups for pair in group]:
            full = lax.all_gather(flat, AXES, axis=0, tiled=True)
            full = full.reshape(SHARDS, shape[0] // SHARDS, shape[1] // D, D)
            parts.append(jnp.swapaxes(full, 1, 2).reshape(SHARDS, -1, D))
        whole = jnp.concatenate(parts, 1)
    whole = whole.reshape(SHARDS // 2, 2, -1, D)
    place, left = 0, list(groups)
    for span in spans:
        results.append(Exchange())
        for _ in range(span):
            count = rows_of([shape for _, shape in left.pop(0)])
            results[-1].results.append(Weights((whole,), place, count // 2))
            place += count
    if extra is not None:
        results[-1].results.append(lax.all_gather(extra[0], AXES, axis=0))


def add_kernel(me_ref, parts, result):
    result[...] = functools.reduce(jnp.add, [part[...] for part in parts])


def sum_cube(order, me, values, results):
    for bits in ((CORE_BIT,), (B_BIT, A_BIT, A_BIT | B_BIT), (LOW_BIT, HIGH_BIT, HIGH_BIT | LOW_BIT)):
        parts = (values, *(swapped(values, bit) for bit in bits))
        yield
        values = order.call(
            add_kernel,
            "small_sum",
            1,
            [scalars(), tuple(in_vmem() for _ in parts)],
            [(in_vmem(), values.shape, F32)],
            [],
            (me, parts),
            8,
            1,
        )[0]
    results.append(values)
    yield


def first_sum_kernel(me_ref, keeps, gots, send_one, keep_one, send_two, keep_two):
    a, b = me_ref[0], me_ref[1]
    place = 0
    for keep, got in zip(keeps, gots):
        half = keep.shape[3] // 2
        low, high, here = slice(0, half), slice(half, 2 * half), slice(place, place + half)
        for other in range(2):
            for ref, pick in ((send_one, 1 - b), (keep_one, b)):
                ref[other, :, here] = keep[other, pick, :, low] + got[other, pick, :, low]
            for ref, pick in ((send_two, 1 - a), (keep_two, a)):
                ref[other, :, here] = keep[pick, other, :, high] + got[pick, other, :, high]
        place += half


def second_sum_kernel(me_ref, keep_one, got_one, keep_two, got_two, send_a, kept_a, send_b, kept_b):
    a, b = me_ref[0], me_ref[1]
    for ref, pick in ((send_a, 1 - a), (kept_a, a)):
        ref[...] = keep_one[pick] + got_one[pick]
    for ref, pick in ((send_b, 1 - b), (kept_b, b)):
        ref[...] = keep_two[pick] + got_two[pick]


def third_sum_kernel(me_ref, keep_one, got_one, keep_two, got_two, send, keep):
    z = me_ref[3]
    half = keep_one.shape[2]
    for high in range(2):
        for ref, pick in ((send, 1 - z), (keep, z)):
            ref[high, :half] = keep_one[high, pick] + got_one[high, pick]
            ref[high, half:] = keep_two[high, pick] + got_two[high, pick]


def fourth_sum_kernel(me_ref, keep, got, send, kept):
    z = me_ref[2]
    for ref, pick in ((send, 1 - z), (kept, z)):
        ref[...] = keep[pick] + got[pick]


def scatter_cube(order, me, name, groups, results):
    got = [swapped(pair[1], CORE_BIT) for pair, _ in groups]
    yield
    keeps = tuple(pair[0].reshape(2, 2, 4, -1, D) for pair, _ in groups)
    got = tuple(part.reshape(2, 2, 4, -1, D) for part in got)
    half = sum(rows_of(shapes) for _, shapes in groups) // 2

    def call(kernel, number, shapes, *args):
        ins = [tuple(in_vmem() for _ in arg) if isinstance(arg, tuple) else in_vmem() for arg in args]
        outs = [(in_vmem(), shape, BF) for shape in shapes]
        return order.call(kernel, f"{name}_sum_{number}", 1, [scalars()] + ins, outs, [], (me, *args), 20, 1)

    send_one, keep_one, send_two, keep_two = call(first_sum_kernel, 1, [(2, 4, half, D)] * 4, keeps, got)
    got = swapped(send_one, B_BIT), swapped(send_two, A_BIT)
    yield
    send_one, keep_one, send_two, keep_two = call(
        second_sum_kernel, 2, [(4, half, D)] * 4, keep_one, got[0], keep_two, got[1]
    )
    got = swapped(send_one, A_BIT), swapped(send_two, B_BIT)
    yield
    views = [part.reshape(2, 2, half, D) for part in (keep_one, got[0], keep_two, got[1])]
    send, keep = call(third_sum_kernel, 3, [(2, 2 * half, D)] * 2, *views)
    got = swapped(send, LOW_BIT)
    yield
    send, keep = call(fourth_sum_kernel, 4, [(2 * half, D)] * 2, keep, got)
    got = swapped(send, HIGH_BIT)
    yield
    plan, outs, place = [], [], 0
    for _, shapes in groups:
        count, first = rows_of(shapes), 0
        for rows, columns in shapes:
            rows, blocks = rows // SHARDS, columns // D
            places = []
            for block in range(blocks):
                at = first + block * rows
                places.append(place + at if at < count // 2 else half + place + at - count // 2)
            first += rows * blocks
            plan.append((rows, blocks, tuple(places)))
            shape = (rows * blocks * 4, 128)
            outs.append((whole_block(*shape), shape, F32))
        place += count // 2
    flat = order.call(
        functools.partial(finish_kernel, plan=plan),
        name + "_finish",
        1,
        [scalars(), in_vmem(), in_vmem()],
        [tuple(outs)],
        [],
        (me, keep, got),
        20,
        1,
    )[0]
    results.extend(part.reshape(-1) for part in flat)
    yield


def finish_kernel(me_ref, keep, got, outs, *, plan):
    for out, (rows, blocks, places) in zip(outs, plan):
        for block, place in enumerate(places):
            part = keep[place : place + rows, :].astype(F32) + got[place : place + rows, :].astype(F32)
            for chunk in range(4):
                out[pl.ds(4 * block + chunk, rows, stride=4 * blocks), :] = part[:, 128 * chunk : 128 * chunk + 128]


def unpack_group(rows, shapes):
    results, first = [], 0
    for shape in shapes:
        count = rows_of((shape,))
        results.append(unpacked(rows[first : first + count], *shape, SHARDS))
        first += count
    return results


def scatter_plain(grads, shapes, devices):
    if devices == SHARDS:
        own = lax.psum_scatter(grads.reshape(-1, D), AXES, scatter_dimension=0, tiled=True)
        return unpack_group(own.astype(F32), shapes)
    grads = grads.reshape(SHARDS, -1, D)
    results, first = [], 0
    for rows, columns in shapes:
        count = rows_of(((rows, columns),))
        part = grads[:, first : first + count].reshape(SHARDS, columns // D, rows // SHARDS, D)
        flat = jnp.swapaxes(part, 1, 2).reshape(devices, -1)
        results.append(lax.psum_scatter(flat, AXES, scatter_dimension=0, tiled=True).reshape(-1).astype(F32))
        first += count
    return results


class Exchange:
    def __init__(self, steps=None):
        self.results = []
        self.steps = None if steps is None else steps(self.results)

    def part(self, number):
        return self.results[number]

    def go(self, count=1):
        if self.steps is not None:
            for _ in range(count):
                next(self.steps)


def count_live(kinds, lengths, ids):
    positions = jnp.arange(SLOT, dtype=jnp.int32)[None, :]
    size = jnp.left_shift(jnp.int32(SLOT // 4), kinds)[:, None]
    sequence = positions // size
    limit = jnp.zeros_like(sequence)
    for entry in range(4):
        limit = jnp.where(sequence == entry, lengths[:, entry : entry + 1], limit)
    live = positions % size < limit
    hits = (ids.reshape(-1)[:, None] == jnp.arange(VOCAB, dtype=jnp.int32)[None, :]) & live.reshape(-1)[:, None]
    return jnp.sum(hits.astype(F32), 0)


def local(
    sizes,
    enc_in,
    dec_in,
    bucket,
    enc_lengths,
    dec_lengths,
    pred_ids,
    running_counts,
    enc_attn_in,
    enc_attn_out,
    enc_ff_in,
    enc_ff_out,
    enc_norms,
    dec_self_in,
    dec_self_out,
    dec_cross_q,
    dec_cross_kv,
    dec_cross_out,
    dec_ff_in,
    dec_ff_out,
    dec_norms,
    enc_cotangent,
    dec_cotangent,
):
    devices = math.prod(sizes)
    cube = sizes == CUBE
    index = lax.axis_index("dp") * lax.axis_size("fsdp") + lax.axis_index("fsdp")
    if cube:
        me = jnp.stack([index >> 4 & 1, index >> 3 & 1, index >> 2 & 1, index >> 1 & 1, index & 1]).astype(jnp.int32)
    else:
        me = jnp.zeros((5,), jnp.int32)

    order = Order()

    def gather(name, groups, spans, extra=None):
        if cube:
            return Exchange(lambda results: gather_cube(order, me, name, groups, spans, extra, results))
        exchange = Exchange()
        gather_plain(groups, spans, extra, devices, exchange.results)
        return exchange

    def scatter(name, *groups):
        if cube and all(len(grads) == 2 for grads, _ in groups):
            return Exchange(lambda results: scatter_cube(order, me, name, groups, results))
        exchange = Exchange()
        for (grads,), shapes in groups:
            exchange.results.extend(scatter_plain(grads, shapes, devices))
        return exchange

    enc_count, dec_count = enc_norms.shape[0], dec_norms.shape[0]
    both = jnp.concatenate([enc_norms, dec_norms])
    norm_part = jnp.pad(both[None, :], ((0, 0), (0, D - both.shape[0])))
    enc_self_group = list(zip((enc_attn_in, enc_attn_out), SELF_SHAPES))
    dec_self_group = list(zip((dec_self_in, dec_self_out), SELF_SHAPES))
    enc_ff_group = list(zip((enc_ff_in, enc_ff_out), FFN_SHAPES))
    cross_group = list(zip((dec_cross_q, dec_cross_kv, dec_cross_out), CROSS_SHAPES))
    dec_ff_group = list(zip((dec_ff_in, dec_ff_out), FFN_SHAPES))
    first = gather("self", [dec_self_group, enc_self_group], [1, 1], norm_part)
    rest = gather("rest", [enc_ff_group, cross_group, dec_ff_group], [1, 2])
    first.go(2)
    rest.go()
    first.go(2)
    dec_chain, enc_chain = first.part(0), first.part(1)
    enc_chain.go()
    dec_chain.go()
    rest.go()
    enc_chain.go()
    dec_chain.go()
    enc_chain.go()
    rest.go()
    dec_chain.go()
    enc_self_w, norm_lines = enc_chain.results
    enc_norm = norm_lines[:, :enc_count].reshape(4, D).astype(F32)
    dec_norm = norm_lines[:, enc_count : enc_count + dec_count].reshape(6, D).astype(F32)

    enc_qkv = project(order, me, enc_in, enc_self_w, enc_norm, "enc_project")
    attended, *enc_kept = self_attend(order, bucket, enc_lengths, me, enc_in, enc_qkv, enc_self_w, False, "enc_attend")
    rest.go()
    ffn_chain, late_chain = rest.part(0), rest.part(1)
    ffn_chain.go()
    late_chain.go()
    (dec_self_w,) = dec_chain.results
    dec_qkv = project(order, me, dec_in, dec_self_w, dec_norm, "dec_project")
    ffn_chain.go()
    first_out, *dec_kept = self_attend(order, bucket, dec_lengths, me, dec_in, dec_qkv, dec_self_w, True, "dec_attend")
    late_chain.go()
    ffn_chain.go()
    (enc_ff_w,) = ffn_chain.results
    memory, active, slope = ffn_forward(order, me, attended, enc_ff_w, enc_norm)
    late_chain.go()
    cross_w, dec_ff_w = late_chain.results
    decoded, grad_first, grad_memory, dec_ff_grads, cross_grads, upper_norm_g = upper(
        order,
        bucket,
        enc_lengths,
        me,
        first_out,
        memory,
        enc_cotangent,
        dec_cotangent,
        cross_w,
        dec_ff_w,
        dec_norm,
        cube,
    )
    fifth = scatter("dec", (dec_ff_grads, FFN_SHAPES), (cross_grads, CROSS_SHAPES))
    fifth.go()
    grad_attended, enc_ff_grads, enc_ffn_norm_g = ffn_backward(
        order, me, grad_memory, attended, active, slope, enc_ff_w, enc_norm, cube
    )
    fifth.go()
    enc_proj = attend_backward(
        order,
        bucket,
        enc_lengths,
        me,
        grad_attended,
        enc_qkv,
        enc_qkv,
        enc_kept,
        enc_self_w,
        False,
        SELF_OUT,
        D,
        "enc_attend_back",
    )
    fifth.go()
    enc_self_grads = self_weights(
        order, me, grad_attended, enc_in, enc_kept[0], enc_proj, enc_norm, cube, "enc_self_weights"
    )
    sixth = scatter("enc", (enc_ff_grads, FFN_SHAPES), (enc_self_grads, SELF_SHAPES))
    sixth.go()
    dec_proj = attend_backward(
        order,
        bucket,
        dec_lengths,
        me,
        grad_first,
        dec_qkv,
        dec_qkv,
        dec_kept,
        dec_self_w,
        True,
        SELF_OUT,
        D,
        "dec_attend_back",
    )
    fifth.go()
    sixth.go()
    dec_self_grads = self_weights(
        order, me, grad_first, dec_in, dec_kept[0], dec_proj, dec_norm, cube, "dec_self_weights"
    )
    seventh = scatter("self", (dec_self_grads, SELF_SHAPES))
    seventh.go()
    fifth.go()
    grad_enc_in, enc_self_norm_g = self_rows(
        order, me, grad_attended, enc_in, enc_proj, enc_self_w, enc_norm, "enc_self_rows"
    )
    seventh.go()
    sixth.go()
    grad_dec_in, dec_self_norm_g = self_rows(order, me, grad_first, dec_in, dec_proj, dec_self_w, dec_norm, "dec_self_rows")
    counted = jnp.pad(count_live(bucket, dec_lengths, pred_ids), (0, 2 * D - VOCAB)).reshape(2, D)
    small = jnp.concatenate(
        [enc_self_norm_g[:2], enc_ffn_norm_g[:2], dec_self_norm_g[:2], upper_norm_g[:4], counted, jnp.zeros((4, D), F32)],
        0,
    )
    if cube:
        summed = Exchange(lambda results: sum_cube(order, me, small, results))
        summed.go()
        seventh.go()
        sixth.go()
        summed.go()
        seventh.go()
        sixth.go()
        summed.go()
        seventh.go()
        fifth.go()
        sixth.go()
        summed.go()
        seventh.go()
        (small,) = summed.results
    else:
        small = sum_everywhere(small, sizes)
    dec_ff_in_g, dec_ff_out_g, cross_q_g, cross_kv_g, cross_out_g = fifth.results
    enc_ff_in_g, enc_ff_out_g, enc_attn_in_g, enc_attn_out_g = sixth.results
    dec_self_in_g, dec_self_out_g = seventh.results

    enc_norm_own = lax.dynamic_slice(small[:4].reshape(-1), (index * enc_count,), (enc_count,))
    dec_norm_own = lax.dynamic_slice(small[4:10].reshape(-1), (index * dec_count,), (dec_count,))
    counts = running_counts + small[10:12].reshape(-1)[:VOCAB].astype(jnp.int32)
    return (
        memory,
        decoded,
        grad_enc_in,
        grad_dec_in,
        enc_attn_in_g,
        enc_attn_out_g,
        enc_ff_in_g,
        enc_ff_out_g,
        enc_norm_own,
        dec_self_in_g,
        dec_self_out_g,
        cross_q_g,
        cross_kv_g,
        cross_out_g,
        dec_ff_in_g,
        dec_ff_out_g,
        dec_norm_own,
        counts,
    )


def solution(mesh):
    rows = P(AXES, None, None)
    pair = P(AXES, None)
    flat = P(AXES)
    return jax.shard_map(
        functools.partial(local, axis_sizes(mesh)),
        mesh=mesh,
        in_specs=(rows, rows, flat, pair, pair, pair, P()) + (flat,) * 13 + (rows, rows),
        out_specs=(rows,) * 4 + (flat,) * 13 + (P(),),
        check_vma=False,
    )
```

time: 511 us -> 371 us (0.73); the launches traced: 504 us -> 370 us
  waiting for transfers between devices: 130 us -> 61.7 us
  Pallas kernels: 273 us -> 231 us
  local copies, waits for them, and re-layouts: 37.6 us -> 15.4 us
  other arithmetic: 9.79 us -> 2.24 us
  starting transfers between devices: 51.9 us -> 57.5 us
    ppermute x52 -> x58, waiting for transfers between devices: 130 us -> 61.7 us  [swapped(): lax.ppermute(values, AXES, [(device, device ^ bit) for device in range(SH...]
    pallas_call x28 -> x45, Pallas kernels: 273 us -> 231 us  [call(): pl.pallas_call(body, name=name, grid=(steps,), in_specs=[tuple((in_place(...]
    select_n x34 -> x1, other arithmetic: 6.36 us -> 0.16 us  [gather_rest(): jnp.where(me[4] == 0, jnp.stack([own, other], 1), jnp.stack([other, own],...]
    ppermute x52 -> x58, starting transfers between devices: 51.9 us -> 57.5 us  [swapped(): lax.ppermute(values, AXES, [(device, device ^ bit) for device in range(SH...]
    unnamed x100 -> x114, local copies, waits for them, and re-layouts: 15.2 us -> 10.6 us
  transfers between devices with their start and end apart: 52 -> 58, of which waited for: 16 -> 24; matrix products, arithmetic and copies ran while one was open for 6% -> 2% of each run, Pallas kernels for 38% -> 40%
where the time goes in v2:
time: 371 us; the launch traced here: 370 us
  Pallas kernels  231 us (62%)
  waiting for transfers between devices  61.7 us (17%)
  starting transfers between devices  57.5 us (15%)
  local copies, waits for them, and re-layouts  15.4 us (4%)
    pallas_call x45, Pallas kernels, call(): pl.pallas_call(body, name=name, grid=(steps,), in_specs=[tuple((in_place(...  231 us
    ppermute x58, waiting for transfers between devices, swapped(): lax.ppermute(values, AXES, [(device, device ^ bit) for device in range(SH...  61.7 us
    ppermute x58, starting transfers between devices, swapped(): lax.ppermute(values, AXES, [(device, device ^ bit) for device in range(SH...  57.5 us
    unnamed x114, local copies, waits for them, and re-layouts  10.6 us
  transfers between devices with their start and end apart: 58, of which 24 were waited for; matrix products, arithmetic and copies ran while one was open for 2% of the time, Pallas kernels for 40%

profile of v2, /device:TPU:0, one launch (start us, length us, event | category | flops | bytes accessed | tf_op | source)
XLA Modules:
  0.0 369.7 jit_solution(10924166336338780652)
XLA Ops:
  5.2 4.1 %collective-permute-start = (bf16[144,512]{1,0:T(8,128)(2,1)S(1)}, bf16[144,512]{1,0:T(8,128)(2,1)S(1)}, u32[]{:S(2)}, u32[]{:S(2)}) collective-permute-start(bf16[144,512]{1,0:T(8,128)(2,1)S(1)} %get-tuple-element.177.refs_1__0__0_), channel_id=1, source_target_pairs={{0,4},{1,5},{2,6},{3,7},{4,0},{5,1},{6,2},{7,3},{8,12},{9,13},{10,... | collective-permute-start | bytes 442376 | tf_op jit(solution)/shard_map/ppermute | solution.py:937
  10.1 6.2 %collective-permute-done.refs_1__0__1_ = bf16[144,512]{1,0:T(8,128)(2,1)S(1)} collective-permute-done((bf16[144,512]{1,0:T(8,128)(2,1)S(1)}, bf16[144,512]{1,0:T(8,128)(2,1)S(1)}, u32[]{:S(2)}, u32[]{:S(2)}) %collective-permute-start) | collective-permute-done | bytes 147488 | tf_op jit(solution)/shard_map/ppermute | solution.py:937
  17.7 7.5 %collective-permute-done.1.refs_1__0__1_ = bf16[2,144,512]{2,1,0:T(8,128)(2,1)S(1)} collective-permute-done((bf16[2,144,512]{2,1,0:T(8,128)(2,1)S(1)}, bf16[2,144,512]{2,1,0:T(8,128)(2,1)S(1)}, u32[]{:S(2)}, u32[]{:S(2)}) %collective-permute-start.1) | collective-permute-done | bytes 294944 | tf_op jit(solution)/shard_map/ppermute | solution.py:937
  29.8 2.2 collective-permute-done.2.refs_1__0__1_
  34.8 4.0 %collective-permute-start.8 = (bf16[320,512]{1,0:T(8,128)(2,1)S(1)}, bf16[320,512]{1,0:T(8,128)(2,1)S(1)}, u32[]{:S(2)}, u32[]{:S(2)}) collective-permute-start(bf16[320,512]{1,0:T(8,128)(2,1)S(1)} %get-tuple-element.190.refs_1__0__0_), channel_id=1, source_target_pairs={{0,4},{1,5},{2,6},{3,7},{4,0},{5,1},{6,2},{7,3},{8,12},{9,13},{10,... | collective-permute-start | bytes 983048 | tf_op jit(solution)/shard_map/ppermute | solution.py:937
  40.9 4.3 %collective-permute-done.6.refs_1__0__1_ = bf16[2,2,2,32,512]{4,3,2,1,0:T(8,128)(2,1)S(1)} collective-permute-done((bf16[2,2,2,32,512]{4,3,2,1,0:T(8,128)(2,1)S(1)}, bf16[2,2,2,32,512]{4,3,2,1,0:T(8,128)(2,1)S(1)}, u32[]{:S(2)}, u32[]{:S(2)}) %collective-permute-start.6) | collective-permute-done | bytes 262176 | tf_op jit(solution)/shard_map/ppermute | solution.py:937
  45.1 1.7 self_1_join_4.1
  52.1 3.5 collective-permute-done.10.refs_1__1__1_
  58.9 4.9 %enc_project.1 = (bf16[2,512,1536]{2,1,0:T(8,128)(2,1)S(1)}, f32[8,128]{1,0:T(8,128)S(1)}) custom-call(f32[8,128]{1,0:T(8,128)S(1)} %get-tuple-element.194.before_0_, s32[5]{0:T(128)S(1)} %stack.29.refs_0_.refs_2_, bf16[2,512,512]{2,1,0:T(8,128)(2,1)} %refs_2_.6, bf16[16,32,512]{2,1,0:T(8,128)(2,1)} %bitcast.175, ...), custom_call_target="tpu_custom_call" | custom-call | flops 17250000896 | bytes 65536 | tf_op jit(solution)/shard_map/enc_project/pallas_call | solution.py:716
  63.9 10.6 %enc_attend.1 = (f32[2,512,512]{2,1,0:T(8,128)}, bf16[2,512,512]{2,1,0:T(8,128)(2,1)}, bf16[2,512,512]{2,1,0:T(8,128)(2,1)}, bf16[2,512,128]{2,1,0:T(8,128)(2,1)}, f32[8,128]{1,0:T(8,128)S(1)}) custom-call(f32[8,128]{1,0:T(8,128)S(1)} %get-tuple-element.197.before_0_, s32[2]{0:T(128)S(1)} %copy-done.4, s32[2,4]{1,0:T(2,128)S(1)} %copy-done.19, ...), custom_call_target="tpu_custom_call" | custom-call | flops 34500001792 | bytes 65536 | tf_op jit(solution)/shard_map/enc_attend/pallas_call | solution.py:716
  79.7 4.9 %dec_project.1 = (bf16[2,512,1536]{2,1,0:T(8,128)(2,1)S(1)}, f32[8,128]{1,0:T(8,128)S(1)}) custom-call(f32[8,128]{1,0:T(8,128)S(1)} %get-tuple-element.201.before_0_, s32[5]{0:T(128)S(1)} %stack.29.refs_0_.refs_2_, bf16[2,512,512]{2,1,0:T(8,128)(2,1)} %refs_2_.7, bf16[16,32,512]{2,1,0:T(8,128)(2,1)} %bitcast.163, bf16[16,32,512]{2,1,0:T(8,128)(2,1)} %bitcast.171, ...), custom_call_target="tpu_custom_call" | custom-call | flops 17250000896 | bytes 65536 | tf_op jit(solution)/shard_map/dec_project/pallas_call | solution.py:716
  88.8 8.5 %dec_attend.1 = (f32[2,512,512]{2,1,0:T(8,128)}, bf16[2,512,512]{2,1,0:T(8,128)(2,1)}, bf16[2,512,512]{2,1,0:T(8,128)(2,1)}, bf16[2,512,128]{2,1,0:T(8,128)(2,1)}, f32[8,128]{1,0:T(8,128)S(1)}) custom-call(f32[8,128]{1,0:T(8,128)S(1)} %get-tuple-element.207.before_0_, s32[2]{0:T(128)S(1)} %copy-done.4, s32[2,4]{1,0:T(2,128)S(1)} %copy-done, ...), custom_call_target="tpu_custom_call" | custom-call | flops 34500001792 | bytes 65536 | tf_op jit(solution)/shard_map/dec_attend/pallas_call | solution.py:716
  98.0 6.6 %collective-permute-done.20.refs_1__0__1_ = bf16[2,2,2,64,512]{4,3,2,1,0:T(8,128)(2,1)S(1)} collective-permute-done((bf16[2,2,2,64,512]{4,3,2,1,0:T(8,128)(2,1)S(1)}, bf16[2,2,2,64,512]{4,3,2,1,0:T(8,128)(2,1)S(1)}, u32[]{:S(2)}, u32[]{:S(2)}) %collective-permute-start.20) | collective-permute-done | bytes 524320 | tf_op jit(solution)/shard_map/ppermute | solution.py:937
  104.6 1.9 rest_0_join_4.1
  111.9 16.0 %ffn_forward.1 = (bf16[2,512,512]{2,1,0:T(8,128)(2,1)}, bf16[2,512,2048]{2,1,0:T(8,128)(2,1)}, bf16[2,512,2048]{2,1,0:T(8,128)(2,1)}, f32[8,128]{1,0:T(8,128)S(1)}) custom-call(f32[8,128]{1,0:T(8,128)S(1)} %get-tuple-element.215.before_0_, s32[5]{0:T(128)S(1)} %stack.29.refs_0_.refs_2_, f32[2,512,512]{2,1,0:T(8,128)} %get-tuple-element.216.refs_1_.refs_2_, ...), custom_call_target="tpu_custom_call" | custom-call | flops 55199997952 | bytes 65536 | tf_op jit(solution)/shard_map/ffn_forward/pallas_call | solution.py:716
  128.0 2.2 rest_1_join_4.1
  134.0 2.2 collective-permute-done.27
  137.4 76.7 %upper_decoder.1 = (bf16[2,512,512]{2,1,0:T(8,128)(2,1)}, f32[2,512,512]{2,1,0:T(8,128)}, f32[2,512,512]{2,1,0:T(8,128)}, bf16[16,128,512]{2,1,0:T(8,128)(2,1)},...) custom-call(f32[8,128]{1,0:T(8,128)} %copy-done.35, ...), custom_call_target="tpu_custom_call" | custom-call | flops 206999994368 | bytes 65536 | tf_op jit(solution)/shard_map/upper_decoder/pallas_call | solution.py:716
  215.4 22.6 %ffn_backward.1 = (f32[2,512,512]{2,1,0:T(8,128)S(1)}, bf16[16,128,512]{2,1,0:T(8,128)(2,1)S(1)}, bf16[16,128,512]{2,1,0:T(8,128)(2,1)}, f32[8,512]{1,0:T(8,128)S(1)}, f32[8,128]{1,0:T(8,128)S(1)}) custom-call(f32[8,128]{1,0:T(8,128)S(1)} %copy-done.36, s32[5]{0:T(128)S(1)} %copy-done.7, f32[2,512,512]{2,1,0:T(8,128)} %get-tuple-element.229.refs_1_, ...), custom_call_target="tpu_custom_call" | custom-call | flops 75900002304 | bytes 65536 | tf_op jit(solution)/shard_map/ffn_backward/pallas_call | solution.py:716
  242.5 17.1 %enc_attend_back.1 = (bf16[2,512,1536]{2,1,0:T(8,128)(2,1)S(1)}, f32[8,128]{1,0:T(8,128)S(1)}) custom-call(f32[8,128]{1,0:T(8,128)S(1)} %get-tuple-element.237.before_0_, s32[2]{0:T(128)S(1)} %copy-done.5, s32[2,4]{1,0:T(2,128)S(1)} %copy-done.20, s32[5]{0:T(128)S(1)} %copy-done.7, f32[2,512,512]{2,1,0:T(8,128)S(1)} %get-tuple-element.238.refs_3_.refs_1_, ...), custom_call_target="tpu_custom_call" | custom-call | flops 55199997952 | bytes 65536 | tf_op jit(solution)/shard_map/enc_attend_back/pallas_call | solution.py:716
  264.4 6.9 %enc_self_weights.1 = (bf16[16,64,512]{2,1,0:T(8,128)(2,1)S(1)}, bf16[16,64,512]{2,1,0:T(8,128)(2,1)S(1)}, f32[8,128]{1,0:T(8,128)S(1)}) custom-call(f32[8,128]{1,0:T(8,128)S(1)} %get-tuple-element.247.before_0_, s32[5]{0:T(128)S(1)} %copy-done.7, f32[2,512,512]{2,1,0:T(8,128)S(1)} %get-tuple-element.238.refs_3_.refs_1_, bf16[2,512,512]{2,1,0:T(8,128)(2,1)} %refs_2_.6, ...), custom_call_target="tpu_custom_call" | custom-call | flops 27599998976 | bytes 65536 | tf_op jit(solution)/shard_map/enc_self_weights/pallas_call | solution.py:716
  271.4 14.7 %dec_attend_back.1 = (bf16[2,512,1536]{2,1,0:T(8,128)(2,1)S(1)}, f32[8,128]{1,0:T(8,128)S(1)}) custom-call(f32[8,128]{1,0:T(8,128)S(1)} %get-tuple-element.249.before_0_, s32[2]{0:T(128)S(1)} %copy-done.5, s32[2,4]{1,0:T(2,128)S(1)} %copy-done.1, s32[5]{0:T(128)S(1)} %copy-done.7, f32[2,512,512]{2,1,0:T(8,128)S(1)} %copy-done.34, ...), custom_call_target="tpu_custom_call" | custom-call | flops 55199997952 | bytes 65536 | tf_op jit(solution)/shard_map/dec_attend_back/pallas_call | solution.py:716
  288.3 1.9 enc_sum_1.1
  290.2 6.7 %dec_self_weights.1 = (bf16[16,64,512]{2,1,0:T(8,128)(2,1)S(1)}, bf16[16,64,512]{2,1,0:T(8,128)(2,1)S(1)}, f32[8,128]{1,0:T(8,128)S(1)}) custom-call(f32[8,128]{1,0:T(8,128)S(1)} %get-tuple-element.264.before_0_, s32[5]{0:T(128)S(1)} %copy-done.7, f32[2,512,512]{2,1,0:T(8,128)S(1)} %copy-done.34, bf16[2,512,512]{2,1,0:T(8,128)(2,1)} %refs_2_.7, ...), custom_call_target="tpu_custom_call" | custom-call | flops 27599998976 | bytes 65536 | tf_op jit(solution)/shard_map/dec_self_weights/pallas_call | solution.py:716
  298.9 6.8 %enc_self_rows.1 = (bf16[2,512,512]{2,1,0:T(8,128)(2,1)}, f32[8,512]{1,0:T(8,128)S(1)}, f32[8,128]{1,0:T(8,128)S(1)}) custom-call(f32[8,128]{1,0:T(8,128)S(1)} %get-tuple-element.269.before_0_, s32[5]{0:T(128)S(1)} %copy-done.7, f32[2,512,512]{2,1,0:T(8,128)} %copy-done.33, bf16[2,512,512]{2,1,0:T(8,128)(2,1)} %refs_2_.6, ...), custom_call_target="tpu_custom_call" | custom-call | flops 24149999616 | bytes 65536 | tf_op jit(solution)/shard_map/enc_self_rows/pallas_call | solution.py:716
  305.7 2.1 collective-permute-start.52
  310.4 7.1 %collective-permute-done.38.refs_2_ = bf16[2,4,96,512]{3,2,1,0:T(8,128)(2,1)S(1)} collective-permute-done((bf16[2,4,96,512]{3,2,1,0:T(8,128)(2,1)S(1)}, bf16[2,4,96,512]{3,2,1,0:T(8,128)(2,1)S(1)}, u32[]{:S(2)}, u32[]{:S(2)}) %collective-permute-start.38) | collective-permute-done | bytes 786464 | tf_op jit(solution)/shard_map/ppermute | solution.py:937
  321.7 6.7 %dec_self_rows.1 = (bf16[2,512,512]{2,1,0:T(8,128)(2,1)}, f32[8,512]{1,0:T(8,128)S(1)}, f32[8,128]{1,0:T(8,128)S(1)}) custom-call(f32[8,128]{1,0:T(8,128)S(1)} %get-tuple-element.279.before_0_, s32[5]{0:T(128)S(1)} %copy-done.7, f32[2,512,512]{2,1,0:T(8,128)} %get-tuple-element.250.refs_3_.refs_1_, bf16[2,512,512]{2,1,0:T(8,128)(2,1)} %refs_2_.7, ...), custom_call_target="tpu_custom_call" | custom-call | flops 24149999616 | bytes 65536 | tf_op jit(solution)/shard_map/dec_self_rows/pallas_call | solution.py:716
  339.7 5.2 %collective-permute-done.47.refs_2_ = bf16[2,192,512]{2,1,0:T(8,128)(2,1)S(1)} collective-permute-done((bf16[2,192,512]{2,1,0:T(8,128)(2,1)S(1)}, bf16[2,192,512]{2,1,0:T(8,128)(2,1)S(1)}, u32[]{:S(2)}, u32[]{:S(2)}) %collective-permute-start.47) | collective-permute-done | bytes 393248 | tf_op jit(solution)/shard_map/ppermute | solution.py:937
  349.4 1.7 collective-permute-start.56
  352.1 2.6 collective-permute-start.57
  356.0 8.5 %collective-permute-done.53.refs_2_ = bf16[192,512]{1,0:T(8,128)(2,1)S(1)} collective-permute-done((bf16[192,512]{1,0:T(8,128)(2,1)S(1)}, bf16[192,512]{1,0:T(8,128)(2,1)S(1)}, u32[]{:S(2)}, u32[]{:S(2)}) %collective-permute-start.53) | collective-permute-done | bytes 196640 | tf_op jit(solution)/shard_map/ppermute | solution.py:937
  (278 shorter events, 89.3 us)
Async XLA Ops:
  28.6 11.7 %collective-permute-start.4 = (bf16[2,2,32,512]{3,2,1,0:T(8,128)(2,1)S(1)}, bf16[2,2,32,512]{3,2,1,0:T(8,128)(2,1)S(1)}, u32[]{:S(2)}, u32[]{:S(2)}) collective-permute-start(bf16[2,2,32,512]{3,2,1,0:T(8,128)(2,1)S(1)} %get-tuple-element.184.refs_1__0__0_), channel_id=1, source_target_pairs={{0,8},{1,9},{2,10},{3,11},{4,12},{5,13},{6,14},{7,15},{8,0},{9,1},... | collective-permute-start | bytes 393224 | tf_op jit(solution)/shard_map/ppermute | solution.py:937
  33.3 11.8 %collective-permute-start.7 = (bf16[2,2,2,48,512]{4,3,2,1,0:T(8,128)(2,1)S(1)}, bf16[2,2,2,48,512]{4,3,2,1,0:T(8,128)(2,1)S(1)}, u32[]{:S(2)}, u32[]{:S(2)}) collective-permute-start(bf16[2,2,2,48,512]{4,3,2,1,0:T(8,128)(2,1)S(1)} %get-tuple-element.188.refs_1__1__0_), channel_id=1, source_target_pairs={{0,8},{1,9},{2,10},{3,11},{4,12},{5,13},{6,14},{7,15},{8,0},{9,1},... | collective-permute-start | bytes 1179656 | tf_op jit(solution)/shard_map/ppermute | solution.py:937
  34.8 15.7 %collective-permute-start.8 = (bf16[320,512]{1,0:T(8,128)(2,1)S(1)}, bf16[320,512]{1,0:T(8,128)(2,1)S(1)}, u32[]{:S(2)}, u32[]{:S(2)}) collective-permute-start(bf16[320,512]{1,0:T(8,128)(2,1)S(1)} %get-tuple-element.190.refs_1__0__0_), channel_id=1, source_target_pairs={{0,4},{1,5},{2,6},{3,7},{4,0},{5,1},{6,2},{7,3},{8,12},{9,13},{10,... | collective-permute-start | bytes 983048 | tf_op jit(solution)/shard_map/ppermute | solution.py:937
  51.1 23.6 %collective-permute-start.13 = (bf16[2,320,512]{2,1,0:T(8,128)(2,1)S(1)}, bf16[2,320,512]{2,1,0:T(8,128)(2,1)S(1)}, u32[]{:S(2)}, u32[]{:S(2)}) collective-permute-start(bf16[2,320,512]{2,1,0:T(8,128)(2,1)S(1)} %get-tuple-element.200.refs_1__0__0_), channel_id=1, source_target_pairs={{0,2},{1,3},{2,0},{3,1},{4,6},{5,7},{6,4},{7,5},{8,10},{9,11},{10,... | collective-permute-start | bytes 1966088 | tf_op jit(solution)/shard_map/ppermute | solution.py:937
  57.4 21.5 %collective-permute-start.14 = (bf16[2,2,2,2,32,512]{5,4,3,2,1,0:T(8,128)(2,1)}, bf16[2,2,2,2,32,512]{5,4,3,2,1,0:T(8,128)(2,1)S(1)}, u32[]{:S(2)}, u32[]{:S(2)}) collective-permute-start(bf16[2,2,2,2,32,512]{5,4,3,2,1,0:T(8,128)(2,1)} %get-tuple-element.202), channel_id=1, source_target_pairs={{0,1},{1,0},{2,3},{3,2},{4,5},{5,4},{6,7},{7,6},{8,9},{9,8},{10,11... | collective-permute-start | bytes 1572872 | tf_op jit(solution)/shard_map/ppermute | solution.py:937
  57.5 21.9 %collective-permute-start.15 = (bf16[2,2,2,2,32,512]{5,4,3,2,1,0:T(8,128)(2,1)}, bf16[2,2,2,2,32,512]{5,4,3,2,1,0:T(8,128)(2,1)}, u32[]{:S(2)}, u32[]{:S(2)}) collective-permute-start(bf16[2,2,2,2,32,512]{5,4,3,2,1,0:T(8,128)(2,1)} %get-tuple-element.203), channel_id=1, source_target_pairs={{0,1},{1,0},{2,3},{3,2},{4,5},{5,4},{6,7},{7,6},{8,9},{9,8},{10,11... | collective-permute-start | bytes 1572872 | tf_op jit(solution)/shard_map/ppermute | solution.py:937
  78.4 18.9 %collective-permute-start.18 = (bf16[2,2,96,512]{3,2,1,0:T(8,128)(2,1)S(1)}, bf16[2,2,96,512]{3,2,1,0:T(8,128)(2,1)S(1)}, u32[]{:S(2)}, u32[]{:S(2)}) collective-permute-start(bf16[2,2,96,512]{3,2,1,0:T(8,128)(2,1)S(1)} %get-tuple-element.210.refs_1__0__0_), channel_id=1, source_target_pairs={{0,8},{1,9},{2,10},{3,11},{4,12},{5,13},{6,14},{7,15},{8,0},{9,1},... | collective-permute-start | bytes 1179656 | tf_op jit(solution)/shard_map/ppermute | solution.py:937
  78.9 18.4 %collective-permute-start.19 = (bf16[2,2,96,512]{3,2,1,0:T(8,128)(2,1)S(1)}, bf16[2,2,96,512]{3,2,1,0:T(8,128)(2,1)S(1)}, u32[]{:S(2)}, u32[]{:S(2)}) collective-permute-start(bf16[2,2,96,512]{3,2,1,0:T(8,128)(2,1)S(1)} %get-tuple-element.211.refs_1__1__0_), channel_id=1, source_target_pairs={{0,16},{1,17},{2,18},{3,19},{4,20},{5,21},{6,22},{7,23},{8,24},{9,... | collective-permute-start | bytes 1179656 | tf_op jit(solution)/shard_map/ppermute | solution.py:937
  86.7 17.9 %collective-permute-start.20 = (bf16[2,2,2,64,512]{4,3,2,1,0:T(8,128)(2,1)S(1)}, bf16[2,2,2,64,512]{4,3,2,1,0:T(8,128)(2,1)S(1)}, u32[]{:S(2)}, u32[]{:S(2)}) collective-permute-start(bf16[2,2,2,64,512]{4,3,2,1,0:T(8,128)(2,1)S(1)} %get-tuple-element.213.refs_1__0__0_), channel_id=1, source_target_pairs={{0,16},{1,17},{2,18},{3,19},{4,20},{5,21},{6,22},{7,23},{8,24},{9,... | collective-permute-start | bytes 1572872 | tf_op jit(solution)/shard_map/ppermute | solution.py:937
  88.3 16.3 %collective-permute-start.21 = (bf16[2,2,2,64,512]{4,3,2,1,0:T(8,128)(2,1)S(1)}, bf16[2,2,2,64,512]{4,3,2,1,0:T(8,128)(2,1)S(1)}, u32[]{:S(2)}, u32[]{:S(2)}) collective-permute-start(bf16[2,2,2,64,512]{4,3,2,1,0:T(8,128)(2,1)S(1)} %get-tuple-element.214.refs_1__1__0_), channel_id=1, source_target_pairs={{0,8},{1,9},{2,10},{3,11},{4,12},{5,13},{6,14},{7,15},{8,0},{9,1},... | collective-permute-start | bytes 1572872 | tf_op jit(solution)/shard_map/ppermute | solution.py:937
  107.3 20.6 %collective-permute-start.24 = (bf16[2,2,2,96,512]{4,3,2,1,0:T(8,128)(2,1)S(1)}, bf16[2,2,2,96,512]{4,3,2,1,0:T(8,128)(2,1)S(1)}, u32[]{:S(2)}, u32[]{:S(2)}) collective-permute-start(bf16[2,2,2,96,512]{4,3,2,1,0:T(8,128)(2,1)S(1)} %get-tuple-element.221.refs_1__0__0_), channel_id=1, source_target_pairs={{0,16},{1,17},{2,18},{3,19},{4,20},{5,21},{6,22},{7,23},{8,24},{9,... | collective-permute-start | bytes 2359304 | tf_op jit(solution)/shard_map/ppermute | solution.py:937
  108.8 19.2 %collective-permute-start.25 = (bf16[2,2,2,96,512]{4,3,2,1,0:T(8,128)(2,1)S(1)}, bf16[2,2,2,96,512]{4,3,2,1,0:T(8,128)(2,1)S(1)}, u32[]{:S(2)}, u32[]{:S(2)}) collective-permute-start(bf16[2,2,2,96,512]{4,3,2,1,0:T(8,128)(2,1)S(1)} %get-tuple-element.222.refs_1__1__0_), channel_id=1, source_target_pairs={{0,8},{1,9},{2,10},{3,11},{4,12},{5,13},{6,14},{7,15},{8,0},{9,1},... | collective-permute-start | bytes 2359304 | tf_op jit(solution)/shard_map/ppermute | solution.py:937
  214.1 25.5 %collective-permute-start.28 = (bf16[16,128,512]{2,1,0:T(8,128)(2,1)}, bf16[16,128,512]{2,1,0:T(8,128)(2,1)S(1)}, u32[]{:S(2)}, u32[]{:S(2)}) collective-permute-start(bf16[16,128,512]{2,1,0:T(8,128)(2,1)} %get-tuple-element.235), channel_id=1, source_target_pairs={{0,1},{1,0},{2,3},{3,2},{4,5},{5,4},{6,7},{7,6},{8,9},{9,8},{10,11... | collective-permute-start | bytes 6291464 | tf_op jit(solution)/shard_map/ppermute | solution.py:937
  214.3 25.3 %collective-permute-start.29 = (bf16[16,64,512]{2,1,0:T(8,128)(2,1)}, bf16[16,64,512]{2,1,0:T(8,128)(2,1)S(1)}, u32[]{:S(2)}, u32[]{:S(2)}) collective-permute-start(bf16[16,64,512]{2,1,0:T(8,128)(2,1)} %get-tuple-element.236), channel_id=1, source_target_pairs={{0,1},{1,0},{2,3},{3,2},{4,5},{5,4},{6,7},{7,6},{8,9},{9,8},{10,11... | collective-permute-start | bytes 3145736 | tf_op jit(solution)/shard_map/ppermute | solution.py:937
  237.9 50.3 %collective-permute-start.34 = (bf16[16,128,512]{2,1,0:T(8,128)(2,1)}, bf16[16,128,512]{2,1,0:T(8,128)(2,1)}, u32[]{:S(2)}, u32[]{:S(2)}) collective-permute-start(bf16[16,128,512]{2,1,0:T(8,128)(2,1)} %get-tuple-element.262), channel_id=1, source_target_pairs={{0,1},{1,0},{2,3},{3,2},{4,5},{5,4},{6,7},{7,6},{8,9},{9,8},{10,11... | collective-permute-start | bytes 6291464 | tf_op jit(solution)/shard_map/ppermute | solution.py:937
  240.5 19.9 %collective-permute-start.30 = (bf16[2,4,96,512]{3,2,1,0:T(8,128)(2,1)S(1)}, bf16[2,4,96,512]{3,2,1,0:T(8,128)(2,1)S(1)}, u32[]{:S(2)}, u32[]{:S(2)}) collective-permute-start(bf16[2,4,96,512]{3,2,1,0:T(8,128)(2,1)S(1)} %get-tuple-element.244), channel_id=1, source_target_pairs={{0,8},{1,9},{2,10},{3,11},{4,12},{5,13},{6,14},{7,15},{8,0},{9,1},... | collective-permute-start | bytes 2359304 | tf_op jit(solution)/shard_map/ppermute | solution.py:937
  241.1 19.6 %collective-permute-start.31 = (bf16[2,4,96,512]{3,2,1,0:T(8,128)(2,1)S(1)}, bf16[2,4,96,512]{3,2,1,0:T(8,128)(2,1)S(1)}, u32[]{:S(2)}, u32[]{:S(2)}) collective-permute-start(bf16[2,4,96,512]{3,2,1,0:T(8,128)(2,1)S(1)} %get-tuple-element.246), channel_id=1, source_target_pairs={{0,16},{1,17},{2,18},{3,19},{4,20},{5,21},{6,22},{7,23},{8,24},{9,... | collective-permute-start | bytes 2359304 | tf_op jit(solution)/shard_map/ppermute | solution.py:937
  261.4 24.7 %collective-permute-start.32 = (bf16[4,96,512]{2,1,0:T(8,128)(2,1)S(1)}, bf16[4,96,512]{2,1,0:T(8,128)(2,1)S(1)}, u32[]{:S(2)}, u32[]{:S(2)}) collective-permute-start(bf16[4,96,512]{2,1,0:T(8,128)(2,1)S(1)} %get-tuple-element.256), channel_id=1, source_target_pairs={{0,16},{1,17},{2,18},{3,19},{4,20},{5,21},{6,22},{7,23},{8,24},{9,... | collective-permute-start | bytes 1179656 | tf_op jit(solution)/shard_map/ppermute | solution.py:937
  262.9 23.2 %collective-permute-start.33 = (bf16[4,96,512]{2,1,0:T(8,128)(2,1)S(1)}, bf16[4,96,512]{2,1,0:T(8,128)(2,1)S(1)}, u32[]{:S(2)}, u32[]{:S(2)}) collective-permute-start(bf16[4,96,512]{2,1,0:T(8,128)(2,1)S(1)} %get-tuple-element.258), channel_id=1, source_target_pairs={{0,8},{1,9},{2,10},{3,11},{4,12},{5,13},{6,14},{7,15},{8,0},{9,1},... | collective-permute-start | bytes 1179656 | tf_op jit(solution)/shard_map/ppermute | solution.py:937
  271.3 17.0 %collective-permute-start.35 = (bf16[16,64,512]{2,1,0:T(8,128)(2,1)S(1)}, bf16[16,64,512]{2,1,0:T(8,128)(2,1)S(1)}, u32[]{:S(2)}, u32[]{:S(2)}) collective-permute-start(bf16[16,64,512]{2,1,0:T(8,128)(2,1)S(1)} %get-tuple-element.263), channel_id=1, source_target_pairs={{0,1},{1,0},{2,3},{3,2},{4,5},{5,4},{6,7},{7,6},{8,9},{9,8},{10,11... | collective-permute-start | bytes 3145736 | tf_op jit(solution)/shard_map/ppermute | solution.py:937
  297.1 20.4 %collective-permute-start.38 = (bf16[2,4,96,512]{3,2,1,0:T(8,128)(2,1)S(1)}, bf16[2,4,96,512]{3,2,1,0:T(8,128)(2,1)S(1)}, u32[]{:S(2)}, u32[]{:S(2)}) collective-permute-start(bf16[2,4,96,512]{3,2,1,0:T(8,128)(2,1)S(1)} %get-tuple-element.276), channel_id=1, source_target_pairs={{0,8},{1,9},{2,10},{3,11},{4,12},{5,13},{6,14},{7,15},{8,0},{9,1},... | collective-permute-start | bytes 2359304 | tf_op jit(solution)/shard_map/ppermute | solution.py:937
  297.7 20.4 %collective-permute-start.39 = (bf16[2,4,96,512]{3,2,1,0:T(8,128)(2,1)S(1)}, bf16[2,4,96,512]{3,2,1,0:T(8,128)(2,1)S(1)}, u32[]{:S(2)}, u32[]{:S(2)}) collective-permute-start(bf16[2,4,96,512]{3,2,1,0:T(8,128)(2,1)S(1)} %get-tuple-element.278), channel_id=1, source_target_pairs={{0,16},{1,17},{2,18},{3,19},{4,20},{5,21},{6,22},{7,23},{8,24},{9,... | collective-permute-start | bytes 2359304 | tf_op jit(solution)/shard_map/ppermute | solution.py:937
  305.7 46.3 %collective-permute-start.52 = (bf16[192,512]{1,0:T(8,128)(2,1)S(1)}, bf16[192,512]{1,0:T(8,128)(2,1)S(1)}, u32[]{:S(2)}, u32[]{:S(2)}) collective-permute-start(bf16[192,512]{1,0:T(8,128)(2,1)S(1)} %get-tuple-element.311), channel_id=1, source_target_pairs={{0,4},{1,5},{2,6},{3,7},{4,0},{5,1},{6,2},{7,3},{8,12},{9,13},{10,... | collective-permute-start | bytes 589832 | tf_op jit(solution)/shard_map/ppermute | solution.py:937
  309.2 19.4 %collective-permute-start.40 = (bf16[2,4,32,512]{3,2,1,0:T(8,128)(2,1)S(1)}, bf16[2,4,32,512]{3,2,1,0:T(8,128)(2,1)S(1)}, u32[]{:S(2)}, u32[]{:S(2)}) collective-permute-start(bf16[2,4,32,512]{3,2,1,0:T(8,128)(2,1)S(1)} %get-tuple-element.283), channel_id=1, source_target_pairs={{0,8},{1,9},{2,10},{3,11},{4,12},{5,13},{6,14},{7,15},{8,0},{9,1},... | collective-permute-start | bytes 786440 | tf_op jit(solution)/shard_map/ppermute | solution.py:937
  309.7 18.9 %collective-permute-start.41 = (bf16[2,4,32,512]{3,2,1,0:T(8,128)(2,1)S(1)}, bf16[2,4,32,512]{3,2,1,0:T(8,128)(2,1)S(1)}, u32[]{:S(2)}, u32[]{:S(2)}) collective-permute-start(bf16[2,4,32,512]{3,2,1,0:T(8,128)(2,1)S(1)} %get-tuple-element.285), channel_id=1, source_target_pairs={{0,16},{1,17},{2,18},{3,19},{4,20},{5,21},{6,22},{7,23},{8,24},{9,... | collective-permute-start | bytes 786440 | tf_op jit(solution)/shard_map/ppermute | solution.py:937
  319.5 13.1 %collective-permute-start.42 = (bf16[4,96,512]{2,1,0:T(8,128)(2,1)S(1)}, bf16[4,96,512]{2,1,0:T(8,128)(2,1)S(1)}, u32[]{:S(2)}, u32[]{:S(2)}) collective-permute-start(bf16[4,96,512]{2,1,0:T(8,128)(2,1)S(1)} %get-tuple-element.288), channel_id=1, source_target_pairs={{0,16},{1,17},{2,18},{3,19},{4,20},{5,21},{6,22},{7,23},{8,24},{9,... | collective-permute-start | bytes 1179656 | tf_op jit(solution)/shard_map/ppermute | solution.py:937
  320.1 13.1 %collective-permute-start.43 = (bf16[4,96,512]{2,1,0:T(8,128)(2,1)S(1)}, bf16[4,96,512]{2,1,0:T(8,128)(2,1)S(1)}, u32[]{:S(2)}, u32[]{:S(2)}) collective-permute-start(bf16[4,96,512]{2,1,0:T(8,128)(2,1)S(1)} %get-tuple-element.290), channel_id=1, source_target_pairs={{0,8},{1,9},{2,10},{3,11},{4,12},{5,13},{6,14},{7,15},{8,0},{9,1},... | collective-permute-start | bytes 1179656 | tf_op jit(solution)/shard_map/ppermute | solution.py:937
  346.7 19.1 %collective-permute-start.54 = (f32[16,512]{1,0:T(8,128)S(1)}, f32[16,512]{1,0:T(8,128)S(1)}, u32[]{:S(2)}, u32[]{:S(2)}) collective-permute-start(f32[16,512]{1,0:T(8,128)S(1)} %get-tuple-element.320.refs_1__0_), channel_id=1, source_target_pairs={{0,2},{1,3},{2,0},{3,1},{4,6},{5,7},{6,4},{7,5},{8,10},{9,11},{10,... | collective-permute-start | bytes 98312 | tf_op jit(solution)/shard_map/ppermute | solution.py:937
  348.2 17.6 %collective-permute-start.55 = (f32[16,512]{1,0:T(8,128)S(1)}, f32[16,512]{1,0:T(8,128)S(1)}, u32[]{:S(2)}, u32[]{:S(2)}) collective-permute-start(f32[16,512]{1,0:T(8,128)S(1)} %get-tuple-element.320.refs_1__0_), channel_id=1, source_target_pairs={{0,4},{1,5},{2,6},{3,7},{4,0},{5,1},{6,2},{7,3},{8,12},{9,13},{10,... | collective-permute-start | bytes 98312 | tf_op jit(solution)/shard_map/ppermute | solution.py:937
  349.4 16.4 %collective-permute-start.56 = (f32[16,512]{1,0:T(8,128)S(1)}, f32[16,512]{1,0:T(8,128)S(1)}, u32[]{:S(2)}, u32[]{:S(2)}) collective-permute-start(f32[16,512]{1,0:T(8,128)S(1)} %get-tuple-element.320.refs_1__0_), channel_id=1, source_target_pairs={{0,6},{1,7},{2,4},{3,5},{4,2},{5,3},{6,0},{7,1},{8,14},{9,15},{10,... | collective-permute-start | bytes 98312 | tf_op jit(solution)/shard_map/ppermute | solution.py:937
  351.1 13.3 %collective-permute-start.53 = (bf16[192,512]{1,0:T(8,128)(2,1)S(1)}, bf16[192,512]{1,0:T(8,128)(2,1)S(1)}, u32[]{:S(2)}, u32[]{:S(2)}) collective-permute-start(bf16[192,512]{1,0:T(8,128)(2,1)S(1)} %get-tuple-element.314), channel_id=1, source_target_pairs={{0,4},{1,5},{2,6},{3,7},{4,0},{5,1},{6,2},{7,3},{8,12},{9,13},{10,... | collective-permute-start | bytes 589832 | tf_op jit(solution)/shard_map/ppermute | solution.py:937
  352.1 16.2 %collective-permute-start.57 = (bf16[64,512]{1,0:T(8,128)(2,1)S(1)}, bf16[64,512]{1,0:T(8,128)(2,1)S(1)}, u32[]{:S(2)}, u32[]{:S(2)}) collective-permute-start(bf16[64,512]{1,0:T(8,128)(2,1)S(1)} %get-tuple-element.324), channel_id=1, source_target_pairs={{0,4},{1,5},{2,6},{3,7},{4,0},{5,1},{6,2},{7,3},{8,12},{9,13},{10,... | collective-permute-start | bytes 196616 | tf_op jit(solution)/shard_map/ppermute | solution.py:937
  (75 other events, 662.5 us)
